TPU v7x, 256 devices: a whole 4x4x8 slice. The times are simulated.
256 devices in a mesh: tm: 8 (over x, core), space: 32 (over y, z).
Axes of the slice: x: 4, y: 4, z: 8, core: 2. Of those that a mesh axis runs over, the one named last changes fastest.
Arguments:
- state: bfloat16 [32, 5, 1280, 1024], P('tm', None, 'space'), may hold values from -2 to 8, as said below
- spectral: bfloat16 [32, 32], replicated, may hold values from -1 to 1
- deriv_i: bfloat16 [1024, 1024], replicated, may hold values from -0.1875 to 0.1875
- deriv_j: bfloat16 [1280, 1280], replicated, may hold values from -0.15625 to 0.15625
- metric_i: float32 [3, 1280, 1024], P(None, 'space'), may hold values from 0.3 to 1.5
- metric_j: float32 [3, 1280, 1024], P(None, 'space'), may hold values from 0.3 to 1.5
Outputs:
- residual: bfloat16 [32, 5, 1280, 1024], P('tm', None, 'space')
Inputs may be any that keep to these rules, and one draw needn't show every extreme that they name: `state`: each cell holds density between 0.6 and 1.6, speeds under 1.3 in each component and pressure between 0.5 and 2, in conserved form.
All inputs are finite; a program needn't handle non-finite values.
Results may differ from a plain program's by a relative error of at most 0.0047.
Values may be sent and summed in bfloat16 or wider, within the bound.
No kernel may reach another device: no remote copies, remote signals or barrier semaphores. Data moves between devices by JAX's collectives and lax.ppermute only.
A program may use at most 128 MiB of HBM per device.

v0:
```python
import jax
import jax.numpy as jnp
from jax import lax
from jax.sharding import PartitionSpec as P


def extended(block, sides, width):
    for axis, dim in sides:
        count = lax.axis_size(axis)
        forward = [(i, i + 1) for i in range(count - 1)]
        backward = [(target, source) for source, target in forward]
        low = lax.ppermute(
            lax.slice_in_dim(block, block.shape[dim] - width, None, axis=dim), axis, forward
        )
        high = lax.ppermute(lax.slice_in_dim(block, 0, width, axis=dim), axis, backward)
        block = jnp.concatenate([low, block, high], axis=dim)
    return block


def rusanov_parts(cons, metric):
    rho = cons[:, 0]
    velocity = cons[:, 1:4] / rho[:, None]
    energy = cons[:, 4]
    pressure = 0.4 * (energy - 0.5 * rho * jnp.sum(velocity * velocity, axis=1))
    contra = jnp.sum(metric[None] * velocity, axis=1)
    flux = jnp.stack(
        [
            rho * contra,
            cons[:, 1] * contra + metric[0][None] * pressure,
            cons[:, 2] * contra + metric[1][None] * pressure,
            cons[:, 3] * contra + metric[2][None] * pressure,
            (energy + pressure) * contra,
        ],
        axis=1,
    )
    radius = jnp.abs(contra) + jnp.sqrt(
        1.4 * pressure / rho * jnp.sum(metric * metric, axis=0)[None]
    )
    return (flux.astype(jnp.bfloat16), radius)


def second_diff(cons, axis):
    width = [(0, 0)] * cons.ndim
    width[axis] = (1, 1)
    padded = jnp.pad(cons, width)
    size = cons.shape[axis]
    upper = lax.slice_in_dim(padded, 2, size + 2, axis=axis)
    lower = lax.slice_in_dim(padded, 0, size, axis=axis)
    return upper + lower - 2.0 * cons


def on_device(state, spectral, deriv_i, deriv_j, metric_i, metric_j):
    local_count = state.shape[0]
    line_count = state.shape[2]
    width_i = state.shape[3]
    first_row = lax.axis_index("tm") * local_count
    own_rows = lax.dynamic_slice_in_dim(spectral, first_row, local_count, 0)
    source = jnp.einsum(
        "nm,mvji->nvji",
        own_rows,
        lax.all_gather(state, "tm", axis=0, tiled=True),
        preferred_element_type=jnp.float32,
    )
    cons = state.astype(jnp.float32)
    flux_i, radius_i = rusanov_parts(cons, metric_i)
    term_i = jnp.einsum("tvji,ki->tvjk", flux_i, deriv_i, preferred_element_type=jnp.float32)
    term_i = term_i - 0.25 * radius_i[:, None] * second_diff(cons, 3)
    flux_j, radius_j = rusanov_parts(cons, metric_j)
    rimmed = extended(state, (("space", 2),), 1).astype(jnp.float32)
    second_j = rimmed[:, :, 2:] + rimmed[:, :, :-2] - 2.0 * cons
    damping_j = 0.25 * radius_j[:, None] * second_j
    outgoing = jnp.transpose(flux_j, (2, 1, 0, 3)).reshape(
        line_count, flux_j.shape[1], local_count * width_i
    )
    slope = jnp.einsum(
        "kj,jvw->kvw",
        deriv_j,
        lax.all_to_all(outgoing, "space", split_axis=2, concat_axis=0, tiled=True),
        preferred_element_type=jnp.float32,
    ).astype(jnp.bfloat16)
    slope_back = lax.all_to_all(slope, "space", split_axis=0, concat_axis=2, tiled=True)
    slope_back = jnp.transpose(
        slope_back.reshape(line_count, flux_j.shape[1], local_count, width_i), (2, 1, 0, 3)
    )
    total = source + term_i + slope_back.astype(jnp.float32) - damping_j
    return total.astype(jnp.bfloat16)


def solution(mesh):
    return jax.shard_map(
        on_device,
        mesh=mesh,
        in_specs=(
            P("tm", None, "space", None),
            P(),
            P(),
            P(),
            P(None, "space", None),
            P(None, "space", None),
        ),
        out_specs=P("tm", None, "space", None),
        check_vma=False,
    )
```

profile of v0, /device:TPU:4, one launch (start us, length us, event | category | flops | bytes accessed | tf_op | source)
XLA Modules:
  0.0 229.8 jit_solution(5668621682577521940)
XLA Ops:
  6.5 0.0 copy-start
  6.5 0.0 all-gather.2.cloned.1.call-start
  6.5 0.7 all-gather.2.cloned.1.call-update
  7.3 1.3 multiply_reduce_fusion.4
  8.6 0.0 copy-start.8
  8.6 0.0 copy-start.9
  8.6 4.4 %copy_convert_fusion = (f32[4,5,40,1024]{3,0,2,1:T(4,128)S(1)}, bf16[4,5,40,1024]{3,0,2,1:T(4,128)(2,1)}) fusion(bf16[4,5,40,1024]{3,2,1,0:T(8,128)(2,1)} %param.6), kind=kLoop, calls=%fused_computation.88 | loop fusion | flops 819200 | bytes 6553600 | tf_op jit(solution)/shard_map/convert_element_type | solution.py:64
  13.0 0.0 copy-done.8
  13.0 0.0 copy-done.9
  13.1 0.1 multiply_bitcast_fusion
  13.2 2.2 multiply_reduce_fusion.2
  15.4 0.0 copy-start.3
  15.4 0.4 fusion.52
  15.9 1.6 fusion.47
  17.5 0.7 fusion.51
  18.2 0.7 fusion.50
  18.9 0.7 fusion.49
  19.6 0.0 copy-done.2
  19.6 0.0 copy-done.3
  19.6 0.0 copy-done.5
  19.6 0.6 fusion.48
  20.3 0.0 copy-start.11
  20.3 1.3 copy-done.11
  21.5 1.1 copy-done.12
  22.7 9.4 %copy.58 = bf16[40,5,4,1024]{0,1,3,2:T(8,128)(2,1)} copy(bf16[40,5,4,1024]{3,2,0,1:T(4,128)(2,1)} %bitcast.145) | data formatting | bytes 3276800 | tf_op jit(solution)/shard_map/reshape | solution.py:72
  32.1 10.7 %reshape.67 = bf16[32,2,12800]{2,1,0:T(2,128)(2,1)} reshape(bf16[4096,5,40]{2,1,0:T(8,128)(2,1)} %bitcast.142) | data formatting | bytes 3276800
  42.8 52.4 %all_to_all.27 = bf16[32,2,12800]{2,1,0:T(2,128)(2,1)} all-to-all(bf16[32,2,12800]{2,1,0:T(2,128)(2,1)} %reshape.67), channel_id=1, replica_groups=mesh['tm'=8,'space'=32] {'space'}, dimensions={0} | all-to-all | bytes 3276800 | tf_op jit(solution)/shard_map/all_to_all | solution.py:78
  95.2 10.2 %reshape.68 = bf16[4096,5,40]{2,1,0:T(8,128)(2,1)} reshape(bf16[32,2,12800]{2,1,0:T(2,128)(2,1)} %all_to_all.27) | data formatting | bytes 3276800
  105.4 8.2 %copy.46 = bf16[32,40,5,128]{3,1,0,2:T(8,128)(2,1)} copy(bf16[32,40,5,128]{1,2,3,0:T(8,128)(2,1)} %bitcast.143) | data formatting | bytes 3276800 | tf_op jit(solution)/shard_map/all_to_all | solution.py:78
  113.5 5.0 %fusion.17 = bf16[1280,5,128]{0,2,1:T(8,128)(2,1)} fusion(bf16[1280,5,128]{2,0,1:T(8,128)(2,1)} %bitcast.146, bf16[1280,1280]{1,0:T(8,128)(2,1)S(1)} %copy-done), kind=kOutput, calls=%fused_computation.19 | convolution fusion | flops 2097971200 | bytes 6553600 | tf_op jit(solution)/shard_map/kj,jvw->kvw/dot_general | solution.py:75
  118.5 4.5 %copy.48 = bf16[1280,5,128]{2,1,0:T(8,128)(2,1)} copy(bf16[1280,5,128]{0,2,1:T(8,128)(2,1)} %fusion.17) | data formatting | bytes 3276800 | tf_op jit(solution)/shard_map/convert_element_type | solution.py:80
  123.0 5.8 %all-to-all-start.1 = ((bf16[1280,5,128]{2,1,0:T(8,128)(2,1)}), bf16[1280,5,128]{2,1,0:T(8,128)(2,1)}, u32[]{:S(2)}, u32[]{:S(2)}) async-start(bf16[1280,5,128]{2,1,0:T(8,128)(2,1)} %copy.48), calls=%async_computation.1 | async-start | bytes 5242880 | tf_op jit(solution)/shard_map/all_to_all | solution.py:81
  128.8 3.6 %collective-permute-start = (bf16[4,5,1,1024]{3,0,2,1:T(4,128)(2,1)S(1)}, bf16[4,5,1,1024]{3,0,2,1:T(4,128)(2,1)S(1)}, u32[]{:S(2)}, u32[]{:S(2)}) collective-permute-start(bf16[4,5,1,1024]{3,0,2,1:T(4,128)(2,1)S(1)} %get-tuple-element.22), channel_id=1, source_target_pairs={{0,1},{1,2},{2,3},{3,4},{4,5},{5,6},{6,7},{7,8},{8,9},{9,10},{10,1... | collective-permute-start | bytes 122888 | tf_op jit(solution)/shard_map/ppermute | solution.py:12
  132.5 1.3 collective-permute-start.1
  133.8 0.0 copy-done.10
  133.8 6.2 %fusion.20 = f32[4,5,40,1024]{3,2,1,0:T(8,128)} fusion(bf16[1024,1024]{1,0:T(8,128)(2,1)} %param.8, bf16[4,5,40,1024]{3,0,2,1:T(4,128)(2,1)} %copy-done.12), kind=kOutput, calls=%fused_computation.20 | convolution fusion | flops 1677721600 | bytes 7012352 | tf_op jit(solution)/shard_map/tvji,ki->tvjk/dot_general | solution.py:66
  140.0 0.0 copy-done.4
  140.0 2.6 %fusion.35 = f32[4,40,1024]{2,0,1:T(4,128)} fusion(f32[4,40,1024]{2,0,1:T(4,128)S(1)} %copy-done.4, f32[40,1024]{1,0:T(8,128)S(1)} %multiply_reduce_fusion.3, f32[4,5,40,1024]{3,0,2,1:T(4,128)} %copy-done.2, f32[4,1,40,1024]{3,0,2,1:T(4,128)S(1)} %copy-done.6), kind=kLoop, calls=%fused_computation.44 | loop fusion | flops 983040 | bytes 2785280 | tf_op jit(solution)/shard_map/mul | solution.py:71
  142.6 40.4 %collective-permute-done = bf16[4,5,1,1024]{3,0,2,1:T(4,128)(2,1)S(1)} collective-permute-done((bf16[4,5,1,1024]{3,0,2,1:T(4,128)(2,1)S(1)}, bf16[4,5,1,1024]{3,0,2,1:T(4,128)(2,1)S(1)}, u32[]{:S(2)}, u32[]{:S(2)}) %collective-permute-start) | collective-permute-done | bytes 40992 | tf_op jit(solution)/shard_map/ppermute | solution.py:12
  182.9 3.5 %collective-permute-done.1 = bf16[4,5,1,1024]{3,0,2,1:T(4,128)(2,1)S(1)} collective-permute-done((bf16[4,5,1,1024]{3,0,2,1:T(4,128)(2,1)S(1)}, bf16[4,5,1,1024]{3,0,2,1:T(4,128)(2,1)S(1)}, u32[]{:S(2)}, u32[]{:S(2)}) %collective-permute-start.1) | collective-permute-done | bytes 40992 | tf_op jit(solution)/shard_map/ppermute | solution.py:15
  186.4 2.9 %maximum_convert_fusion = f32[4,5,42,1024]{3,0,2,1:T(4,128)} fusion(bf16[4,5,1,1024]{3,0,2,1:T(4,128)(2,1)S(1)} %collective-permute-done.1, bf16[4,5,40,1024]{3,0,2,1:T(4,128)(2,1)S(1)} %copy-done.7, bf16[4,5,1,1024]{3,0,2,1:T(4,128)(2,1)S(1)} %collective-permute-done), kind=kLoop, calls=%fused_computation.26 | loop fusion | flops 2580480 | bytes 5160960 | tf_op jit(solution)/shard_map/convert_element_type | solution.py:69
  189.3 2.6 %all-to-all-done.1 = bf16[1280,5,128]{2,1,0:T(8,128)(2,1)} async-done(((bf16[1280,5,128]{2,1,0:T(8,128)(2,1)}), bf16[1280,5,128]{2,1,0:T(8,128)(2,1)}, u32[]{:S(2)}, u32[]{:S(2)}) %all-to-all-start.1) | async-done | bytes 1638432 | tf_op jit(solution)/shard_map/all_to_all | solution.py:81
  191.9 2.0 copy.49
  193.9 0.2 convert_bitcast_fusion
  194.1 2.3 copy.50
  196.4 5.0 %reshape.62 = f32[40,5,4,1024]{3,2,0,1:T(4,128)} reshape(f32[40,5,32,128]{3,2,0,1:T(8,128)} %copy.50) | data formatting | bytes 6553600 | tf_op jit(solution)/shard_map/convert_element_type | solution.py:85
  201.4 18.4 %fusion.13 = bf16[4,5,40,1024]{3,0,2,1:T(4,128)(2,1)} fusion(f32[4,5,42,1024]{3,0,2,1:T(4,128)} %maximum_convert_fusion, f32[40,5,4,1024]{3,2,0,1:T(4,128)} %reshape.62, f32[4,5,40,1024]{3,0,2,1:T(4,128)} %copy-done.2, f32[4,5,40,1024]{3,2,1,0:T(8,128)} %fusion.20, f32[4,40,1024]{2,0,1:T(4,128)} %fusion.35, f32[4,40,1024]{2,0,1:T(4,128)} %get-tuple-element.8, ...), kind=kOutput, calls=%fused_computation.17 | convolution fusion | flops 62259200 | bytes 32441348 | tf_op jit(solution)/shard_map/nm,mvji->nvji/dot_general | solution.py:58
  219.8 3.1 %copy.54 = bf16[4,5,40,1024]{3,2,1,0:T(8,128)(2,1)} copy(bf16[4,5,40,1024]{3,0,2,1:T(4,128)(2,1)} %fusion.13) | data formatting | bytes 3276800 | tf_op jit(solution)/shard_map/convert_element_type | solution.py:86
  (16 shorter events, 0.1 us)
Async XLA Ops:
  6.5 107.0 %copy-start = (bf16[1280,1280]{1,0:T(8,128)(2,1)S(1)}, bf16[1280,1280]{1,0:T(8,128)(2,1)}, u32[]{:S(2)}) copy-start(bf16[1280,1280]{1,0:T(8,128)(2,1)} %param.9) | copy-start | bytes 9830404
  6.5 194.8 %all-gather.2.cloned.1.call-start = ((), (), s32[]{:S(2)}) async-start(), calls=%async_computation.2 | async-start | bytes 14745600 | tf_op jit(solution)/shard_map/all_gather | solution.py:61
  8.6 4.4 %copy-start.8 = (f32[3,40,1024]{2,1,0:T(8,128)S(1)}, f32[3,40,1024]{2,1,0:T(8,128)}, u32[]{:S(2)}) copy-start(f32[3,40,1024]{2,1,0:T(8,128)} %param.10) | copy-start | bytes 1474564
  8.6 4.4 %copy-start.9 = (f32[3,40,1024]{2,1,0:T(8,128)S(1)}, f32[3,40,1024]{2,1,0:T(8,128)}, u32[]{:S(2)}) copy-start(f32[3,40,1024]{2,1,0:T(8,128)} %param.11) | copy-start | bytes 1474564
  13.0 6.6 %copy-start.2 = (f32[4,5,40,1024]{3,0,2,1:T(4,128)}, f32[4,5,40,1024]{3,0,2,1:T(4,128)S(1)}, u32[]{:S(2)}) copy-start(f32[4,5,40,1024]{3,0,2,1:T(4,128)S(1)} %get-tuple-element.20) | copy-start | bytes 9830404
  15.4 4.2 %copy-start.3 = (f32[4,40,1024]{2,0,1:T(4,128)}, f32[4,40,1024]{2,0,1:T(4,128)S(1)}, u32[]{:S(2)}) copy-start(f32[4,40,1024]{2,0,1:T(4,128)S(1)} %get-tuple-element.6) | copy-start | bytes 1966084
  17.5 2.1 copy-start.5
  20.3 1.3 copy-start.11
  21.5 1.2 copy-start.12
  123.0 5.8 %copy-start.7 = (bf16[4,5,40,1024]{3,0,2,1:T(4,128)(2,1)S(1)}, bf16[4,5,40,1024]{3,0,2,1:T(4,128)(2,1)}, u32[]{:S(2)}) copy-start(bf16[4,5,40,1024]{3,0,2,1:T(4,128)(2,1)} %get-tuple-element.21) | copy-start | bytes 4915204
  123.0 10.8 %copy-start.10 = (f32[3,40,1024]{2,1,0:T(8,128)S(1)}, f32[3,40,1024]{2,1,0:T(8,128)}, u32[]{:S(2)}) copy-start(f32[3,40,1024]{2,1,0:T(8,128)} %param.11) | copy-start | bytes 1474564
  123.0 68.9 %all-to-all-start.1 = ((bf16[1280,5,128]{2,1,0:T(8,128)(2,1)}), bf16[1280,5,128]{2,1,0:T(8,128)(2,1)}, u32[]{:S(2)}, u32[]{:S(2)}) async-start(bf16[1280,5,128]{2,1,0:T(8,128)(2,1)} %copy.48), calls=%async_computation.1 | async-start | bytes 5242880 | tf_op jit(solution)/shard_map/all_to_all | solution.py:81
  128.8 54.1 %collective-permute-start = (bf16[4,5,1,1024]{3,0,2,1:T(4,128)(2,1)S(1)}, bf16[4,5,1,1024]{3,0,2,1:T(4,128)(2,1)S(1)}, u32[]{:S(2)}, u32[]{:S(2)}) collective-permute-start(bf16[4,5,1,1024]{3,0,2,1:T(4,128)(2,1)S(1)} %get-tuple-element.22), channel_id=1, source_target_pairs={{0,1},{1,2},{2,3},{3,4},{4,5},{5,6},{6,7},{7,8},{8,9},{9,10},{10,1... | collective-permute-start | bytes 122888 | tf_op jit(solution)/shard_map/ppermute | solution.py:12
  132.5 54.0 %collective-permute-start.1 = (bf16[4,5,1,1024]{3,0,2,1:T(4,128)(2,1)S(1)}, bf16[4,5,1,1024]{3,0,2,1:T(4,128)(2,1)S(1)}, u32[]{:S(2)}, u32[]{:S(2)}) collective-permute-start(bf16[4,5,1,1024]{3,0,2,1:T(4,128)(2,1)S(1)} %get-tuple-element.23), channel_id=1, source_target_pairs={{1,0},{2,1},{3,2},{4,3},{5,4},{6,5},{7,6},{8,7},{9,8},{10,9},{11,1... | collective-permute-start | bytes 122888 | tf_op jit(solution)/shard_map/ppermute | solution.py:15
  133.8 6.2 %copy-start.4 = (f32[4,40,1024]{2,0,1:T(4,128)S(1)}, f32[4,40,1024]{2,0,1:T(4,128)}, u32[]{:S(2)}) copy-start(f32[4,40,1024]{2,0,1:T(4,128)} %copy-done.3) | copy-start | bytes 1966084
  133.8 6.2 %copy-start.6 = (f32[4,1,40,1024]{3,0,2,1:T(4,128)S(1)}, f32[4,1,40,1024]{3,0,2,1:T(4,128)}, u32[]{:S(2)}) copy-start(f32[4,1,40,1024]{3,0,2,1:T(4,128)} %copy-done.5) | copy-start | bytes 1966084
  201.4 21.5 %copy-start.1 = (bf16[1280,1280]{1,0:T(8,128)(2,1)S(1)}, bf16[1280,1280]{1,0:T(8,128)(2,1)}, u32[]{:S(2)}) copy-start(bf16[1280,1280]{1,0:T(8,128)(2,1)} %param.9) | copy-start | bytes 9830404
Sparse Core Ops, SparseCore 0:
  9.2 74.1 all-gather.1
where the time goes:
time: 231 us; the launch traced here: 230 us
  local copies, waits for them, and re-layouts  57.7 us (25%)
  blocking collectives  52.4 us (23%)
  waiting for transfers between devices  47.1 us (20%)
  matrix products  29.6 us (13%)
  other arithmetic  18.5 us (8%)
  between operations  13.6 us (6%)
  starting transfers between devices  10.7 us (5%)
    all_to_all x1, blocking collectives, on_device(): lax.all_to_all(outgoing, 'space', split_axis=2, concat_axis=0, tiled=True)  52.4 us
    ppermute x1, waiting for transfers between devices, extended(): lax.ppermute(lax.slice_in_dim(block, block.shape[dim] - width, None, axis...  40.4 us
    unnamed x28, local copies, waits for them, and re-layouts  23.3 us
    dot_general x1, matrix products, on_device(): jnp.einsum('nm,mvji->nvji', own_rows, lax.all_gather(state, 'tm', axis=0,...  18.4 us
    reshape x1, local copies, waits for them, and re-layouts, on_device(): jnp.transpose(flux_j, (2, 1, 0, 3))  9.41 us
    all_to_all x1, local copies, waits for them, and re-layouts, on_device(): lax.all_to_all(outgoing, 'space', split_axis=2, concat_axis=0, tiled=True)  8.15 us
    convert_element_type x2, local copies, waits for them, and re-layouts, on_device(): total = source + term_i + slope_back.astype(jnp.float32) - damping_j  7.27 us
    dot_general x1, matrix products, on_device(): jnp.einsum('tvji,ki->tvjk', flux_i, deriv_i, preferred_element_type=jnp.f...  6.17 us
  transfers between devices with their start and end apart: 4, of which 3 were waited for; matrix products, arithmetic and copies ran while one was open for 36% of the time, Pallas kernels for 0%

commit v1 on v0

v1 whole, which is shorter than its diff:
```python
import jax
import jax.numpy as jnp
from jax import lax
from jax.experimental import pallas as pl
from jax.experimental.pallas import tpu as pltpu
from jax.sharding import PartitionSpec as P

LANES = 128
VMEM_LIMIT = 40 * 1024 * 1024


def primitives(cons, metric):
    rho, mx, my, mz, energy = cons
    ax, ay, az = metric
    inv = 1.0 / rho
    contra = (ax * mx + ay * my + az * mz) * inv
    pressure = 0.4 * (energy - 0.5 * (mx * mx + my * my + mz * mz) * inv)
    return inv, contra, pressure


def flux_of(cons, metric, contra, pressure):
    rho, mx, my, mz, energy = cons
    ax, ay, az = metric
    return (
        rho * contra,
        mx * contra + ax * pressure,
        my * contra + ay * pressure,
        mz * contra + az * pressure,
        (energy + pressure) * contra,
    )


def radius_of(metric, inv, contra, pressure):
    ax, ay, az = metric
    return jnp.abs(contra) + jnp.sqrt(1.4 * pressure * inv * (ax * ax + ay * ay + az * az))


def flux_j_kernel(state_ref, metric_ref, out_ref):
    blocks = state_ref.shape[3] // LANES
    for b in range(blocks):
        cols = slice(b * LANES, (b + 1) * LANES)
        cons = [state_ref[0, v, :, cols].astype(jnp.float32) for v in range(5)]
        metric = [metric_ref[c, :, cols] for c in range(3)]
        _, contra, pressure = primitives(cons, metric)
        for v, f in enumerate(flux_of(cons, metric, contra, pressure)):
            out_ref[0, b, :, v * LANES : (v + 1) * LANES] = f.astype(jnp.bfloat16)


def flux_j_blocks(state, metric_j):
    nt, nv, nj, ni = state.shape
    blocks = ni // LANES
    return pl.pallas_call(
        flux_j_kernel,
        grid=(nt,),
        out_shape=jax.ShapeDtypeStruct((nt, blocks, nj, nv * LANES), jnp.bfloat16),
        in_specs=[
            pl.BlockSpec((1, nv, nj, ni), lambda t: (t, 0, 0, 0)),
            pl.BlockSpec((3, nj, ni), lambda t: (0, 0, 0)),
        ],
        out_specs=pl.BlockSpec((1, blocks, nj, nv * LANES), lambda t: (t, 0, 0, 0)),
        compiler_params=pltpu.CompilerParams(vmem_limit_bytes=VMEM_LIMIT),
        cost_estimate=pl.CostEstimate(flops=10_000_000, bytes_accessed=4_000_000, transcendentals=200_000),
        name="flux_j",
    )(state, metric_j)


def local_kernel(state_ref, metric_i_ref, metric_j_ref, low_ref, high_ref, deriv_ref, out_ref, flux_ref):
    nv, nj, ni = state_ref.shape[1:]
    metric_i = [metric_i_ref[c] for c in range(3)]
    cons = [state_ref[0, v].astype(jnp.float32) for v in range(nv)]
    inv, contra, pressure = primitives(cons, metric_i)
    for v, f in enumerate(flux_of(cons, metric_i, contra, pressure)):
        flux_ref[v * nj : (v + 1) * nj, :] = f
    radius_i = 0.25 * radius_of(metric_i, inv, contra, pressure)
    metric_j = [metric_j_ref[c] for c in range(3)]
    inv, contra, pressure = primitives(cons, metric_j)
    radius_j = 0.25 * radius_of(metric_j, inv, contra, pressure)
    term = lax.dot_general(
        flux_ref[...].astype(jnp.bfloat16),
        deriv_ref[...],
        (((1,), (1,)), ((), ())),
        preferred_element_type=jnp.float32,
    )
    row = lax.broadcasted_iota(jnp.int32, (nj, ni), 0)
    col = lax.broadcasted_iota(jnp.int32, (nj, ni), 1)
    low = low_ref[0].astype(jnp.float32)
    high = high_ref[0].astype(jnp.float32)
    for v in range(nv):
        c = cons[v]
        right = jnp.where(col == ni - 1, 0.0, pltpu.roll(c, ni - 1, 1))
        left = jnp.where(col == 0, 0.0, pltpu.roll(c, 1, 1))
        up = jnp.where(row == nj - 1, high[v : v + 1], pltpu.roll(c, nj - 1, 0))
        down = jnp.where(row == 0, low[v : v + 1], pltpu.roll(c, 1, 0))
        twice = 2.0 * c
        damping = radius_i * (right + left - twice) + radius_j * (up + down - twice)
        out_ref[0, v] = term[v * nj : (v + 1) * nj] - damping


def local_terms(state, metric_i, metric_j, low, high, deriv_i):
    nt, nv, nj, ni = state.shape
    whole3 = pl.BlockSpec((3, nj, ni), lambda t: (0, 0, 0))
    halo = pl.BlockSpec((1, nv, ni), lambda t: (t, 0, 0))
    per_t = pl.BlockSpec((1, nv, nj, ni), lambda t: (t, 0, 0, 0))
    return pl.pallas_call(
        local_kernel,
        grid=(nt,),
        out_shape=jax.ShapeDtypeStruct((nt, nv, nj, ni), jnp.float32),
        in_specs=[per_t, whole3, whole3, halo, halo, pl.BlockSpec((ni, ni), lambda t: (0, 0))],
        out_specs=per_t,
        scratch_shapes=[pltpu.VMEM((nv * nj, ni), jnp.float32)],
        compiler_params=pltpu.CompilerParams(vmem_limit_bytes=VMEM_LIMIT),
        cost_estimate=pl.CostEstimate(
            flops=2 * nt * nv * nj * ni * ni, bytes_accessed=9_000_000, transcendentals=600_000
        ),
        name="local_terms",
    )(state, metric_i, metric_j, low, high, deriv_i)


def slope_kernel(deriv_ref, lines_ref, out_ref):
    out_ref[...] = jnp.dot(
        deriv_ref[...], lines_ref[...], preferred_element_type=jnp.float32
    ).astype(jnp.bfloat16)


def slope_lines(deriv_j, lines):
    size, width = lines.shape
    rows = 256
    return pl.pallas_call(
        slope_kernel,
        grid=(size // rows,),
        out_shape=jax.ShapeDtypeStruct((size, width), jnp.bfloat16),
        in_specs=[
            pl.BlockSpec((rows, size), lambda k: (k, 0)),
            pl.BlockSpec((size, width), lambda k: (0, 0)),
        ],
        out_specs=pl.BlockSpec((rows, width), lambda k: (k, 0)),
        compiler_params=pltpu.CompilerParams(vmem_limit_bytes=VMEM_LIMIT),
        cost_estimate=pl.CostEstimate(
            flops=2 * size * size * width, bytes_accessed=7_000_000, transcendentals=0
        ),
        name="slope_lines",
    )(deriv_j, lines)


def finish_kernel(total_ref, slope_ref, out_ref):
    nv = total_ref.shape[1]
    for b in range(slope_ref.shape[1]):
        cols = slice(b * LANES, (b + 1) * LANES)
        for v in range(nv):
            s = slope_ref[0, b, :, v * LANES : (v + 1) * LANES].astype(jnp.float32)
            out_ref[0, v, :, cols] = (total_ref[0, v, :, cols] + s).astype(jnp.bfloat16)


def finish(total, slope):
    nt, nv, nj, ni = total.shape
    per_t = pl.BlockSpec((1, nv, nj, ni), lambda t: (t, 0, 0, 0))
    return pl.pallas_call(
        finish_kernel,
        grid=(nt,),
        out_shape=jax.ShapeDtypeStruct((nt, nv, nj, ni), jnp.bfloat16),
        in_specs=[per_t, pl.BlockSpec((1,) + slope.shape[1:], lambda t: (t, 0, 0, 0))],
        out_specs=per_t,
        compiler_params=pltpu.CompilerParams(vmem_limit_bytes=VMEM_LIMIT),
        cost_estimate=pl.CostEstimate(flops=1_000_000, bytes_accessed=7_000_000, transcendentals=0),
        name="finish",
    )(total, slope)


def on_device(state, spectral, deriv_i, deriv_j, metric_i, metric_j):
    nt, nv, nj, ni = state.shape
    count = lax.axis_size("space")
    forward = [(i, i + 1) for i in range(count - 1)]
    backward = [(target, source) for source, target in forward]
    gathered = lax.all_gather(state, "tm", axis=0, tiled=True)
    low = lax.ppermute(state[:, :, nj - 1, :], "space", forward)
    high = lax.ppermute(state[:, :, 0, :], "space", backward)
    outgoing = flux_j_blocks(state, metric_j).reshape(count, nj, nv * LANES)
    lines = lax.all_to_all(outgoing, "space", split_axis=0, concat_axis=0, tiled=True)
    lines, low, high = lax.optimization_barrier((lines, low, high))
    partial = local_terms(state, metric_i, metric_j, low, high, deriv_i)
    slope = slope_lines(deriv_j, lines.reshape(count * nj, nv * LANES))
    slope = lax.all_to_all(
        slope.reshape(count, nj, nv * LANES), "space", split_axis=0, concat_axis=0, tiled=True
    )
    own_rows = lax.dynamic_slice_in_dim(spectral, lax.axis_index("tm") * nt, nt, 0)
    source = jnp.einsum("nm,mvji->nvji", own_rows, gathered, preferred_element_type=jnp.float32)
    total = source + partial
    return finish(total, slope.reshape(nt, ni // LANES, nj, nv * LANES))


def solution(mesh):
    return jax.shard_map(
        on_device,
        mesh=mesh,
        in_specs=(
            P("tm", None, "space", None),
            P(),
            P(),
            P(),
            P(None, "space", None),
            P(None, "space", None),
        ),
        out_specs=P("tm", None, "space", None),
        check_vma=False,
    )
```

time: 231 us -> 129 us (0.56)
  blocking collectives: 52.4 us -> 0 us
  local copies, waits for them, and re-layouts: 57.7 us -> 9.1 us
  other arithmetic: 18.5 us -> 1.95 us
  Pallas kernels: 0 us -> 15.3 us
  starting transfers between devices: 10.7 us -> 21.3 us
  matrix products: 29.6 us -> 19.2 us
    all_to_all x1 -> x0, blocking collectives: 52.4 us -> none  [on_device(): lax.all_to_all(outgoing, 'space', split_axis=2, concat_axis=0, tiled=True)]
    pallas_call x0 -> x4, Pallas kernels: none -> 15.3 us  [the longest x1 5.9 us: local_terms(): pl.pallas_call(local_kernel, grid=(nt,), out_shape=jax.ShapeDtypeStruct((...]
    convert_element_type x4 -> x0, local copies, waits for them, and re-layouts: 14.8 us -> none  [the longest x2 7.27 us: on_device(): total = source + term_i + slope_back.astype(jnp.float32) - damping_j]
    unnamed x28 -> x24, local copies, waits for them, and re-layouts: 23.3 us -> 8.97 us
    all_to_all x1 -> x2, waiting for transfers between devices: 2.59 us -> 14.3 us  [the longest x1 10.3 us: on_device(): lax.all_to_all(slope.reshape(count, nj, nv * LANES), 'space', split_axis=...]
    all_to_all x1 -> x2, starting transfers between devices: 5.81 us -> 16.3 us  [the longest x1 11.5 us: on_device(): lax.all_to_all(outgoing, 'space', split_axis=0, concat_axis=0, tiled=True)]
    ppermute x2, waiting for transfers between devices: 43.8 us -> 33.3 us  [the longest x1 29.7 us: on_device(): low = lax.ppermute(state[:, :, nj - 1, :], 'space', forward)]
    dot_general x3 -> x1, matrix products: 29.6 us -> 19.2 us  [on_device(): jnp.einsum('nm,mvji->nvji', own_rows, gathered, preferred_element_type=jn...]
  transfers between devices with their start and end apart: 4 -> 5, of which waited for: 3 -> 4; matrix products, arithmetic and copies ran while one was open for 36% -> 17% of each run, Pallas kernels for 0% -> 9%
where the time goes in v1:
time: 129 us
  waiting for transfers between devices  48.3 us (37%)
  starting transfers between devices  21.3 us (17%)
  matrix products  19.2 us (15%)
  Pallas kernels  15.3 us (12%)
  between operations  13.5 us (10%)
  local copies, waits for them, and re-layouts  9.1 us (7%)
  other arithmetic  1.95 us (2%)
    ppermute x1, waiting for transfers between devices, on_device(): low = lax.ppermute(state[:, :, nj - 1, :], 'space', forward)  29.7 us
    dot_general x1, matrix products, on_device(): jnp.einsum('nm,mvji->nvji', own_rows, gathered, preferred_element_type=jn...  19.2 us
    all_to_all x1, starting transfers between devices, on_device(): lax.all_to_all(outgoing, 'space', split_axis=0, concat_axis=0, tiled=True)  11.5 us
    all_to_all x1, waiting for transfers between devices, on_device(): lax.all_to_all(slope.reshape(count, nj, nv * LANES), 'space', split_axis=...  10.3 us
    unnamed x24, local copies, waits for them, and re-layouts  8.97 us
    pallas_call x1, Pallas kernels, local_terms(): pl.pallas_call(local_kernel, grid=(nt,), out_shape=jax.ShapeDtypeStruct((...  5.9 us
    all_to_all x1, starting transfers between devices, on_device(): lax.all_to_all(slope.reshape(count, nj, nv * LANES), 'space', split_axis=...  4.86 us
    all_to_all x1, waiting for transfers between devices, on_device(): lax.all_to_all(outgoing, 'space', split_axis=0, concat_axis=0, tiled=True)  3.96 us
  transfers between devices with their start and end apart: 5, of which 4 were waited for; matrix products, arithmetic and copies ran while one was open for 17% of the time, Pallas kernels for 9%

profile of v1, /device:TPU:4, one launch (start us, length us, event | category | flops | bytes accessed | tf_op | source)
XLA Modules:
  0.0 128.8 jit_solution(9764242611713155799)
XLA Ops:
  6.5 0.0 copy-start
  6.5 0.0 all-gather.2.cloned.1.call-start
  6.5 0.7 all-gather.2.cloned.1.call-update
  7.3 0.0 copy-start.1
  7.3 1.4 %copy-done.1 = bf16[4,5,40,1024]{3,2,1,0:T(8,128)(2,1)S(1)} copy-done((bf16[4,5,40,1024]{3,2,1,0:T(8,128)(2,1)S(1)}, bf16[4,5,40,1024]{3,2,1,0:T(8,128)(2,1)}, u32[]{:S(2)}) %copy-start.1) | copy-done | bytes 1638424
  8.7 0.0 copy-start.6
  8.7 1.0 copy-done.6
  9.7 0.0 copy-start.2
  9.7 2.2 %flux_j.1 = bf16[4,8,40,640]{3,2,1,0:T(8,128)(2,1)} custom-call(bf16[4,5,40,1024]{3,2,1,0:T(8,128)(2,1)S(1)} %copy-done.1, f32[3,40,1024]{2,1,0:T(8,128)S(1)} %copy-done.6), custom_call_target="tpu_custom_call" | custom-call | flops 10000000 | bytes 4000000 | tf_op jit(solution)/shard_map/flux_j/pallas_call | solution.py:52
  11.9 11.5 %all-to-all-start = ((bf16[32,40,640]{2,1,0:T(8,128)(2,1)}), bf16[32,40,640]{2,1,0:T(8,128)(2,1)S(1)}, u32[]{:S(2)}, u32[]{:S(2)}) async-start(bf16[32,40,640]{2,1,0:T(8,128)(2,1)} %bitcast.2), calls=%async_computation | async-start | bytes 3276800 | tf_op jit(solution)/shard_map/all_to_all | solution.py:178
  23.4 0.0 copy-done.2
  23.4 0.1 fusion.5
  23.6 3.7 %collective-permute-start = (bf16[4,5,1024]{2,1,0:T(8,128)(2,1)S(1)}, bf16[4,5,1024]{2,1,0:T(8,128)(2,1)S(1)}, u32[]{:S(2)}, u32[]{:S(2)}) collective-permute-start(bf16[4,5,1024]{2,1,0:T(8,128)(2,1)S(1)} %bitcast.17), channel_id=1, source_target_pairs={{0,1},{1,2},{2,3},{3,4},{4,5},{5,6},{6,7},{7,8},{8,9},{9,10},{10,1... | collective-permute-start | bytes 122888 | tf_op jit(solution)/shard_map/ppermute | solution.py:175
  27.3 1.3 %collective-permute-start.1 = (bf16[4,5,1024]{2,1,0:T(8,128)(2,1)S(1)}, bf16[4,5,1024]{2,1,0:T(8,128)(2,1)S(1)}, u32[]{:S(2)}, u32[]{:S(2)}) collective-permute-start(bf16[4,5,1024]{2,1,0:T(8,128)(2,1)S(1)} %bitcast.18), channel_id=1, source_target_pairs={{1,0},{2,1},{3,2},{4,3},{5,4},{6,5},{7,6},{8,7},{9,8},{10,9},{11,1... | collective-permute-start | bytes 122888 | tf_op jit(solution)/shard_map/ppermute | solution.py:176
  28.6 29.7 %collective-permute-done.low_ref = bf16[4,5,1024]{2,1,0:T(8,128)(2,1)S(1)} collective-permute-done((bf16[4,5,1024]{2,1,0:T(8,128)(2,1)S(1)}, bf16[4,5,1024]{2,1,0:T(8,128)(2,1)S(1)}, u32[]{:S(2)}, u32[]{:S(2)}) %collective-permute-start) | collective-permute-done | bytes 40992 | tf_op jit(solution)/shard_map/ppermute | solution.py:175
  58.3 3.7 %collective-permute-done.1.high_ref = bf16[4,5,1024]{2,1,0:T(8,128)(2,1)S(1)} collective-permute-done((bf16[4,5,1024]{2,1,0:T(8,128)(2,1)S(1)}, bf16[4,5,1024]{2,1,0:T(8,128)(2,1)S(1)}, u32[]{:S(2)}, u32[]{:S(2)}) %collective-permute-start.1) | collective-permute-done | bytes 40992 | tf_op jit(solution)/shard_map/ppermute | solution.py:176
  62.0 4.0 %all-to-all-done = bf16[32,40,640]{2,1,0:T(8,128)(2,1)S(1)} async-done(((bf16[32,40,640]{2,1,0:T(8,128)(2,1)}), bf16[32,40,640]{2,1,0:T(8,128)(2,1)S(1)}, u32[]{:S(2)}, u32[]{:S(2)}) %all-to-all-start) | async-done | bytes 1638432 | tf_op jit(solution)/shard_map/all_to_all | solution.py:178
  65.9 0.0 copy-start.10
  65.9 2.0 %copy-done.10 = bf16[1280,1280]{1,0:T(8,128)(2,1)S(1)} copy-done((bf16[1280,1280]{1,0:T(8,128)(2,1)S(1)}, bf16[1280,1280]{1,0:T(8,128)(2,1)}, u32[]{:S(2)}) %copy-start.10) | copy-done | bytes 3276824
  67.9 3.4 %slope_lines.1 = bf16[1280,640]{1,0:T(8,128)(2,1)S(1)} custom-call(bf16[1280,1280]{1,0:T(8,128)(2,1)S(1)} %copy-done.10, bf16[1280,640]{1,0:T(8,128)(2,1)S(1)} %bitcast.16), custom_call_target="tpu_custom_call" | custom-call | flops 2097152000 | bytes 7000000 | tf_op jit(solution)/shard_map/slope_lines/pallas_call | solution.py:128
  71.3 0.0 copy-start.8
  71.4 1.2 copy-done.8
  72.5 0.0 copy-start.7
  72.5 0.0 copy-start.9
  72.5 4.9 %all-to-all-start.1 = ((bf16[32,40,640]{2,1,0:T(8,128)(2,1)}), bf16[32,40,640]{2,1,0:T(8,128)(2,1)}, u32[]{:S(2)}, u32[]{:S(2)}) async-start(bf16[32,40,640]{2,1,0:T(8,128)(2,1)} %bitcast.15), calls=%async_computation.1 | async-start | bytes 3276800 | tf_op jit(solution)/shard_map/all_to_all | solution.py:182
  77.4 0.0 copy-done.7
  77.4 0.0 copy-done.9
  77.4 0.0 copy-start.5
  77.4 1.6 %copy-done.5 = bf16[1024,1024]{1,0:T(8,128)(2,1)S(1)} copy-done((bf16[1024,1024]{1,0:T(8,128)(2,1)S(1)}, bf16[1024,1024]{1,0:T(8,128)(2,1)}, u32[]{:S(2)}) %copy-start.5) | copy-done | bytes 2097176
  79.1 5.9 %local_terms.1 = f32[4,5,40,1024]{3,2,1,0:T(8,128)S(1)} custom-call(bf16[4,5,40,1024]{3,2,1,0:T(8,128)(2,1)S(1)} %copy-done.2, f32[3,40,1024]{2,1,0:T(8,128)S(1)} %copy-done.9, f32[3,40,1024]{2,1,0:T(8,128)S(1)} %copy-done.7, bf16[4,5,1024]{2,1,0:T(8,128)(2,1)S(1)} %collective-permute-done.low_ref, bf16[4,5,1024]{2,1,0:T(8,128)(2,1)S(1)} %collective-permute-done.1.high_ref, ...), custom_call_target="tpu_custom_call" | custom-call | flops 1677721600 | bytes 9000000 | tf_op jit(solution)/shard_map/local_terms/pallas_call | solution.py:104
  85.0 0.0 copy-start.3
  85.0 1.7 %copy-done.3 = f32[4,5,40,1024]{3,2,1,0:T(8,128)} copy-done((f32[4,5,40,1024]{3,2,1,0:T(8,128)}, f32[4,5,40,1024]{3,2,1,0:T(8,128)S(1)}, u32[]{:S(2)}) %copy-start.3) | copy-done | bytes 3276824
  86.7 0.0 all-gather.2.cloned.1.call-done
  86.7 0.0 copy-done
  86.7 0.0 copy-start.4
  86.7 19.2 %fusion = f32[4,5,40,1024]{3,0,2,1:T(4,128)S(1)} fusion(bf16[32,5,40,1024]{3,2,1,0:T(8,128)(2,1)} %all-gather.2.cloned.1.call-done, bf16[32,32]{1,0:T(8,128)(2,1)S(1)} %copy-done, s32[]{:T(128)S(6)} %select_n.3), kind=kOutput, calls=%fused_computation | convolution fusion | flops 52428800 | bytes 16385028 | tf_op jit(solution)/shard_map/nm,mvji->nvji/dot_general | solution.py:186
  105.9 0.0 copy-done.4
  105.9 2.0 %copy_add_fusion.total_ref = f32[4,5,40,1024]{3,2,1,0:T(8,128)S(1)} fusion(f32[4,5,40,1024]{3,2,1,0:T(8,128)S(1)} %copy-done.4, f32[4,5,40,1024]{3,0,2,1:T(4,128)S(1)} %fusion), kind=kLoop, calls=%fused_computation.2 | loop fusion | flops 819200 | bytes 9830400 | tf_op jit(solution)/shard_map/add | solution.py:187
  107.8 10.3 %all-to-all-done.1 = bf16[32,40,640]{2,1,0:T(8,128)(2,1)} async-done(((bf16[32,40,640]{2,1,0:T(8,128)(2,1)}), bf16[32,40,640]{2,1,0:T(8,128)(2,1)}, u32[]{:S(2)}, u32[]{:S(2)}) %all-to-all-start.1) | async-done | bytes 1638432 | tf_op jit(solution)/shard_map/all_to_all | solution.py:182
  118.1 3.8 %finish.1 = bf16[4,5,40,1024]{3,2,1,0:T(8,128)(2,1)} custom-call(f32[4,5,40,1024]{3,2,1,0:T(8,128)S(1)} %copy_add_fusion.total_ref, bf16[4,8,40,640]{3,2,1,0:T(8,128)(2,1)} %bitcast.7.slope_ref), custom_call_target="tpu_custom_call" | custom-call | flops 1000000 | bytes 7000000 | tf_op jit(solution)/shard_map/finish/pallas_call | solution.py:157
  (2 shorter events, 0.1 us)
Async XLA Ops:
  6.5 80.1 %copy-start = (bf16[32,32]{1,0:T(8,128)(2,1)S(1)}, bf16[32,32]{1,0:T(8,128)(2,1)}, u32[]{:S(2)}) copy-start(bf16[32,32]{1,0:T(8,128)(2,1)} %param.7) | copy-start | bytes 6148
  6.5 80.1 %all-gather.2.cloned.1.call-start = ((), (), s32[]{:S(2)}) async-start(), calls=%async_computation.2 | async-start | bytes 14745600 | tf_op jit(solution)/shard_map/all_gather | solution.py:174
  7.3 1.4 %copy-start.1 = (bf16[4,5,40,1024]{3,2,1,0:T(8,128)(2,1)S(1)}, bf16[4,5,40,1024]{3,2,1,0:T(8,128)(2,1)}, u32[]{:S(2)}) copy-start(bf16[4,5,40,1024]{3,2,1,0:T(8,128)(2,1)} %state_ref.3) | copy-start | bytes 4915204
  8.7 1.0 copy-start.6
  9.7 13.7 %copy-start.2 = (bf16[4,5,40,1024]{3,2,1,0:T(8,128)(2,1)S(1)}, bf16[4,5,40,1024]{3,2,1,0:T(8,128)(2,1)}, u32[]{:S(2)}) copy-start(bf16[4,5,40,1024]{3,2,1,0:T(8,128)(2,1)} %state_ref.3) | copy-start | bytes 4915204
  11.9 54.0 %all-to-all-start = ((bf16[32,40,640]{2,1,0:T(8,128)(2,1)}), bf16[32,40,640]{2,1,0:T(8,128)(2,1)S(1)}, u32[]{:S(2)}, u32[]{:S(2)}) async-start(bf16[32,40,640]{2,1,0:T(8,128)(2,1)} %bitcast.2), calls=%async_computation | async-start | bytes 3276800 | tf_op jit(solution)/shard_map/all_to_all | solution.py:178
  23.6 34.7 %collective-permute-start = (bf16[4,5,1024]{2,1,0:T(8,128)(2,1)S(1)}, bf16[4,5,1024]{2,1,0:T(8,128)(2,1)S(1)}, u32[]{:S(2)}, u32[]{:S(2)}) collective-permute-start(bf16[4,5,1024]{2,1,0:T(8,128)(2,1)S(1)} %bitcast.17), channel_id=1, source_target_pairs={{0,1},{1,2},{2,3},{3,4},{4,5},{5,6},{6,7},{7,8},{8,9},{9,10},{10,1... | collective-permute-start | bytes 122888 | tf_op jit(solution)/shard_map/ppermute | solution.py:175
  27.3 34.6 %collective-permute-start.1 = (bf16[4,5,1024]{2,1,0:T(8,128)(2,1)S(1)}, bf16[4,5,1024]{2,1,0:T(8,128)(2,1)S(1)}, u32[]{:S(2)}, u32[]{:S(2)}) collective-permute-start(bf16[4,5,1024]{2,1,0:T(8,128)(2,1)S(1)} %bitcast.18), channel_id=1, source_target_pairs={{1,0},{2,1},{3,2},{4,3},{5,4},{6,5},{7,6},{8,7},{9,8},{10,9},{11,1... | collective-permute-start | bytes 122888 | tf_op jit(solution)/shard_map/ppermute | solution.py:176
  65.9 2.0 %copy-start.10 = (bf16[1280,1280]{1,0:T(8,128)(2,1)S(1)}, bf16[1280,1280]{1,0:T(8,128)(2,1)}, u32[]{:S(2)}) copy-start(bf16[1280,1280]{1,0:T(8,128)(2,1)} %deriv_ref.3) | copy-start | bytes 9830404
  71.3 1.2 copy-start.8
  72.5 4.9 %copy-start.7 = (f32[3,40,1024]{2,1,0:T(8,128)S(1)}, f32[3,40,1024]{2,1,0:T(8,128)}, u32[]{:S(2)}) copy-start(f32[3,40,1024]{2,1,0:T(8,128)} %metric_j_ref.1) | copy-start | bytes 1474564
  72.5 4.9 %copy-start.9 = (f32[3,40,1024]{2,1,0:T(8,128)S(1)}, f32[3,40,1024]{2,1,0:T(8,128)}, u32[]{:S(2)}) copy-start(f32[3,40,1024]{2,1,0:T(8,128)} %metric_i_ref.1) | copy-start | bytes 1474564
  72.5 45.6 %all-to-all-start.1 = ((bf16[32,40,640]{2,1,0:T(8,128)(2,1)}), bf16[32,40,640]{2,1,0:T(8,128)(2,1)}, u32[]{:S(2)}, u32[]{:S(2)}) async-start(bf16[32,40,640]{2,1,0:T(8,128)(2,1)} %bitcast.15), calls=%async_computation.1 | async-start | bytes 3276800 | tf_op jit(solution)/shard_map/all_to_all | solution.py:182
  77.4 1.6 %copy-start.5 = (bf16[1024,1024]{1,0:T(8,128)(2,1)S(1)}, bf16[1024,1024]{1,0:T(8,128)(2,1)}, u32[]{:S(2)}) copy-start(bf16[1024,1024]{1,0:T(8,128)(2,1)} %deriv_ref.2) | copy-start | bytes 6291460
  85.0 1.7 %copy-start.3 = (f32[4,5,40,1024]{3,2,1,0:T(8,128)}, f32[4,5,40,1024]{3,2,1,0:T(8,128)S(1)}, u32[]{:S(2)}) copy-start(f32[4,5,40,1024]{3,2,1,0:T(8,128)S(1)} %local_terms.1) | copy-start | bytes 9830404
  86.7 19.2 %copy-start.4 = (f32[4,5,40,1024]{3,2,1,0:T(8,128)S(1)}, f32[4,5,40,1024]{3,2,1,0:T(8,128)}, u32[]{:S(2)}) copy-start(f32[4,5,40,1024]{3,2,1,0:T(8,128)} %copy-done.3) | copy-start | bytes 9830404
Sparse Core Ops, SparseCore 0:
  9.2 74.1 all-gather.1

commit v2 on v1

v2 whole, which is shorter than its diff:
```python
import jax
import jax.numpy as jnp
from jax import lax
from jax.experimental import pallas as pl
from jax.experimental.pallas import tpu as pltpu
from jax.sharding import PartitionSpec as P

LANES = 128
VMEM_LIMIT = 40 * 1024 * 1024


def primitives(cons, metric):
    rho, mx, my, mz, energy = cons
    ax, ay, az = metric
    inv = 1.0 / rho
    contra = (ax * mx + ay * my + az * mz) * inv
    pressure = 0.4 * (energy - 0.5 * (mx * mx + my * my + mz * mz) * inv)
    return inv, contra, pressure


def flux_of(cons, metric, contra, pressure):
    rho, mx, my, mz, energy = cons
    ax, ay, az = metric
    return (
        rho * contra,
        mx * contra + ax * pressure,
        my * contra + ay * pressure,
        mz * contra + az * pressure,
        (energy + pressure) * contra,
    )


def radius_of(metric, inv, contra, pressure):
    ax, ay, az = metric
    return jnp.abs(contra) + jnp.sqrt(1.4 * pressure * inv * (ax * ax + ay * ay + az * az))


def flux_j_kernel(state_hbm, metric_hbm, out_hbm, state_ref, metric_ref, out_ref, in_sems, out_sems):
    nt = state_ref.shape[0]
    blocks = out_ref.shape[1]
    half = blocks // 2
    metric_copy = pltpu.make_async_copy(metric_hbm, metric_ref, in_sems.at[nt])
    metric_copy.start()
    copies = [
        pltpu.make_async_copy(state_hbm.at[t], state_ref.at[t], in_sems.at[t]) for t in range(nt)
    ]
    for copy in copies:
        copy.start()
    metric_copy.wait()
    sent = []
    for t in range(nt):
        copies[t].wait()
        for b in range(blocks):
            cols = slice(b * LANES, (b + 1) * LANES)
            cons = [state_ref[t, v, :, cols].astype(jnp.float32) for v in range(5)]
            metric = [metric_ref[c, :, cols] for c in range(3)]
            _, contra, pressure = primitives(cons, metric)
            for v, f in enumerate(flux_of(cons, metric, contra, pressure)):
                out_ref[t, b, :, v * LANES : (v + 1) * LANES] = f.astype(jnp.bfloat16)
            if (b + 1) % half == 0:
                part = pl.ds(b + 1 - half, half)
                copy = pltpu.make_async_copy(
                    out_ref.at[t, part], out_hbm.at[t, part], out_sems.at[len(sent)]
                )
                copy.start()
                sent.append(copy)
    for copy in sent:
        copy.wait()


def in_hbm(x):
    return pltpu.with_memory_space_constraint(x, pltpu.HBM)


def flux_j_blocks(state, metric_j):
    nt, nv, nj, ni = state.shape
    blocks = ni // LANES
    hbm = pl.BlockSpec(memory_space=pltpu.HBM)
    shape = (nt, blocks, nj, nv * LANES)
    return pl.pallas_call(
        flux_j_kernel,
        out_shape=pltpu.HBM(shape, jnp.bfloat16),
        in_specs=[hbm, hbm],
        out_specs=hbm,
        scratch_shapes=[
            pltpu.VMEM(state.shape, jnp.bfloat16),
            pltpu.VMEM(metric_j.shape, jnp.float32),
            pltpu.VMEM(shape, jnp.bfloat16),
            pltpu.SemaphoreType.DMA((nt + 1,)),
            pltpu.SemaphoreType.DMA((2 * nt,)),
        ],
        compiler_params=pltpu.CompilerParams(vmem_limit_bytes=VMEM_LIMIT),
        cost_estimate=pl.CostEstimate(flops=10_000_000, bytes_accessed=4_000_000, transcendentals=200_000),
        name="flux_j",
    )(in_hbm(state), in_hbm(metric_j))


def pack_kernel(me_ref, state_ref, first_ref, last_ref, *outs):
    nv, nj = state_ref.shape[1:3]
    for k, out in enumerate(outs):
        cols = pl.ds(pl.multiple_of((me_ref[0] ^ k) * LANES, LANES), LANES)
        for v in range(nv):
            out[0, v] = state_ref[0, v, :, cols]
    cons = [state_ref[0, v].astype(jnp.float32) for v in range(nv)]
    first_ref[0] = jnp.concatenate([c[:1] for c in cons], axis=0).astype(jnp.bfloat16)
    last_ref[0] = jnp.concatenate([c[nj - 1 :] for c in cons], axis=0).astype(jnp.bfloat16)


def pack_blocks(me, state):
    nt, nv, nj, ni = state.shape
    peers = ni // LANES
    block = pl.BlockSpec((1, nv, nj, LANES), lambda t: (t, 0, 0, 0))
    edge = pl.BlockSpec((1, nv, ni), lambda t: (t, 0, 0))
    first, last, *blocks = pl.pallas_call(
        pack_kernel,
        grid=(nt,),
        out_shape=[pltpu.HBM((nt, nv, ni), state.dtype)] * 2
        + [pltpu.HBM((nt, nv, nj, LANES), state.dtype)] * peers,
        in_specs=[
            pl.BlockSpec(memory_space=pltpu.SMEM),
            pl.BlockSpec((1, nv, nj, ni), lambda t: (t, 0, 0, 0)),
        ],
        out_specs=[edge] * 2 + [block] * peers,
        compiler_params=pltpu.CompilerParams(vmem_limit_bytes=VMEM_LIMIT),
        cost_estimate=pl.CostEstimate(flops=0, bytes_accessed=3_300_000, transcendentals=0),
        name="pack_blocks",
    )(me, in_hbm(state))
    return first, last, blocks


def source_weights(me, spectral, nt):
    size = spectral.shape[0]
    row = lax.broadcasted_iota(jnp.int32, (size * 8, size), 0)
    col = lax.broadcasted_iota(jnp.int32, (size * 8, size), 1)
    instance = (me ^ (row // (nt * 8))) * nt + (row // 8) % nt
    pick = jnp.where(instance == col, 1.0, 0.0).astype(jnp.bfloat16)
    rows = jnp.dot(pick, spectral, preferred_element_type=jnp.float32).astype(jnp.bfloat16)
    full = lax.dot_general(
        rows, pick, (((1,), (1,)), ((), ())), preferred_element_type=jnp.float32
    )
    r = lax.broadcasted_iota(jnp.int32, full.shape, 0)
    c = lax.broadcasted_iota(jnp.int32, full.shape, 1)
    return jnp.where(r % 8 == c % 8, full, 0.0).astype(jnp.bfloat16)


def source_kernel(me_ref, spectral_ref, deriv_hbm, *refs):
    taken, made, stage, result, in_sems, out_sems, sem = refs[-7:]
    peers = taken.shape[0]
    ins, outs, held = refs[:peers], refs[peers : 2 * peers], refs[2 * peers]
    fetches = [pltpu.make_async_copy(ins[k], taken.at[k], in_sems.at[k]) for k in range(peers)]
    for copy in fetches:
        copy.start()
    fetch = pltpu.make_async_copy(deriv_hbm, held, sem)
    fetch.start()
    nt, nv, nj = taken.shape[1:4]
    tiles = nj // 8
    weights = source_weights(me_ref[0], spectral_ref[...], nt)
    for k in range(peers):
        fetches[k].wait()
        for t in range(nt):
            m = k * nt + t
            for v in range(nv):
                x = taken[k, t, v].astype(jnp.float32)
                for b in range(tiles):
                    stage[b, m * 8 : (m + 1) * 8, v * LANES : (v + 1) * LANES] = x[b * 8 : (b + 1) * 8]
    for b in range(tiles):
        result[b] = jnp.dot(
            weights, stage[b].astype(jnp.bfloat16), preferred_element_type=jnp.float32
        )
    sent = []
    for k in range(peers):
        for t in range(nt):
            n = k * nt + t
            for v in range(nv):
                parts = [
                    result[b, n * 8 : (n + 1) * 8, v * LANES : (v + 1) * LANES] for b in range(tiles)
                ]
                made[k, t, v] = jnp.concatenate(parts, axis=0).astype(jnp.bfloat16)
        copy = pltpu.make_async_copy(made.at[k], outs[k], out_sems.at[k])
        copy.start()
        sent.append(copy)
    for copy in sent:
        copy.wait()
    fetch.wait()


def source_blocks(me, spectral, deriv_j, blocks):
    shape = blocks[0].shape
    nt, nv, nj, _ = shape
    peers = len(blocks)
    rows = peers * nt * 8
    vmem = pl.BlockSpec(memory_space=pltpu.VMEM)
    hbm = pl.BlockSpec(memory_space=pltpu.HBM)
    *sources, held = pl.pallas_call(
        source_kernel,
        out_shape=[pltpu.HBM(shape, jnp.bfloat16)] * peers
        + [pltpu.VMEM(deriv_j.shape, deriv_j.dtype)],
        in_specs=[pl.BlockSpec(memory_space=pltpu.SMEM), vmem, hbm] + [hbm] * peers,
        out_specs=[hbm] * peers + [vmem],
        scratch_shapes=[pltpu.VMEM((peers,) + shape, jnp.bfloat16)] * 2
        + [pltpu.VMEM((nj // 8, rows, nv * LANES), jnp.float32)] * 2
        + [pltpu.SemaphoreType.DMA((peers,))] * 2
        + [pltpu.SemaphoreType.DMA],
        compiler_params=pltpu.CompilerParams(vmem_limit_bytes=VMEM_LIMIT),
        cost_estimate=pl.CostEstimate(flops=420_000_000, bytes_accessed=10_000_000, transcendentals=0),
        name="source_blocks",
    )(me, spectral, in_hbm(deriv_j), *[in_hbm(b) for b in blocks])
    return sources, held


def local_kernel(
    me_ref, state_ref, metric_i_ref, metric_j_ref, low_ref, high_ref, deriv_ref, *refs
):
    sources, out_ref, flux_ref = refs[:-2], refs[-2], refs[-1]
    nv, nj, ni = state_ref.shape[1:]
    metric_i = [metric_i_ref[c] for c in range(3)]
    cons = [state_ref[0, v].astype(jnp.float32) for v in range(nv)]
    inv, contra, pressure = primitives(cons, metric_i)
    for v, f in enumerate(flux_of(cons, metric_i, contra, pressure)):
        flux_ref[v * nj : (v + 1) * nj, :] = f
    radius_i = 0.25 * radius_of(metric_i, inv, contra, pressure)
    metric_j = [metric_j_ref[c] for c in range(3)]
    inv, contra, pressure = primitives(cons, metric_j)
    radius_j = 0.25 * radius_of(metric_j, inv, contra, pressure)
    term = lax.dot_general(
        flux_ref[...].astype(jnp.bfloat16),
        deriv_ref[...],
        (((1,), (1,)), ((), ())),
        preferred_element_type=jnp.float32,
    )
    row = lax.broadcasted_iota(jnp.int32, (nj, ni), 0)
    col = lax.broadcasted_iota(jnp.int32, (nj, ni), 1)
    low = low_ref[0].astype(jnp.float32)
    high = high_ref[0].astype(jnp.float32)
    for v in range(nv):
        c = cons[v]
        right = jnp.where(col == ni - 1, 0.0, pltpu.roll(c, ni - 1, 1))
        left = jnp.where(col == 0, 0.0, pltpu.roll(c, 1, 1))
        up = jnp.where(row == nj - 1, high[v : v + 1], pltpu.roll(c, nj - 1, 0))
        down = jnp.where(row == 0, low[v : v + 1], pltpu.roll(c, 1, 0))
        twice = 2.0 * c
        damping = radius_i * (right + left - twice) + radius_j * (up + down - twice)
        out_ref[0, v] = term[v * nj : (v + 1) * nj] - damping
    for k, source_ref in enumerate(sources):
        cols = pl.ds(pl.multiple_of((me_ref[0] ^ k) * LANES, LANES), LANES)
        for v in range(nv):
            out_ref[0, v, :, cols] += source_ref[0, v].astype(jnp.float32)


def local_terms(me, state, metric_i, metric_j, low, high, deriv_i, sources):
    nt, nv, nj, ni = state.shape
    whole3 = pl.BlockSpec((3, nj, ni), lambda t: (0, 0, 0))
    halo = pl.BlockSpec((1, nv, ni), lambda t: (t, 0, 0))
    per_t = pl.BlockSpec((1, nv, nj, ni), lambda t: (t, 0, 0, 0))
    block = pl.BlockSpec((1, nv, nj, LANES), lambda t: (t, 0, 0, 0))
    return pl.pallas_call(
        local_kernel,
        grid=(nt,),
        out_shape=pltpu.VMEM((nt, nv, nj, ni), jnp.float32),
        in_specs=[
            pl.BlockSpec(memory_space=pltpu.SMEM),
            per_t,
            whole3,
            whole3,
            halo,
            halo,
            pl.BlockSpec((ni, ni), lambda t: (0, 0)),
        ]
        + [block] * len(sources),
        out_specs=per_t,
        scratch_shapes=[pltpu.VMEM((nv * nj, ni), jnp.float32)],
        compiler_params=pltpu.CompilerParams(vmem_limit_bytes=VMEM_LIMIT),
        cost_estimate=pl.CostEstimate(
            flops=2 * nt * nv * nj * ni * ni, bytes_accessed=11_000_000, transcendentals=600_000
        ),
        name="local_terms",
    )(me, *[in_hbm(x) for x in (state, metric_i, metric_j, low, high, deriv_i, *sources)])


ROWS = 256


def slope_kernel(deriv_ref, lines_hbm, out_hbm, lines_ref, out_ref, in_sems, out_sems):
    chunks = out_ref.shape[0] // ROWS
    pieces = [pl.ds(c * ROWS, ROWS) for c in range(chunks)]
    fetches = [
        pltpu.make_async_copy(lines_hbm.at[p], lines_ref.at[p], in_sems.at[c])
        for c, p in enumerate(pieces)
    ]
    for copy in fetches:
        copy.start()
    copies = []
    for c, rows in enumerate(pieces):
        if c == 0:
            total = None
            for d, p in enumerate(pieces):
                fetches[d].wait()
                part = jnp.dot(
                    deriv_ref[rows, d * ROWS : (d + 1) * ROWS],
                    lines_ref[p, :],
                    preferred_element_type=jnp.float32,
                )
                total = part if total is None else total + part
        else:
            total = jnp.dot(deriv_ref[rows, :], lines_ref[...], preferred_element_type=jnp.float32)
        out_ref[rows, :] = total.astype(jnp.bfloat16)
        copy = pltpu.make_async_copy(out_ref.at[rows], out_hbm.at[rows], out_sems.at[c])
        copy.start()
        copies.append(copy)
    for copy in copies:
        copy.wait()


def slope_lines(deriv_j, lines):
    size, width = lines.shape
    hbm = pl.BlockSpec(memory_space=pltpu.HBM)
    return pl.pallas_call(
        slope_kernel,
        out_shape=pltpu.HBM((size, width), jnp.bfloat16),
        in_specs=[pl.BlockSpec(memory_space=pltpu.VMEM), hbm],
        out_specs=hbm,
        scratch_shapes=[pltpu.VMEM((size, width), jnp.bfloat16)] * 2
        + [pltpu.SemaphoreType.DMA((size // ROWS,))] * 2,
        compiler_params=pltpu.CompilerParams(vmem_limit_bytes=VMEM_LIMIT),
        cost_estimate=pl.CostEstimate(
            flops=2 * size * size * width, bytes_accessed=7_000_000, transcendentals=0
        ),
        name="slope_lines",
    )(deriv_j, in_hbm(lines))


def finish_kernel(total_ref, slope_hbm, out_hbm, slope_ref, out_ref, in_sems, out_sems):
    nt, nv = total_ref.shape[:2]
    copies = [
        pltpu.make_async_copy(slope_hbm.at[t], slope_ref.at[t], in_sems.at[t]) for t in range(nt)
    ]
    for copy in copies:
        copy.start()
    sent = []
    for t in range(nt):
        copies[t].wait()
        for b in range(slope_ref.shape[1]):
            cols = slice(b * LANES, (b + 1) * LANES)
            for v in range(nv):
                s = slope_ref[t, b, :, v * LANES : (v + 1) * LANES].astype(jnp.float32)
                out_ref[t, v, :, cols] = (total_ref[t, v, :, cols] + s).astype(jnp.bfloat16)
        copy = pltpu.make_async_copy(out_ref.at[t], out_hbm.at[t], out_sems.at[t])
        copy.start()
        sent.append(copy)
    for copy in sent:
        copy.wait()


def finish(total, slope):
    nt = total.shape[0]
    hbm = pl.BlockSpec(memory_space=pltpu.HBM)
    return pl.pallas_call(
        finish_kernel,
        out_shape=jax.ShapeDtypeStruct(total.shape, jnp.bfloat16),
        in_specs=[pl.BlockSpec(memory_space=pltpu.VMEM), hbm],
        out_specs=hbm,
        scratch_shapes=[
            pltpu.VMEM(slope.shape, jnp.bfloat16),
            pltpu.VMEM(total.shape, jnp.bfloat16),
            pltpu.SemaphoreType.DMA((nt,)),
            pltpu.SemaphoreType.DMA((nt,)),
        ],
        compiler_params=pltpu.CompilerParams(vmem_limit_bytes=VMEM_LIMIT),
        cost_estimate=pl.CostEstimate(flops=1_000_000, bytes_accessed=7_000_000, transcendentals=0),
        name="finish",
    )(total, in_hbm(slope))


def on_device(state, spectral, deriv_i, deriv_j, metric_i, metric_j):
    nt, nv, nj, ni = state.shape
    count = lax.axis_size("space")
    forward = [(i, i + 1) for i in range(count - 1)]
    backward = [(target, source) for source, target in forward]
    peers = lax.axis_size("tm")
    swaps = [[(i, i ^ k) for i in range(peers)] for k in range(peers)]
    rank = lax.axis_index("tm")
    me = jnp.reshape(rank, (1,)).astype(jnp.int32)
    outgoing = flux_j_blocks(state, metric_j).reshape(count, nj, nv * LANES)
    lines = lax.all_to_all(outgoing, "space", split_axis=0, concat_axis=0, tiled=True)
    first, last, own = pack_blocks(me, state)
    low = lax.ppermute(last, "space", forward)
    high = lax.ppermute(first, "space", backward)
    blocks = own[:1] + [lax.ppermute(own[k], "tm", swaps[k]) for k in range(1, peers)]
    sources, held = source_blocks(me, spectral, deriv_j, blocks)
    lines, low, high = lax.optimization_barrier((lines, low, high))
    sources = sources[:1] + [lax.ppermute(sources[k], "tm", swaps[k]) for k in range(1, peers)]
    partial = local_terms(me, state, metric_i, metric_j, low, high, deriv_i, sources)
    slope = slope_lines(held, lines.reshape(count * nj, nv * LANES))
    slope = lax.all_to_all(
        slope.reshape(count, nj, nv * LANES), "space", split_axis=0, concat_axis=0, tiled=True
    )
    return finish(partial, slope.reshape(nt, ni // LANES, nj, nv * LANES))


def solution(mesh):
    return jax.shard_map(
        on_device,
        mesh=mesh,
        in_specs=(
            P("tm", None, "space", None),
            P(),
            P(),
            P(),
            P(None, "space", None),
            P(None, "space", None),
        ),
        out_specs=P("tm", None, "space", None),
        check_vma=False,
    )
```

time: 129 us -> 111 us (0.86)
  matrix products: 19.2 us -> 0 us
  between operations: 13.5 us -> 0.43 us
  starting transfers between devices: 21.3 us -> 32.9 us
  Pallas kernels: 15.3 us -> 26.5 us
  local copies, waits for them, and re-layouts: 9.1 us -> 1.37 us
  other arithmetic: 1.95 us -> 0 us
    dot_general x1 -> x0, matrix products: 19.2 us -> none  [on_device(): jnp.einsum('nm,mvji->nvji', own_rows, gathered, preferred_element_type=jn...]
    ppermute x2 -> x16, starting transfers between devices: 4.99 us -> 16.4 us  [the longest x7 5.8 us: on_device(): lax.ppermute(sources[k], 'tm', swaps[k])]
    pallas_call x4 -> x6, Pallas kernels: 15.3 us -> 26.5 us  [the longest x1 8.7 us: local_terms(): pl.pallas_call(local_kernel, grid=(nt,), out_shape=pltpu.VMEM((nt, nv, nj...]
    unnamed x24 -> x48, local copies, waits for them, and re-layouts: 8.97 us -> 1.37 us
    ppermute x2 -> x16, waiting for transfers between devices: 33.3 us -> 39.3 us  [the longest x7 19.6 us: on_device(): lax.ppermute(sources[k], 'tm', swaps[k])]
    all_to_all x1, waiting for transfers between devices: 10.3 us -> 5.79 us  [on_device(): lax.all_to_all(slope.reshape(count, nj, nv * LANES), 'space', split_axis=...]
    add x1 -> x0, other arithmetic: 1.95 us -> none  [on_device(): total = source + partial]
  transfers between devices with their start and end apart: 5 -> 18, of which waited for: 4 -> 16; matrix products, arithmetic and copies ran while one was open for 17% -> 0% of each run, Pallas kernels for 9% -> 15%
where the time goes in v2:
time: 111 us; the launch traced here: 110 us
  waiting for transfers between devices  49.2 us (44%)
  starting transfers between devices  32.9 us (30%)
  Pallas kernels  26.5 us (24%)
  local copies, waits for them, and re-layouts  1.37 us (1%)
    ppermute x7, waiting for transfers between devices, on_device(): lax.ppermute(sources[k], 'tm', swaps[k])  19.6 us
    ppermute x7, waiting for transfers between devices, on_device(): lax.ppermute(own[k], 'tm', swaps[k])  14.9 us
    all_to_all x1, starting transfers between devices, on_device(): lax.all_to_all(outgoing, 'space', split_axis=0, concat_axis=0, tiled=True)  11.6 us
    pallas_call x1, Pallas kernels, local_terms(): pl.pallas_call(local_kernel, grid=(nt,), out_shape=pltpu.VMEM((nt, nv, nj...  8.7 us
    ppermute x7, starting transfers between devices, on_device(): lax.ppermute(sources[k], 'tm', swaps[k])  5.8 us
    all_to_all x1, waiting for transfers between devices, on_device(): lax.all_to_all(slope.reshape(count, nj, nv * LANES), 'space', split_axis=...  5.79 us
    ppermute x7, starting transfers between devices, on_device(): lax.ppermute(own[k], 'tm', swaps[k])  5.71 us
    pallas_call x1, Pallas kernels, slope_lines(): pl.pallas_call(slope_kernel, out_shape=pltpu.HBM((size, width), jnp.bfloa...  5.31 us
  transfers between devices with their start and end apart: 18, of which 16 were waited for; matrix products, arithmetic and copies ran while one was open for 0% of the time, Pallas kernels for 15%

profile of v2, /device:TPU:4, one launch (start us, length us, event | category | flops | bytes accessed | tf_op | source)
XLA Modules:
  0.0 110.4 jit_solution(17769480717509906061)
XLA Ops:
  0.0 2.8 %flux_j.1 = bf16[4,8,40,640]{3,2,1,0:T(8,128)(2,1)} custom-call(bf16[4,5,40,1024]{3,2,1,0:T(8,128)(2,1)} %state_ref.3, f32[3,40,1024]{2,1,0:T(8,128)} %metric_j_ref.1), custom_call_target="tpu_custom_call" | custom-call | flops 10000000 | bytes 4000000 | tf_op jit(solution)/shard_map/flux_j/pallas_call | solution.py:80
  2.8 11.6 %all-to-all-start = ((bf16[32,40,640]{2,1,0:T(8,128)(2,1)}), bf16[32,40,640]{2,1,0:T(8,128)(2,1)}, u32[]{:S(2)}, u32[]{:S(2)}) async-start(bf16[32,40,640]{2,1,0:T(8,128)(2,1)} %bitcast.5), calls=%async_computation | async-start | bytes 3276800 | tf_op jit(solution)/shard_map/all_to_all | solution.py:384
  14.4 0.0 copy-start
  14.5 3.9 %pack_blocks.1 = (bf16[4,5,1024]{2,1,0:T(8,128)(2,1)}, bf16[4,5,1024]{2,1,0:T(8,128)(2,1)}, bf16[4,5,40,128]{3,2,1,0:T(8,128)(2,1)}, bf16[4,5,40,128]{3,2,1,0:T(...) custom-call(s32[1]{0:T(128)} %bitcast.me_ref, ...), custom_call_target="tpu_custom_call" | custom-call | bytes 3300000 | tf_op jit(solution)/shard_map/pack_blocks/pallas_call | solution.py:114
  18.3 0.1 collective-permute-start.2
  18.4 1.3 %collective-permute-start.3 = (bf16[4,5,40,128]{3,2,1,0:T(8,128)(2,1)}, bf16[4,5,40,128]{3,2,1,0:T(8,128)(2,1)S(1)}, u32[]{:S(2)}, u32[]{:S(2)}) collective-permute-start(bf16[4,5,40,128]{3,2,1,0:T(8,128)(2,1)} %get-tuple-element.33), channel_id=1, source_target_pairs={{0,64},{32,96},{64,0},{96,32},{128,192},{160,224},{192,128},{224,1... | collective-permute-start | bytes 614408 | tf_op jit(solution)/shard_map/ppermute | solution.py:388
  19.7 0.6 collective-permute-start.4
  20.3 0.5 collective-permute-start.5
  20.8 2.7 %collective-permute-start.6 = (bf16[4,5,40,128]{3,2,1,0:T(8,128)(2,1)}, bf16[4,5,40,128]{3,2,1,0:T(8,128)(2,1)S(1)}, u32[]{:S(2)}, u32[]{:S(2)}) collective-permute-start(bf16[4,5,40,128]{3,2,1,0:T(8,128)(2,1)} %get-tuple-element.36), channel_id=1, source_target_pairs={{0,160},{32,128},{64,224},{96,192},{128,32},{160,0},{192,96},{224,... | collective-permute-start | bytes 614408 | tf_op jit(solution)/shard_map/ppermute | solution.py:388
  23.5 0.0 collective-permute-done.2.refs_1_
  23.5 0.5 collective-permute-start.7
  24.0 2.5 %collective-permute-done.3.refs_2_ = bf16[4,5,40,128]{3,2,1,0:T(8,128)(2,1)S(1)} collective-permute-done((bf16[4,5,40,128]{3,2,1,0:T(8,128)(2,1)}, bf16[4,5,40,128]{3,2,1,0:T(8,128)(2,1)S(1)}, u32[]{:S(2)}, u32[]{:S(2)}) %collective-permute-start.3) | collective-permute-done | bytes 204832 | tf_op jit(solution)/shard_map/ppermute | solution.py:388
  26.6 0.0 collective-permute-start.8
  26.6 3.4 %collective-permute-done.4.refs_3_ = bf16[4,5,40,128]{3,2,1,0:T(8,128)(2,1)S(1)} collective-permute-done((bf16[4,5,40,128]{3,2,1,0:T(8,128)(2,1)}, bf16[4,5,40,128]{3,2,1,0:T(8,128)(2,1)S(1)}, u32[]{:S(2)}, u32[]{:S(2)}) %collective-permute-start.4) | collective-permute-done | bytes 204832 | tf_op jit(solution)/shard_map/ppermute | solution.py:388
  30.0 3.6 %collective-permute-start = (bf16[4,5,1024]{2,1,0:T(8,128)(2,1)}, bf16[4,5,1024]{2,1,0:T(8,128)(2,1)S(1)}, u32[]{:S(2)}, u32[]{:S(2)}) collective-permute-start(bf16[4,5,1024]{2,1,0:T(8,128)(2,1)} %get-tuple-element.27), channel_id=1, source_target_pairs={{0,1},{1,2},{2,3},{3,4},{4,5},{5,6},{6,7},{7,8},{8,9},{9,10},{10,1... | collective-permute-start | bytes 122888 | tf_op jit(solution)/shard_map/ppermute | solution.py:386
  33.7 1.8 %collective-permute-done.5.refs_4_ = bf16[4,5,40,128]{3,2,1,0:T(8,128)(2,1)S(1)} collective-permute-done((bf16[4,5,40,128]{3,2,1,0:T(8,128)(2,1)}, bf16[4,5,40,128]{3,2,1,0:T(8,128)(2,1)S(1)}, u32[]{:S(2)}, u32[]{:S(2)}) %collective-permute-start.5) | collective-permute-done | bytes 204832 | tf_op jit(solution)/shard_map/ppermute | solution.py:388
  35.5 1.3 %collective-permute-start.1 = (bf16[4,5,1024]{2,1,0:T(8,128)(2,1)}, bf16[4,5,1024]{2,1,0:T(8,128)(2,1)S(1)}, u32[]{:S(2)}, u32[]{:S(2)}) collective-permute-start(bf16[4,5,1024]{2,1,0:T(8,128)(2,1)} %get-tuple-element.28), channel_id=1, source_target_pairs={{1,0},{2,1},{3,2},{4,3},{5,4},{6,5},{7,6},{8,7},{9,8},{10,9},{11,1... | collective-permute-start | bytes 122888 | tf_op jit(solution)/shard_map/ppermute | solution.py:387
  36.7 2.1 %collective-permute-done.6.refs_5_ = bf16[4,5,40,128]{3,2,1,0:T(8,128)(2,1)S(1)} collective-permute-done((bf16[4,5,40,128]{3,2,1,0:T(8,128)(2,1)}, bf16[4,5,40,128]{3,2,1,0:T(8,128)(2,1)S(1)}, u32[]{:S(2)}, u32[]{:S(2)}) %collective-permute-start.6) | collective-permute-done | bytes 204832 | tf_op jit(solution)/shard_map/ppermute | solution.py:388
  38.9 1.5 %collective-permute-done.7.refs_6_ = bf16[4,5,40,128]{3,2,1,0:T(8,128)(2,1)S(1)} collective-permute-done((bf16[4,5,40,128]{3,2,1,0:T(8,128)(2,1)}, bf16[4,5,40,128]{3,2,1,0:T(8,128)(2,1)S(1)}, u32[]{:S(2)}, u32[]{:S(2)}) %collective-permute-start.7) | collective-permute-done | bytes 204832 | tf_op jit(solution)/shard_map/ppermute | solution.py:388
  40.4 3.5 %collective-permute-done.8.refs_7_ = bf16[4,5,40,128]{3,2,1,0:T(8,128)(2,1)S(1)} collective-permute-done((bf16[4,5,40,128]{3,2,1,0:T(8,128)(2,1)}, bf16[4,5,40,128]{3,2,1,0:T(8,128)(2,1)S(1)}, u32[]{:S(2)}, u32[]{:S(2)}) %collective-permute-start.8) | collective-permute-done | bytes 204832 | tf_op jit(solution)/shard_map/ppermute | solution.py:388
  43.9 0.6 copy-done.14
  44.5 3.5 %source_blocks.1 = (bf16[4,5,40,128]{3,2,1,0:T(8,128)(2,1)}, bf16[4,5,40,128]{3,2,1,0:T(8,128)(2,1)}, bf16[4,5,40,128]{3,2,1,0:T(8,128)(2,1)}, bf16[4,5,40,128]{...) custom-call(s32[1]{0:T(128)} %bitcast.me_ref, ...), custom_call_target="tpu_custom_call" | custom-call | flops 420000000 | bytes 10000000 | tf_op jit(solution)/shard_map/source_blocks/pallas_call | solution.py:194
  48.0 1.3 %collective-permute-done.low_ref = bf16[4,5,1024]{2,1,0:T(8,128)(2,1)S(1)} collective-permute-done((bf16[4,5,1024]{2,1,0:T(8,128)(2,1)}, bf16[4,5,1024]{2,1,0:T(8,128)(2,1)S(1)}, u32[]{:S(2)}, u32[]{:S(2)}) %collective-permute-start) | collective-permute-done | bytes 40992 | tf_op jit(solution)/shard_map/ppermute | solution.py:386
  49.4 3.5 %collective-permute-done.1.high_ref = bf16[4,5,1024]{2,1,0:T(8,128)(2,1)S(1)} collective-permute-done((bf16[4,5,1024]{2,1,0:T(8,128)(2,1)}, bf16[4,5,1024]{2,1,0:T(8,128)(2,1)S(1)}, u32[]{:S(2)}, u32[]{:S(2)}) %collective-permute-start.1) | collective-permute-done | bytes 40992 | tf_op jit(solution)/shard_map/ppermute | solution.py:387
  52.9 4.1 %all-to-all-done = bf16[32,40,640]{2,1,0:T(8,128)(2,1)} async-done(((bf16[32,40,640]{2,1,0:T(8,128)(2,1)}), bf16[32,40,640]{2,1,0:T(8,128)(2,1)}, u32[]{:S(2)}, u32[]{:S(2)}) %all-to-all-start) | async-done | bytes 1638432 | tf_op jit(solution)/shard_map/all_to_all | solution.py:384
  57.0 5.3 %slope_lines.1 = bf16[1280,640]{1,0:T(8,128)(2,1)} custom-call(bf16[1280,1280]{1,0:T(8,128)(2,1)S(1)} %get-tuple-element.47.deriv_ref, bf16[1280,640]{1,0:T(8,128)(2,1)} %bitcast.2.lines_hbm), custom_call_target="tpu_custom_call" | custom-call | flops 2097152000 | bytes 7000000 | tf_op jit(solution)/shard_map/slope_lines/pallas_call | solution.py:317
  62.3 0.0 copy-done.15
  62.3 0.0 copy-done.16
  62.3 0.0 copy-start.23
  62.4 4.8 %all-to-all-start.1 = ((bf16[32,40,640]{2,1,0:T(8,128)(2,1)}), bf16[32,40,640]{2,1,0:T(8,128)(2,1)}, u32[]{:S(2)}, u32[]{:S(2)}) async-start(bf16[32,40,640]{2,1,0:T(8,128)(2,1)} %bitcast.6), calls=%async_computation.1 | async-start | bytes 3276800 | tf_op jit(solution)/shard_map/all_to_all | solution.py:394
  67.2 0.1 collective-permute-start.9
  67.3 1.3 %collective-permute-start.10 = (bf16[4,5,40,128]{3,2,1,0:T(8,128)(2,1)S(1)}, bf16[4,5,40,128]{3,2,1,0:T(8,128)(2,1)S(1)}, u32[]{:S(2)}, u32[]{:S(2)}) collective-permute-start(bf16[4,5,40,128]{3,2,1,0:T(8,128)(2,1)S(1)} %copy-done.22), channel_id=1, source_target_pairs={{0,64},{32,96},{64,0},{96,32},{128,192},{160,224},{192,128},{224,1... | collective-permute-start | bytes 614408 | tf_op jit(solution)/shard_map/ppermute | solution.py:391
  68.6 0.6 collective-permute-start.11
  69.2 0.5 collective-permute-start.12
  69.7 2.7 %collective-permute-start.13 = (bf16[4,5,40,128]{3,2,1,0:T(8,128)(2,1)S(1)}, bf16[4,5,40,128]{3,2,1,0:T(8,128)(2,1)S(1)}, u32[]{:S(2)}, u32[]{:S(2)}) collective-permute-start(bf16[4,5,40,128]{3,2,1,0:T(8,128)(2,1)S(1)} %copy-done.19), channel_id=1, source_target_pairs={{0,160},{32,128},{64,224},{96,192},{128,32},{160,0},{192,96},{224,... | collective-permute-start | bytes 614408 | tf_op jit(solution)/shard_map/ppermute | solution.py:391
  72.4 0.0 collective-permute-done.9.refs_1_
  72.4 0.6 collective-permute-start.14
  73.1 2.2 %collective-permute-done.10.refs_2_ = bf16[4,5,40,128]{3,2,1,0:T(8,128)(2,1)S(1)} collective-permute-done((bf16[4,5,40,128]{3,2,1,0:T(8,128)(2,1)S(1)}, bf16[4,5,40,128]{3,2,1,0:T(8,128)(2,1)S(1)}, u32[]{:S(2)}, u32[]{:S(2)}) %collective-permute-start.10) | collective-permute-done | bytes 204832 | tf_op jit(solution)/shard_map/ppermute | solution.py:391
  75.3 0.0 collective-permute-start.15
  75.3 3.4 %collective-permute-done.11.refs_3_ = bf16[4,5,40,128]{3,2,1,0:T(8,128)(2,1)S(1)} collective-permute-done((bf16[4,5,40,128]{3,2,1,0:T(8,128)(2,1)S(1)}, bf16[4,5,40,128]{3,2,1,0:T(8,128)(2,1)S(1)}, u32[]{:S(2)}, u32[]{:S(2)}) %collective-permute-start.11) | collective-permute-done | bytes 204832 | tf_op jit(solution)/shard_map/ppermute | solution.py:391
  78.8 5.4 %collective-permute-done.12.refs_4_ = bf16[4,5,40,128]{3,2,1,0:T(8,128)(2,1)S(1)} collective-permute-done((bf16[4,5,40,128]{3,2,1,0:T(8,128)(2,1)S(1)}, bf16[4,5,40,128]{3,2,1,0:T(8,128)(2,1)S(1)}, u32[]{:S(2)}, u32[]{:S(2)}) %collective-permute-start.12) | collective-permute-done | bytes 204832 | tf_op jit(solution)/shard_map/ppermute | solution.py:391
  84.2 3.4 %collective-permute-done.13.refs_5_ = bf16[4,5,40,128]{3,2,1,0:T(8,128)(2,1)S(1)} collective-permute-done((bf16[4,5,40,128]{3,2,1,0:T(8,128)(2,1)S(1)}, bf16[4,5,40,128]{3,2,1,0:T(8,128)(2,1)S(1)}, u32[]{:S(2)}, u32[]{:S(2)}) %collective-permute-start.13) | collective-permute-done | bytes 204832 | tf_op jit(solution)/shard_map/ppermute | solution.py:391
  87.6 1.6 %collective-permute-done.14.refs_6_ = bf16[4,5,40,128]{3,2,1,0:T(8,128)(2,1)S(1)} collective-permute-done((bf16[4,5,40,128]{3,2,1,0:T(8,128)(2,1)S(1)}, bf16[4,5,40,128]{3,2,1,0:T(8,128)(2,1)S(1)}, u32[]{:S(2)}, u32[]{:S(2)}) %collective-permute-start.14) | collective-permute-done | bytes 204832 | tf_op jit(solution)/shard_map/ppermute | solution.py:391
  89.2 3.5 %collective-permute-done.15.refs_7_ = bf16[4,5,40,128]{3,2,1,0:T(8,128)(2,1)S(1)} collective-permute-done((bf16[4,5,40,128]{3,2,1,0:T(8,128)(2,1)S(1)}, bf16[4,5,40,128]{3,2,1,0:T(8,128)(2,1)S(1)}, u32[]{:S(2)}, u32[]{:S(2)}) %collective-permute-start.15) | collective-permute-done | bytes 204832 | tf_op jit(solution)/shard_map/ppermute | solution.py:391
  92.7 0.6 copy-done.7
  93.3 8.7 %local_terms.1.total_ref = f32[4,5,40,1024]{3,2,1,0:T(8,128)S(1)} custom-call(s32[1]{0:T(128)} %bitcast.me_ref, bf16[4,5,40,1024]{3,2,1,0:T(8,128)(2,1)} %state_ref.3, f32[3,40,1024]{2,1,0:T(8,128)} %metric_i_ref.1, f32[3,40,1024]{2,1,0:T(8,128)} %metric_j_ref.1, bf16[4,5,1024]{2,1,0:T(8,128)(2,1)} %copy-done.15, bf16[4,5,1024]{2,1,0:T(8,128)(2,1)} %copy-done.16, ...), custom_call_target="tpu_custom_call" | custom-call | flops 1677721600 | bytes 11000000 | tf_op jit(solution)/shard_map/local_terms/pallas_call | solution.py:256
  102.1 5.8 %all-to-all-done.1 = bf16[32,40,640]{2,1,0:T(8,128)(2,1)} async-done(((bf16[32,40,640]{2,1,0:T(8,128)(2,1)}), bf16[32,40,640]{2,1,0:T(8,128)(2,1)}, u32[]{:S(2)}, u32[]{:S(2)}) %all-to-all-start.1) | async-done | bytes 1638432 | tf_op jit(solution)/shard_map/all_to_all | solution.py:394
  107.9 2.3 %finish.1 = bf16[4,5,40,1024]{3,2,1,0:T(8,128)(2,1)} custom-call(f32[4,5,40,1024]{3,2,1,0:T(8,128)S(1)} %local_terms.1.total_ref, bf16[4,8,40,640]{3,2,1,0:T(8,128)(2,1)} %bitcast.4.slope_hbm), custom_call_target="tpu_custom_call" | custom-call | flops 1000000 | bytes 7000000 | tf_op jit(solution)/shard_map/finish/pallas_call | solution.py:357
  (42 shorter events, 0.1 us)
Async XLA Ops:
  2.8 54.1 %all-to-all-start = ((bf16[32,40,640]{2,1,0:T(8,128)(2,1)}), bf16[32,40,640]{2,1,0:T(8,128)(2,1)}, u32[]{:S(2)}, u32[]{:S(2)}) async-start(bf16[32,40,640]{2,1,0:T(8,128)(2,1)} %bitcast.5), calls=%async_computation | async-start | bytes 3276800 | tf_op jit(solution)/shard_map/all_to_all | solution.py:384
  14.4 30.1 %copy-start = (bf16[32,32]{1,0:T(8,128)(2,1)S(1)}, bf16[32,32]{1,0:T(8,128)(2,1)}, u32[]{:S(2)}) copy-start(bf16[32,32]{1,0:T(8,128)(2,1)} %spectral_ref.1) | copy-start | bytes 6148
  18.3 5.2 %collective-permute-start.2 = (bf16[4,5,40,128]{3,2,1,0:T(8,128)(2,1)}, bf16[4,5,40,128]{3,2,1,0:T(8,128)(2,1)S(1)}, u32[]{:S(2)}, u32[]{:S(2)}) collective-permute-start(bf16[4,5,40,128]{3,2,1,0:T(8,128)(2,1)} %get-tuple-element.32), channel_id=1, source_target_pairs={{0,32},{32,0},{64,96},{96,64},{128,160},{160,128},{192,224},{224,1... | collective-permute-start | bytes 614408 | tf_op jit(solution)/shard_map/ppermute | solution.py:388
  18.4 8.2 %collective-permute-start.3 = (bf16[4,5,40,128]{3,2,1,0:T(8,128)(2,1)}, bf16[4,5,40,128]{3,2,1,0:T(8,128)(2,1)S(1)}, u32[]{:S(2)}, u32[]{:S(2)}) collective-permute-start(bf16[4,5,40,128]{3,2,1,0:T(8,128)(2,1)} %get-tuple-element.33), channel_id=1, source_target_pairs={{0,64},{32,96},{64,0},{96,32},{128,192},{160,224},{192,128},{224,1... | collective-permute-start | bytes 614408 | tf_op jit(solution)/shard_map/ppermute | solution.py:388
  19.7 10.3 %collective-permute-start.4 = (bf16[4,5,40,128]{3,2,1,0:T(8,128)(2,1)}, bf16[4,5,40,128]{3,2,1,0:T(8,128)(2,1)S(1)}, u32[]{:S(2)}, u32[]{:S(2)}) collective-permute-start(bf16[4,5,40,128]{3,2,1,0:T(8,128)(2,1)} %get-tuple-element.34), channel_id=1, source_target_pairs={{0,96},{32,64},{64,32},{96,0},{128,224},{160,192},{192,160},{224,1... | collective-permute-start | bytes 614408 | tf_op jit(solution)/shard_map/ppermute | solution.py:388
  20.3 15.2 %collective-permute-start.5 = (bf16[4,5,40,128]{3,2,1,0:T(8,128)(2,1)}, bf16[4,5,40,128]{3,2,1,0:T(8,128)(2,1)S(1)}, u32[]{:S(2)}, u32[]{:S(2)}) collective-permute-start(bf16[4,5,40,128]{3,2,1,0:T(8,128)(2,1)} %get-tuple-element.35), channel_id=1, source_target_pairs={{0,128},{32,160},{64,192},{96,224},{128,0},{160,32},{192,64},{224,... | collective-permute-start | bytes 614408 | tf_op jit(solution)/shard_map/ppermute | solution.py:388
  20.8 18.1 %collective-permute-start.6 = (bf16[4,5,40,128]{3,2,1,0:T(8,128)(2,1)}, bf16[4,5,40,128]{3,2,1,0:T(8,128)(2,1)S(1)}, u32[]{:S(2)}, u32[]{:S(2)}) collective-permute-start(bf16[4,5,40,128]{3,2,1,0:T(8,128)(2,1)} %get-tuple-element.36), channel_id=1, source_target_pairs={{0,160},{32,128},{64,224},{96,192},{128,32},{160,0},{192,96},{224,... | collective-permute-start | bytes 614408 | tf_op jit(solution)/shard_map/ppermute | solution.py:388
  23.5 20.3 %copy-start.8 = (bf16[4,5,40,128]{3,2,1,0:T(8,128)(2,1)}, bf16[4,5,40,128]{3,2,1,0:T(8,128)(2,1)S(1)}, u32[]{:S(2)}) copy-start(bf16[4,5,40,128]{3,2,1,0:T(8,128)(2,1)S(1)} %collective-permute-done.2.refs_1_) | copy-start | bytes 614404
  23.5 16.9 %collective-permute-start.7 = (bf16[4,5,40,128]{3,2,1,0:T(8,128)(2,1)}, bf16[4,5,40,128]{3,2,1,0:T(8,128)(2,1)S(1)}, u32[]{:S(2)}, u32[]{:S(2)}) collective-permute-start(bf16[4,5,40,128]{3,2,1,0:T(8,128)(2,1)} %get-tuple-element.37), channel_id=1, source_target_pairs={{0,192},{32,224},{64,128},{96,160},{128,64},{160,96},{192,0},{224,... | collective-permute-start | bytes 614408 | tf_op jit(solution)/shard_map/ppermute | solution.py:388
  26.6 17.3 %copy-start.9 = (bf16[4,5,40,128]{3,2,1,0:T(8,128)(2,1)}, bf16[4,5,40,128]{3,2,1,0:T(8,128)(2,1)S(1)}, u32[]{:S(2)}) copy-start(bf16[4,5,40,128]{3,2,1,0:T(8,128)(2,1)S(1)} %collective-permute-done.3.refs_2_) | copy-start | bytes 614404
  26.6 17.2 %collective-permute-start.8 = (bf16[4,5,40,128]{3,2,1,0:T(8,128)(2,1)}, bf16[4,5,40,128]{3,2,1,0:T(8,128)(2,1)S(1)}, u32[]{:S(2)}, u32[]{:S(2)}) collective-permute-start(bf16[4,5,40,128]{3,2,1,0:T(8,128)(2,1)} %get-tuple-element.38), channel_id=1, source_target_pairs={{0,224},{32,192},{64,160},{96,128},{128,96},{160,64},{192,32},{224... | collective-permute-start | bytes 614408 | tf_op jit(solution)/shard_map/ppermute | solution.py:388
  30.0 13.8 %copy-start.10 = (bf16[4,5,40,128]{3,2,1,0:T(8,128)(2,1)}, bf16[4,5,40,128]{3,2,1,0:T(8,128)(2,1)S(1)}, u32[]{:S(2)}) copy-start(bf16[4,5,40,128]{3,2,1,0:T(8,128)(2,1)S(1)} %collective-permute-done.4.refs_3_) | copy-start | bytes 614404
  30.0 19.3 %collective-permute-start = (bf16[4,5,1024]{2,1,0:T(8,128)(2,1)}, bf16[4,5,1024]{2,1,0:T(8,128)(2,1)S(1)}, u32[]{:S(2)}, u32[]{:S(2)}) collective-permute-start(bf16[4,5,1024]{2,1,0:T(8,128)(2,1)} %get-tuple-element.27), channel_id=1, source_target_pairs={{0,1},{1,2},{2,3},{3,4},{4,5},{5,6},{6,7},{7,8},{8,9},{9,10},{10,1... | collective-permute-start | bytes 122888 | tf_op jit(solution)/shard_map/ppermute | solution.py:386
  35.4 8.4 %copy-start.11 = (bf16[4,5,40,128]{3,2,1,0:T(8,128)(2,1)}, bf16[4,5,40,128]{3,2,1,0:T(8,128)(2,1)S(1)}, u32[]{:S(2)}) copy-start(bf16[4,5,40,128]{3,2,1,0:T(8,128)(2,1)S(1)} %collective-permute-done.5.refs_4_) | copy-start | bytes 614404
  35.5 17.5 %collective-permute-start.1 = (bf16[4,5,1024]{2,1,0:T(8,128)(2,1)}, bf16[4,5,1024]{2,1,0:T(8,128)(2,1)S(1)}, u32[]{:S(2)}, u32[]{:S(2)}) collective-permute-start(bf16[4,5,1024]{2,1,0:T(8,128)(2,1)} %get-tuple-element.28), channel_id=1, source_target_pairs={{1,0},{2,1},{3,2},{4,3},{5,4},{6,5},{7,6},{8,7},{9,8},{10,9},{11,1... | collective-permute-start | bytes 122888 | tf_op jit(solution)/shard_map/ppermute | solution.py:387
  38.9 5.0 %copy-start.12 = (bf16[4,5,40,128]{3,2,1,0:T(8,128)(2,1)}, bf16[4,5,40,128]{3,2,1,0:T(8,128)(2,1)S(1)}, u32[]{:S(2)}) copy-start(bf16[4,5,40,128]{3,2,1,0:T(8,128)(2,1)S(1)} %collective-permute-done.6.refs_5_) | copy-start | bytes 614404
  40.4 3.5 %copy-start.13 = (bf16[4,5,40,128]{3,2,1,0:T(8,128)(2,1)}, bf16[4,5,40,128]{3,2,1,0:T(8,128)(2,1)S(1)}, u32[]{:S(2)}) copy-start(bf16[4,5,40,128]{3,2,1,0:T(8,128)(2,1)S(1)} %collective-permute-done.7.refs_6_) | copy-start | bytes 614404
  43.8 0.7 copy-start.14
  49.4 12.9 %copy-start.15 = (bf16[4,5,1024]{2,1,0:T(8,128)(2,1)}, bf16[4,5,1024]{2,1,0:T(8,128)(2,1)S(1)}, u32[]{:S(2)}) copy-start(bf16[4,5,1024]{2,1,0:T(8,128)(2,1)S(1)} %collective-permute-done.low_ref) | copy-start | bytes 122884
  52.9 9.4 %copy-start.16 = (bf16[4,5,1024]{2,1,0:T(8,128)(2,1)}, bf16[4,5,1024]{2,1,0:T(8,128)(2,1)S(1)}, u32[]{:S(2)}) copy-start(bf16[4,5,1024]{2,1,0:T(8,128)(2,1)S(1)} %collective-permute-done.1.high_ref) | copy-start | bytes 122884
  62.3 4.9 %copy-start.23 = (bf16[4,5,40,128]{3,2,1,0:T(8,128)(2,1)S(1)}, bf16[4,5,40,128]{3,2,1,0:T(8,128)(2,1)}, u32[]{:S(2)}) copy-start(bf16[4,5,40,128]{3,2,1,0:T(8,128)(2,1)} %get-tuple-element.40) | copy-start | bytes 614404
  62.3 5.0 %copy-start.22 = (bf16[4,5,40,128]{3,2,1,0:T(8,128)(2,1)S(1)}, bf16[4,5,40,128]{3,2,1,0:T(8,128)(2,1)}, u32[]{:S(2)}) copy-start(bf16[4,5,40,128]{3,2,1,0:T(8,128)(2,1)} %get-tuple-element.41) | copy-start | bytes 614404
  62.3 6.3 %copy-start.21 = (bf16[4,5,40,128]{3,2,1,0:T(8,128)(2,1)S(1)}, bf16[4,5,40,128]{3,2,1,0:T(8,128)(2,1)}, u32[]{:S(2)}) copy-start(bf16[4,5,40,128]{3,2,1,0:T(8,128)(2,1)} %get-tuple-element.42) | copy-start | bytes 614404
  62.3 6.9 %copy-start.20 = (bf16[4,5,40,128]{3,2,1,0:T(8,128)(2,1)S(1)}, bf16[4,5,40,128]{3,2,1,0:T(8,128)(2,1)}, u32[]{:S(2)}) copy-start(bf16[4,5,40,128]{3,2,1,0:T(8,128)(2,1)} %get-tuple-element.43) | copy-start | bytes 614404
  62.3 7.4 %copy-start.19 = (bf16[4,5,40,128]{3,2,1,0:T(8,128)(2,1)S(1)}, bf16[4,5,40,128]{3,2,1,0:T(8,128)(2,1)}, u32[]{:S(2)}) copy-start(bf16[4,5,40,128]{3,2,1,0:T(8,128)(2,1)} %get-tuple-element.44) | copy-start | bytes 614404
  62.4 10.1 %copy-start.18 = (bf16[4,5,40,128]{3,2,1,0:T(8,128)(2,1)S(1)}, bf16[4,5,40,128]{3,2,1,0:T(8,128)(2,1)}, u32[]{:S(2)}) copy-start(bf16[4,5,40,128]{3,2,1,0:T(8,128)(2,1)} %get-tuple-element.45) | copy-start | bytes 614404
  62.4 13.0 %copy-start.17 = (bf16[4,5,40,128]{3,2,1,0:T(8,128)(2,1)S(1)}, bf16[4,5,40,128]{3,2,1,0:T(8,128)(2,1)}, u32[]{:S(2)}) copy-start(bf16[4,5,40,128]{3,2,1,0:T(8,128)(2,1)} %get-tuple-element.46) | copy-start | bytes 614404
  62.4 45.5 %all-to-all-start.1 = ((bf16[32,40,640]{2,1,0:T(8,128)(2,1)}), bf16[32,40,640]{2,1,0:T(8,128)(2,1)}, u32[]{:S(2)}, u32[]{:S(2)}) async-start(bf16[32,40,640]{2,1,0:T(8,128)(2,1)} %bitcast.6), calls=%async_computation.1 | async-start | bytes 3276800 | tf_op jit(solution)/shard_map/all_to_all | solution.py:394
  67.2 5.2 %collective-permute-start.9 = (bf16[4,5,40,128]{3,2,1,0:T(8,128)(2,1)S(1)}, bf16[4,5,40,128]{3,2,1,0:T(8,128)(2,1)S(1)}, u32[]{:S(2)}, u32[]{:S(2)}) collective-permute-start(bf16[4,5,40,128]{3,2,1,0:T(8,128)(2,1)S(1)} %copy-done.23), channel_id=1, source_target_pairs={{0,32},{32,0},{64,96},{96,64},{128,160},{160,128},{192,224},{224,1... | collective-permute-start | bytes 614408 | tf_op jit(solution)/shard_map/ppermute | solution.py:391
  67.3 8.0 %collective-permute-start.10 = (bf16[4,5,40,128]{3,2,1,0:T(8,128)(2,1)S(1)}, bf16[4,5,40,128]{3,2,1,0:T(8,128)(2,1)S(1)}, u32[]{:S(2)}, u32[]{:S(2)}) collective-permute-start(bf16[4,5,40,128]{3,2,1,0:T(8,128)(2,1)S(1)} %copy-done.22), channel_id=1, source_target_pairs={{0,64},{32,96},{64,0},{96,32},{128,192},{160,224},{192,128},{224,1... | collective-permute-start | bytes 614408 | tf_op jit(solution)/shard_map/ppermute | solution.py:391
  68.6 10.1 %collective-permute-start.11 = (bf16[4,5,40,128]{3,2,1,0:T(8,128)(2,1)S(1)}, bf16[4,5,40,128]{3,2,1,0:T(8,128)(2,1)S(1)}, u32[]{:S(2)}, u32[]{:S(2)}) collective-permute-start(bf16[4,5,40,128]{3,2,1,0:T(8,128)(2,1)S(1)} %copy-done.21), channel_id=1, source_target_pairs={{0,96},{32,64},{64,32},{96,0},{128,224},{160,192},{192,160},{224,1... | collective-permute-start | bytes 614408 | tf_op jit(solution)/shard_map/ppermute | solution.py:391
  69.2 14.9 %collective-permute-start.12 = (bf16[4,5,40,128]{3,2,1,0:T(8,128)(2,1)S(1)}, bf16[4,5,40,128]{3,2,1,0:T(8,128)(2,1)S(1)}, u32[]{:S(2)}, u32[]{:S(2)}) collective-permute-start(bf16[4,5,40,128]{3,2,1,0:T(8,128)(2,1)S(1)} %copy-done.20), channel_id=1, source_target_pairs={{0,128},{32,160},{64,192},{96,224},{128,0},{160,32},{192,64},{224,... | collective-permute-start | bytes 614408 | tf_op jit(solution)/shard_map/ppermute | solution.py:391
  69.7 17.9 %collective-permute-start.13 = (bf16[4,5,40,128]{3,2,1,0:T(8,128)(2,1)S(1)}, bf16[4,5,40,128]{3,2,1,0:T(8,128)(2,1)S(1)}, u32[]{:S(2)}, u32[]{:S(2)}) collective-permute-start(bf16[4,5,40,128]{3,2,1,0:T(8,128)(2,1)S(1)} %copy-done.19), channel_id=1, source_target_pairs={{0,160},{32,128},{64,224},{96,192},{128,32},{160,0},{192,96},{224,... | collective-permute-start | bytes 614408 | tf_op jit(solution)/shard_map/ppermute | solution.py:391
  72.4 20.2 %copy-start.1 = (bf16[4,5,40,128]{3,2,1,0:T(8,128)(2,1)}, bf16[4,5,40,128]{3,2,1,0:T(8,128)(2,1)S(1)}, u32[]{:S(2)}) copy-start(bf16[4,5,40,128]{3,2,1,0:T(8,128)(2,1)S(1)} %collective-permute-done.9.refs_1_) | copy-start | bytes 614404
  72.4 16.7 %collective-permute-start.14 = (bf16[4,5,40,128]{3,2,1,0:T(8,128)(2,1)S(1)}, bf16[4,5,40,128]{3,2,1,0:T(8,128)(2,1)S(1)}, u32[]{:S(2)}, u32[]{:S(2)}) collective-permute-start(bf16[4,5,40,128]{3,2,1,0:T(8,128)(2,1)S(1)} %copy-done.18), channel_id=1, source_target_pairs={{0,192},{32,224},{64,128},{96,160},{128,64},{160,96},{192,0},{224,... | collective-permute-start | bytes 614408 | tf_op jit(solution)/shard_map/ppermute | solution.py:391
  75.3 17.3 %copy-start.2 = (bf16[4,5,40,128]{3,2,1,0:T(8,128)(2,1)}, bf16[4,5,40,128]{3,2,1,0:T(8,128)(2,1)S(1)}, u32[]{:S(2)}) copy-start(bf16[4,5,40,128]{3,2,1,0:T(8,128)(2,1)S(1)} %collective-permute-done.10.refs_2_) | copy-start | bytes 614404
  75.3 17.3 %collective-permute-start.15 = (bf16[4,5,40,128]{3,2,1,0:T(8,128)(2,1)S(1)}, bf16[4,5,40,128]{3,2,1,0:T(8,128)(2,1)S(1)}, u32[]{:S(2)}, u32[]{:S(2)}) collective-permute-start(bf16[4,5,40,128]{3,2,1,0:T(8,128)(2,1)S(1)} %copy-done.17), channel_id=1, source_target_pairs={{0,224},{32,192},{64,160},{96,128},{128,96},{160,64},{192,32},{224... | collective-permute-start | bytes 614408 | tf_op jit(solution)/shard_map/ppermute | solution.py:391
  78.8 13.9 %copy-start.3 = (bf16[4,5,40,128]{3,2,1,0:T(8,128)(2,1)}, bf16[4,5,40,128]{3,2,1,0:T(8,128)(2,1)S(1)}, u32[]{:S(2)}) copy-start(bf16[4,5,40,128]{3,2,1,0:T(8,128)(2,1)S(1)} %collective-permute-done.11.refs_3_) | copy-start | bytes 614404
  84.2 8.5 %copy-start.4 = (bf16[4,5,40,128]{3,2,1,0:T(8,128)(2,1)}, bf16[4,5,40,128]{3,2,1,0:T(8,128)(2,1)S(1)}, u32[]{:S(2)}) copy-start(bf16[4,5,40,128]{3,2,1,0:T(8,128)(2,1)S(1)} %collective-permute-done.12.refs_4_) | copy-start | bytes 614404
  87.6 5.1 %copy-start.5 = (bf16[4,5,40,128]{3,2,1,0:T(8,128)(2,1)}, bf16[4,5,40,128]{3,2,1,0:T(8,128)(2,1)S(1)}, u32[]{:S(2)}) copy-start(bf16[4,5,40,128]{3,2,1,0:T(8,128)(2,1)S(1)} %collective-permute-done.13.refs_5_) | copy-start | bytes 614404
  89.2 3.5 %copy-start.6 = (bf16[4,5,40,128]{3,2,1,0:T(8,128)(2,1)}, bf16[4,5,40,128]{3,2,1,0:T(8,128)(2,1)S(1)}, u32[]{:S(2)}) copy-start(bf16[4,5,40,128]{3,2,1,0:T(8,128)(2,1)S(1)} %collective-permute-done.14.refs_6_) | copy-start | bytes 614404
  92.7 0.7 copy-start.7

commit v3 on v2

--- a/solution.py
+++ b/solution.py
@@ -6,7 +6,8 @@
 from jax.sharding import PartitionSpec as P
 
 LANES = 128
-VMEM_LIMIT = 40 * 1024 * 1024
+VMEM_LIMIT = 28 * 1024 * 1024
+VMEM_SMALL = 12 * 1024 * 1024
 
 
 def primitives(cons, metric):
@@ -38,7 +39,6 @@
 def flux_j_kernel(state_hbm, metric_hbm, out_hbm, state_ref, metric_ref, out_ref, in_sems, out_sems):
     nt = state_ref.shape[0]
     blocks = out_ref.shape[1]
-    half = blocks // 2
     metric_copy = pltpu.make_async_copy(metric_hbm, metric_ref, in_sems.at[nt])
     metric_copy.start()
     copies = [
@@ -47,9 +47,10 @@
     for copy in copies:
         copy.start()
     metric_copy.wait()
-    sent = []
-    for t in range(nt):
-        copies[t].wait()
+
+    @pl.loop(0, nt)
+    def _(t):
+        pltpu.make_async_copy(state_hbm.at[t], state_ref.at[t], in_sems.at[t]).wait()
         for b in range(blocks):
             cols = slice(b * LANES, (b + 1) * LANES)
             cons = [state_ref[t, v, :, cols].astype(jnp.float32) for v in range(5)]
@@ -57,15 +58,11 @@
             _, contra, pressure = primitives(cons, metric)
             for v, f in enumerate(flux_of(cons, metric, contra, pressure)):
                 out_ref[t, b, :, v * LANES : (v + 1) * LANES] = f.astype(jnp.bfloat16)
-            if (b + 1) % half == 0:
-                part = pl.ds(b + 1 - half, half)
-                copy = pltpu.make_async_copy(
-                    out_ref.at[t, part], out_hbm.at[t, part], out_sems.at[len(sent)]
-                )
-                copy.start()
-                sent.append(copy)
-    for copy in sent:
-        copy.wait()
+        pltpu.make_async_copy(out_ref.at[t], out_hbm.at[t], out_sems.at[t]).start()
+
+    @pl.loop(0, nt)
+    def _(t):
+        pltpu.make_async_copy(out_ref.at[t], out_hbm.at[t], out_sems.at[t]).wait()
 
 
 def in_hbm(x):
@@ -87,7 +84,7 @@
             pltpu.VMEM(metric_j.shape, jnp.float32),
             pltpu.VMEM(shape, jnp.bfloat16),
             pltpu.SemaphoreType.DMA((nt + 1,)),
-            pltpu.SemaphoreType.DMA((2 * nt,)),
+            pltpu.SemaphoreType.DMA((nt,)),
         ],
         compiler_params=pltpu.CompilerParams(vmem_limit_bytes=VMEM_LIMIT),
         cost_estimate=pl.CostEstimate(flops=10_000_000, bytes_accessed=4_000_000, transcendentals=200_000),
@@ -150,7 +147,7 @@
     fetches = [pltpu.make_async_copy(ins[k], taken.at[k], in_sems.at[k]) for k in range(peers)]
     for copy in fetches:
         copy.start()
-    fetch = pltpu.make_async_copy(deriv_hbm, held, sem)
+    fetch = pltpu.make_async_copy(deriv_hbm.at[pl.ds(0, held.shape[0])], held, sem)
     fetch.start()
     nt, nv, nj = taken.shape[1:4]
     tiles = nj // 8
@@ -194,7 +191,7 @@
     *sources, held = pl.pallas_call(
         source_kernel,
         out_shape=[pltpu.HBM(shape, jnp.bfloat16)] * peers
-        + [pltpu.VMEM(deriv_j.shape, deriv_j.dtype)],
+        + [pltpu.VMEM((deriv_j.shape[0] // 2, deriv_j.shape[1]), deriv_j.dtype)],
         in_specs=[pl.BlockSpec(memory_space=pltpu.SMEM), vmem, hbm] + [hbm] * peers,
         out_specs=[hbm] * peers + [vmem],
         scratch_shapes=[pltpu.VMEM((peers,) + shape, jnp.bfloat16)] * 2
@@ -209,9 +206,8 @@
 
 
 def local_kernel(
-    me_ref, state_ref, metric_i_ref, metric_j_ref, low_ref, high_ref, deriv_ref, *refs
+    state_ref, metric_i_ref, metric_j_ref, low_ref, high_ref, deriv_ref, out_ref, flux_ref
 ):
-    sources, out_ref, flux_ref = refs[:-2], refs[-2], refs[-1]
     nv, nj, ni = state_ref.shape[1:]
     metric_i = [metric_i_ref[c] for c in range(3)]
     cons = [state_ref[0, v].astype(jnp.float32) for v in range(nv)]
@@ -241,32 +237,18 @@
         twice = 2.0 * c
         damping = radius_i * (right + left - twice) + radius_j * (up + down - twice)
         out_ref[0, v] = term[v * nj : (v + 1) * nj] - damping
-    for k, source_ref in enumerate(sources):
-        cols = pl.ds(pl.multiple_of((me_ref[0] ^ k) * LANES, LANES), LANES)
-        for v in range(nv):
-            out_ref[0, v, :, cols] += source_ref[0, v].astype(jnp.float32)
-
-
-def local_terms(me, state, metric_i, metric_j, low, high, deriv_i, sources):
+
+
+def local_terms(state, metric_i, metric_j, low, high, deriv_i):
     nt, nv, nj, ni = state.shape
     whole3 = pl.BlockSpec((3, nj, ni), lambda t: (0, 0, 0))
     halo = pl.BlockSpec((1, nv, ni), lambda t: (t, 0, 0))
     per_t = pl.BlockSpec((1, nv, nj, ni), lambda t: (t, 0, 0, 0))
-    block = pl.BlockSpec((1, nv, nj, LANES), lambda t: (t, 0, 0, 0))
     return pl.pallas_call(
         local_kernel,
         grid=(nt,),
-        out_shape=pltpu.VMEM((nt, nv, nj, ni), jnp.float32),
-        in_specs=[
-            pl.BlockSpec(memory_space=pltpu.SMEM),
-            per_t,
-            whole3,
-            whole3,
-            halo,
-            halo,
-            pl.BlockSpec((ni, ni), lambda t: (0, 0)),
-        ]
-        + [block] * len(sources),
+        out_shape=pltpu.HBM((nt, nv, nj, ni), jnp.float32),
+        in_specs=[per_t, whole3, whole3, halo, halo, pl.BlockSpec((ni, ni), lambda t: (0, 0))],
         out_specs=per_t,
         scratch_shapes=[pltpu.VMEM((nv * nj, ni), jnp.float32)],
         compiler_params=pltpu.CompilerParams(vmem_limit_bytes=VMEM_LIMIT),
@@ -274,81 +256,127 @@
             flops=2 * nt * nv * nj * ni * ni, bytes_accessed=11_000_000, transcendentals=600_000
         ),
         name="local_terms",
-    )(me, *[in_hbm(x) for x in (state, metric_i, metric_j, low, high, deriv_i, *sources)])
-
-
-ROWS = 256
-
-
-def slope_kernel(deriv_ref, lines_hbm, out_hbm, lines_ref, out_ref, in_sems, out_sems):
-    chunks = out_ref.shape[0] // ROWS
-    pieces = [pl.ds(c * ROWS, ROWS) for c in range(chunks)]
-    fetches = [
-        pltpu.make_async_copy(lines_hbm.at[p], lines_ref.at[p], in_sems.at[c])
-        for c, p in enumerate(pieces)
-    ]
-    for copy in fetches:
-        copy.start()
-    copies = []
-    for c, rows in enumerate(pieces):
-        if c == 0:
-            total = None
-            for d, p in enumerate(pieces):
-                fetches[d].wait()
-                part = jnp.dot(
-                    deriv_ref[rows, d * ROWS : (d + 1) * ROWS],
-                    lines_ref[p, :],
-                    preferred_element_type=jnp.float32,
-                )
-                total = part if total is None else total + part
-        else:
-            total = jnp.dot(deriv_ref[rows, :], lines_ref[...], preferred_element_type=jnp.float32)
-        out_ref[rows, :] = total.astype(jnp.bfloat16)
-        copy = pltpu.make_async_copy(out_ref.at[rows], out_hbm.at[rows], out_sems.at[c])
-        copy.start()
-        copies.append(copy)
-    for copy in copies:
-        copy.wait()
-
-
-def slope_lines(deriv_j, lines):
+    )(*[in_hbm(x) for x in (state, metric_i, metric_j, low, high, deriv_i)])
+
+
+def add_kernel(me_ref, partial_hbm, *refs):
+    out_ref, partial_ref, taken, part_sems, in_sems = refs[-5:]
+    sources = refs[:-5]
+    nt, nv = out_ref.shape[:2]
+    for t in range(nt):
+        pltpu.make_async_copy(partial_hbm.at[t], partial_ref.at[t], part_sems.at[t]).start()
+    for k, source in enumerate(sources):
+        pltpu.make_async_copy(source, taken.at[k], in_sems.at[k]).start()
+    for k, source in enumerate(sources):
+        pltpu.make_async_copy(source, taken.at[k], in_sems.at[k]).wait()
+
+    @pl.loop(0, nt)
+    def _(t):
+        pltpu.make_async_copy(partial_hbm.at[t], partial_ref.at[t], part_sems.at[t]).wait()
+        for k in range(len(sources)):
+            cols = pl.ds(pl.multiple_of((me_ref[0] ^ k) * LANES, LANES), LANES)
+            for v in range(nv):
+                out_ref[t, v, :, cols] = partial_ref[t, v, :, cols] + taken[k, t, v].astype(jnp.float32)
+
+
+def add_sources(me, partial, sources):
+    peers = len(sources)
+    hbm = pl.BlockSpec(memory_space=pltpu.HBM)
+    return pl.pallas_call(
+        add_kernel,
+        out_shape=pltpu.VMEM(partial.shape, jnp.float32),
+        in_specs=[pl.BlockSpec(memory_space=pltpu.SMEM)] + [hbm] * (peers + 1),
+        out_specs=pl.BlockSpec(memory_space=pltpu.VMEM),
+        scratch_shapes=[
+            pltpu.VMEM(partial.shape, jnp.float32),
+            pltpu.VMEM((peers,) + sources[0].shape, jnp.bfloat16),
+            pltpu.SemaphoreType.DMA((partial.shape[0],)),
+            pltpu.SemaphoreType.DMA((peers,)),
+        ],
+        compiler_params=pltpu.CompilerParams(vmem_limit_bytes=VMEM_SMALL),
+        cost_estimate=pl.CostEstimate(flops=1_000_000, bytes_accessed=8_000_000, transcendentals=0),
+        name="add_sources",
+    )(me, partial, *[in_hbm(x) for x in sources])
+
+
+def slope_kernel(held_ref, lines_ref, deriv_hbm, out_hbm, rest_ref, out_ref, in_sem, sems):
+    half = held_ref.shape[0]
+    rest = pltpu.make_async_copy(deriv_hbm.at[pl.ds(half, half)], rest_ref, in_sem)
+    rest.start()
+    sizes = (256, 256, half - 512)
+
+    def multiply(deriv_ref, base, first_sem):
+        row = 0
+        for c, size in enumerate(sizes):
+            rows = pl.ds(base + row, size)
+            out_ref[rows, :] = jnp.dot(
+                deriv_ref[row : row + size, :], lines_ref[...], preferred_element_type=jnp.float32
+            ).astype(jnp.bfloat16)
+            sent = pltpu.make_async_copy(out_ref.at[rows], out_hbm.at[rows], sems.at[first_sem + c])
+            sent.start()
+            row += size
+
+    @pl.loop(0, 3)
+    def _(step):
+        @pl.when(step == 0)
+        def _():
+            multiply(held_ref, 0, 0)
+
+        @pl.when(step == 1)
+        def _():
+            rest.wait()
+            multiply(rest_ref, half, len(sizes))
+
+        @pl.when(step == 2)
+        def _():
+            row = 0
+            for c, size in enumerate(sizes * 2):
+                rows = pl.ds(row, size)
+                pltpu.make_async_copy(out_ref.at[rows], out_hbm.at[rows], sems.at[c]).wait()
+                row += size
+
+
+def slope_lines(held, lines, deriv_j):
     size, width = lines.shape
+    vmem = pl.BlockSpec(memory_space=pltpu.VMEM)
     hbm = pl.BlockSpec(memory_space=pltpu.HBM)
     return pl.pallas_call(
         slope_kernel,
         out_shape=pltpu.HBM((size, width), jnp.bfloat16),
-        in_specs=[pl.BlockSpec(memory_space=pltpu.VMEM), hbm],
+        in_specs=[vmem, vmem, hbm],
         out_specs=hbm,
-        scratch_shapes=[pltpu.VMEM((size, width), jnp.bfloat16)] * 2
-        + [pltpu.SemaphoreType.DMA((size // ROWS,))] * 2,
-        compiler_params=pltpu.CompilerParams(vmem_limit_bytes=VMEM_LIMIT),
+        scratch_shapes=[
+            pltpu.VMEM(held.shape, jnp.bfloat16),
+            pltpu.VMEM((size, width), jnp.bfloat16),
+            pltpu.SemaphoreType.DMA,
+            pltpu.SemaphoreType.DMA((6,)),
+        ],
+        compiler_params=pltpu.CompilerParams(vmem_limit_bytes=VMEM_SMALL),
         cost_estimate=pl.CostEstimate(
             flops=2 * size * size * width, bytes_accessed=7_000_000, transcendentals=0
         ),
         name="slope_lines",
-    )(deriv_j, in_hbm(lines))
+    )(held, lines, in_hbm(deriv_j))
 
 
 def finish_kernel(total_ref, slope_hbm, out_hbm, slope_ref, out_ref, in_sems, out_sems):
     nt, nv = total_ref.shape[:2]
-    copies = [
-        pltpu.make_async_copy(slope_hbm.at[t], slope_ref.at[t], in_sems.at[t]) for t in range(nt)
-    ]
-    for copy in copies:
-        copy.start()
-    sent = []
     for t in range(nt):
-        copies[t].wait()
+        pltpu.make_async_copy(slope_hbm.at[t], slope_ref.at[t], in_sems.at[t]).start()
+
+    @pl.loop(0, nt)
+    def _(t):
+        pltpu.make_async_copy(slope_hbm.at[t], slope_ref.at[t], in_sems.at[t]).wait()
         for b in range(slope_ref.shape[1]):
             cols = slice(b * LANES, (b + 1) * LANES)
             for v in range(nv):
                 s = slope_ref[t, b, :, v * LANES : (v + 1) * LANES].astype(jnp.float32)
                 out_ref[t, v, :, cols] = (total_ref[t, v, :, cols] + s).astype(jnp.bfloat16)
-        copy = pltpu.make_async_copy(out_ref.at[t], out_hbm.at[t], out_sems.at[t])
-        copy.start()
-        sent.append(copy)
-    for copy in sent:
-        copy.wait()
+        pltpu.make_async_copy(out_ref.at[t], out_hbm.at[t], out_sems.at[t]).start()
+
+    @pl.loop(0, nt)
+    def _(t):
+        pltpu.make_async_copy(out_ref.at[t], out_hbm.at[t], out_sems.at[t]).wait()
 
 
 def finish(total, slope):
@@ -387,14 +415,15 @@
     high = lax.ppermute(first, "space", backward)
     blocks = own[:1] + [lax.ppermute(own[k], "tm", swaps[k]) for k in range(1, peers)]
     sources, held = source_blocks(me, spectral, deriv_j, blocks)
-    lines, low, high = lax.optimization_barrier((lines, low, high))
     sources = sources[:1] + [lax.ppermute(sources[k], "tm", swaps[k]) for k in range(1, peers)]
-    partial = local_terms(me, state, metric_i, metric_j, low, high, deriv_i, sources)
-    slope = slope_lines(held, lines.reshape(count * nj, nv * LANES))
+    slope = slope_lines(held, lines.reshape(count * nj, nv * LANES), deriv_j)
+    slope, low, high = lax.optimization_barrier((slope, low, high))
     slope = lax.all_to_all(
         slope.reshape(count, nj, nv * LANES), "space", split_axis=0, concat_axis=0, tiled=True
     )
-    return finish(partial, slope.reshape(nt, ni // LANES, nj, nv * LANES))
+    partial = local_terms(state, metric_i, metric_j, low, high, deriv_i)
+    total = add_sources(me, partial, sources)
+    return finish(total, slope.reshape(nt, ni // LANES, nj, nv * LANES))
 
 
 def solution(mesh):

time: 111 us -> 109 us (0.982)
  waiting for transfers between devices: 49.2 us -> 43.4 us
  local copies, waits for them, and re-layouts: 1.37 us -> 3.87 us
    ppermute x7, waiting for transfers between devices: 19.6 us -> 11 us  [on_device(): lax.ppermute(sources[k], 'tm', swaps[k])]
    all_to_all x1, waiting for transfers between devices: 4.06 us -> 8.94 us  [on_device(): lax.all_to_all(outgoing, 'space', split_axis=0, concat_axis=0, tiled=True)]
    ppermute x1, waiting for transfers between devices: 3.54 us -> 0.01 us  [on_device(): high = lax.ppermute(first, 'space', backward)]
    all_to_all x1, waiting for transfers between devices: 5.79 us -> 8.63 us  [on_device(): lax.all_to_all(slope.reshape(count, nj, nv * LANES), 'space', split_axis=...]
    pallas_call x1 -> x2, Pallas kernels: 8.7 us -> 11.3 us  [the longest x1 8.54 us: local_terms(): pl.pallas_call(local_kernel, grid=(nt,), out_shape=pltpu.HBM((nt, nv, nj,...]
    unnamed x48 -> x50, local copies, waits for them, and re-layouts: 1.37 us -> 3.87 us
    pallas_call x1, Pallas kernels: 5.31 us -> 3.69 us  [slope_lines(): pl.pallas_call(slope_kernel, out_shape=pltpu.HBM((size, width), jnp.bfloa...]
    ppermute x1, waiting for transfers between devices: 1.35 us -> 0.01 us  [on_device(): low = lax.ppermute(last, 'space', forward)]
  transfers between devices with their start and end apart: 18 -> 18, of which waited for: 16 -> 13; matrix products, arithmetic and copies ran while one was open for 0% -> 0% of each run, Pallas kernels for 15% -> 21%
where the time goes in v3:
time: 109 us; the launch traced here: 108 us
  waiting for transfers between devices  43.4 us (40%)
  starting transfers between devices  32.9 us (30%)
  Pallas kernels  27.6 us (25%)
  local copies, waits for them, and re-layouts  3.87 us (4%)
    ppermute x7, waiting for transfers between devices, on_device(): lax.ppermute(own[k], 'tm', swaps[k])  14.8 us
    all_to_all x1, starting transfers between devices, on_device(): lax.all_to_all(outgoing, 'space', split_axis=0, concat_axis=0, tiled=True)  11.5 us
    ppermute x7, waiting for transfers between devices, on_device(): lax.ppermute(sources[k], 'tm', swaps[k])  11 us
    all_to_all x1, waiting for transfers between devices, on_device(): lax.all_to_all(outgoing, 'space', split_axis=0, concat_axis=0, tiled=True)  8.94 us
    all_to_all x1, waiting for transfers between devices, on_device(): lax.all_to_all(slope.reshape(count, nj, nv * LANES), 'space', split_axis=...  8.63 us
    pallas_call x1, Pallas kernels, local_terms(): pl.pallas_call(local_kernel, grid=(nt,), out_shape=pltpu.HBM((nt, nv, nj,...  8.54 us
    ppermute x7, starting transfers between devices, on_device(): lax.ppermute(sources[k], 'tm', swaps[k])  5.98 us
    ppermute x7, starting transfers between devices, on_device(): lax.ppermute(own[k], 'tm', swaps[k])  5.71 us
  transfers between devices with their start and end apart: 18, of which 13 were waited for; matrix products, arithmetic and copies ran while one was open for 0% of the time, Pallas kernels for 21%

profile of v3, /device:TPU:4, one launch (start us, length us, event | category | flops | bytes accessed | tf_op | source)
XLA Modules:
  0.0 108.1 jit_solution(12938678088811878555)
XLA Ops:
  0.0 2.9 %flux_j.1 = bf16[4,8,40,640]{3,2,1,0:T(8,128)(2,1)} custom-call(bf16[4,5,40,1024]{3,2,1,0:T(8,128)(2,1)} %state_ref.3, f32[3,40,1024]{2,1,0:T(8,128)} %metric_j_ref.1), custom_call_target="tpu_custom_call" | custom-call | flops 10000000 | bytes 4000000 | tf_op jit(solution)/shard_map/flux_j/pallas_call | solution.py:77
  2.9 11.5 %all-to-all-start = ((bf16[32,40,640]{2,1,0:T(8,128)(2,1)}), bf16[32,40,640]{2,1,0:T(8,128)(2,1)S(1)}, u32[]{:S(2)}, u32[]{:S(2)}) async-start(bf16[32,40,640]{2,1,0:T(8,128)(2,1)} %bitcast.6), calls=%async_computation | async-start | bytes 3276800 | tf_op jit(solution)/shard_map/all_to_all | solution.py:412
  14.4 0.0 copy-start.1
  14.4 3.9 %pack_blocks.1 = (bf16[4,5,1024]{2,1,0:T(8,128)(2,1)}, bf16[4,5,1024]{2,1,0:T(8,128)(2,1)}, bf16[4,5,40,128]{3,2,1,0:T(8,128)(2,1)}, bf16[4,5,40,128]{3,2,1,0:T(...) custom-call(s32[1]{0:T(128)} %bitcast.me_ref, ...), custom_call_target="tpu_custom_call" | custom-call | bytes 3300000 | tf_op jit(solution)/shard_map/pack_blocks/pallas_call | solution.py:111
  18.3 0.1 collective-permute-start
  18.3 1.3 %collective-permute-start.1 = (bf16[4,5,40,128]{3,2,1,0:T(8,128)(2,1)}, bf16[4,5,40,128]{3,2,1,0:T(8,128)(2,1)S(1)}, u32[]{:S(2)}, u32[]{:S(2)}) collective-permute-start(bf16[4,5,40,128]{3,2,1,0:T(8,128)(2,1)} %get-tuple-element.29), channel_id=1, source_target_pairs={{0,64},{32,96},{64,0},{96,32},{128,192},{160,224},{192,128},{224,1... | collective-permute-start | bytes 614408 | tf_op jit(solution)/shard_map/ppermute | solution.py:416
  19.6 0.6 collective-permute-start.2
  20.2 0.5 collective-permute-start.3
  20.7 2.7 %collective-permute-start.4 = (bf16[4,5,40,128]{3,2,1,0:T(8,128)(2,1)}, bf16[4,5,40,128]{3,2,1,0:T(8,128)(2,1)S(1)}, u32[]{:S(2)}, u32[]{:S(2)}) collective-permute-start(bf16[4,5,40,128]{3,2,1,0:T(8,128)(2,1)} %get-tuple-element.32), channel_id=1, source_target_pairs={{0,160},{32,128},{64,224},{96,192},{128,32},{160,0},{192,96},{224,... | collective-permute-start | bytes 614408 | tf_op jit(solution)/shard_map/ppermute | solution.py:416
  23.4 0.0 collective-permute-done.refs_1_
  23.4 0.5 collective-permute-start.5
  24.0 2.5 %collective-permute-done.1.refs_2_ = bf16[4,5,40,128]{3,2,1,0:T(8,128)(2,1)S(1)} collective-permute-done((bf16[4,5,40,128]{3,2,1,0:T(8,128)(2,1)}, bf16[4,5,40,128]{3,2,1,0:T(8,128)(2,1)S(1)}, u32[]{:S(2)}, u32[]{:S(2)}) %collective-permute-start.1) | collective-permute-done | bytes 204832 | tf_op jit(solution)/shard_map/ppermute | solution.py:416
  26.5 0.0 collective-permute-start.6
  26.5 3.4 %collective-permute-done.2.refs_3_ = bf16[4,5,40,128]{3,2,1,0:T(8,128)(2,1)S(1)} collective-permute-done((bf16[4,5,40,128]{3,2,1,0:T(8,128)(2,1)}, bf16[4,5,40,128]{3,2,1,0:T(8,128)(2,1)S(1)}, u32[]{:S(2)}, u32[]{:S(2)}) %collective-permute-start.2) | collective-permute-done | bytes 204832 | tf_op jit(solution)/shard_map/ppermute | solution.py:416
  30.0 3.7 %collective-permute-start.7 = (bf16[4,5,1024]{2,1,0:T(8,128)(2,1)}, bf16[4,5,1024]{2,1,0:T(8,128)(2,1)S(1)}, u32[]{:S(2)}, u32[]{:S(2)}) collective-permute-start(bf16[4,5,1024]{2,1,0:T(8,128)(2,1)} %get-tuple-element.36), channel_id=1, source_target_pairs={{0,1},{1,2},{2,3},{3,4},{4,5},{5,6},{6,7},{7,8},{8,9},{9,10},{10,1... | collective-permute-start | bytes 122888 | tf_op jit(solution)/shard_map/ppermute | solution.py:414
  33.7 1.7 %collective-permute-done.3.refs_4_ = bf16[4,5,40,128]{3,2,1,0:T(8,128)(2,1)S(1)} collective-permute-done((bf16[4,5,40,128]{3,2,1,0:T(8,128)(2,1)}, bf16[4,5,40,128]{3,2,1,0:T(8,128)(2,1)S(1)}, u32[]{:S(2)}, u32[]{:S(2)}) %collective-permute-start.3) | collective-permute-done | bytes 204832 | tf_op jit(solution)/shard_map/ppermute | solution.py:416
  35.4 1.3 %collective-permute-start.8 = (bf16[4,5,1024]{2,1,0:T(8,128)(2,1)}, bf16[4,5,1024]{2,1,0:T(8,128)(2,1)S(1)}, u32[]{:S(2)}, u32[]{:S(2)}) collective-permute-start(bf16[4,5,1024]{2,1,0:T(8,128)(2,1)} %get-tuple-element.37), channel_id=1, source_target_pairs={{1,0},{2,1},{3,2},{4,3},{5,4},{6,5},{7,6},{8,7},{9,8},{10,9},{11,1... | collective-permute-start | bytes 122888 | tf_op jit(solution)/shard_map/ppermute | solution.py:415
  36.7 2.1 %collective-permute-done.4.refs_5_ = bf16[4,5,40,128]{3,2,1,0:T(8,128)(2,1)S(1)} collective-permute-done((bf16[4,5,40,128]{3,2,1,0:T(8,128)(2,1)}, bf16[4,5,40,128]{3,2,1,0:T(8,128)(2,1)S(1)}, u32[]{:S(2)}, u32[]{:S(2)}) %collective-permute-start.4) | collective-permute-done | bytes 204832 | tf_op jit(solution)/shard_map/ppermute | solution.py:416
  38.8 1.5 %collective-permute-done.5.refs_6_ = bf16[4,5,40,128]{3,2,1,0:T(8,128)(2,1)S(1)} collective-permute-done((bf16[4,5,40,128]{3,2,1,0:T(8,128)(2,1)}, bf16[4,5,40,128]{3,2,1,0:T(8,128)(2,1)S(1)}, u32[]{:S(2)}, u32[]{:S(2)}) %collective-permute-start.5) | collective-permute-done | bytes 204832 | tf_op jit(solution)/shard_map/ppermute | solution.py:416
  40.3 3.5 %collective-permute-done.6.refs_7_ = bf16[4,5,40,128]{3,2,1,0:T(8,128)(2,1)S(1)} collective-permute-done((bf16[4,5,40,128]{3,2,1,0:T(8,128)(2,1)}, bf16[4,5,40,128]{3,2,1,0:T(8,128)(2,1)S(1)}, u32[]{:S(2)}, u32[]{:S(2)}) %collective-permute-start.6) | collective-permute-done | bytes 204832 | tf_op jit(solution)/shard_map/ppermute | solution.py:416
  43.8 0.6 copy-done.13
  44.5 3.5 %source_blocks.1 = (bf16[4,5,40,128]{3,2,1,0:T(8,128)(2,1)}, bf16[4,5,40,128]{3,2,1,0:T(8,128)(2,1)}, bf16[4,5,40,128]{3,2,1,0:T(8,128)(2,1)}, bf16[4,5,40,128]{...) custom-call(s32[1]{0:T(128)} %bitcast.me_ref, ...), custom_call_target="tpu_custom_call" | custom-call | flops 420000000 | bytes 10000000 | tf_op jit(solution)/shard_map/source_blocks/pallas_call | solution.py:191
  47.9 8.9 %all-to-all-done = bf16[32,40,640]{2,1,0:T(8,128)(2,1)S(1)} async-done(((bf16[32,40,640]{2,1,0:T(8,128)(2,1)}), bf16[32,40,640]{2,1,0:T(8,128)(2,1)S(1)}, u32[]{:S(2)}, u32[]{:S(2)}) %all-to-all-start) | async-done | bytes 1638432 | tf_op jit(solution)/shard_map/all_to_all | solution.py:412
  56.9 3.7 %slope_lines.1 = bf16[1280,640]{1,0:T(8,128)(2,1)} custom-call(bf16[640,1280]{1,0:T(8,128)(2,1)S(1)} %get-tuple-element.35.held_ref, bf16[1280,640]{1,0:T(8,128)(2,1)S(1)} %bitcast.5, bf16[1280,1280]{1,0:T(8,128)(2,1)} %deriv_hbm.3), custom_call_target="tpu_custom_call" | custom-call | flops 2097152000 | bytes 7000000 | tf_op jit(solution)/shard_map/slope_lines/pallas_call | solution.py:343
  60.6 0.0 collective-permute-done.7.low_ref
  60.6 0.0 collective-permute-done.8.high_ref
  60.7 0.5 copy-done.16
  61.2 0.0 copy-done.17
  61.3 4.7 %all-to-all-start.1 = ((bf16[32,40,640]{2,1,0:T(8,128)(2,1)}), bf16[32,40,640]{2,1,0:T(8,128)(2,1)}, u32[]{:S(2)}, u32[]{:S(2)}) async-start(bf16[32,40,640]{2,1,0:T(8,128)(2,1)} %bitcast.7), calls=%async_computation.1 | async-start | bytes 3276800 | tf_op jit(solution)/shard_map/all_to_all | solution.py:421
  66.0 0.1 collective-permute-start.9
  66.1 1.3 %collective-permute-start.10 = (bf16[4,5,40,128]{3,2,1,0:T(8,128)(2,1)S(1)}, bf16[4,5,40,128]{3,2,1,0:T(8,128)(2,1)S(1)}, u32[]{:S(2)}, u32[]{:S(2)}) collective-permute-start(bf16[4,5,40,128]{3,2,1,0:T(8,128)(2,1)S(1)} %copy-done.23), channel_id=1, source_target_pairs={{0,64},{32,96},{64,0},{96,32},{128,192},{160,224},{192,128},{224,1... | collective-permute-start | bytes 614408 | tf_op jit(solution)/shard_map/ppermute | solution.py:418
  67.4 0.6 collective-permute-start.11
  68.0 0.5 collective-permute-start.12
  68.5 2.7 %collective-permute-start.13 = (bf16[4,5,40,128]{3,2,1,0:T(8,128)(2,1)S(1)}, bf16[4,5,40,128]{3,2,1,0:T(8,128)(2,1)S(1)}, u32[]{:S(2)}, u32[]{:S(2)}) collective-permute-start(bf16[4,5,40,128]{3,2,1,0:T(8,128)(2,1)S(1)} %copy-done.20), channel_id=1, source_target_pairs={{0,160},{32,128},{64,224},{96,192},{128,32},{160,0},{192,96},{224,... | collective-permute-start | bytes 614408 | tf_op jit(solution)/shard_map/ppermute | solution.py:418
  71.2 0.0 collective-permute-done.9.refs_1_
  71.2 0.8 collective-permute-start.14
  72.0 2.1 %collective-permute-done.10.refs_2_ = bf16[4,5,40,128]{3,2,1,0:T(8,128)(2,1)S(1)} collective-permute-done((bf16[4,5,40,128]{3,2,1,0:T(8,128)(2,1)S(1)}, bf16[4,5,40,128]{3,2,1,0:T(8,128)(2,1)S(1)}, u32[]{:S(2)}, u32[]{:S(2)}) %collective-permute-start.10) | collective-permute-done | bytes 204832 | tf_op jit(solution)/shard_map/ppermute | solution.py:418
  74.1 8.5 %local_terms.1.partial_hbm = f32[4,5,40,1024]{3,2,1,0:T(8,128)} custom-call(bf16[4,5,40,1024]{3,2,1,0:T(8,128)(2,1)} %state_ref.3, f32[3,40,1024]{2,1,0:T(8,128)} %metric_i_ref.1, f32[3,40,1024]{2,1,0:T(8,128)} %metric_j_ref.1, bf16[4,5,1024]{2,1,0:T(8,128)(2,1)} %copy-done.16, bf16[4,5,1024]{2,1,0:T(8,128)(2,1)} %copy-done.17, bf16[1024,1024]{1,0:T(8,128)(2,1)} %deriv_ref.1), custom_call_target="tpu_custom_call" | custom-call | flops 1677721600 | bytes 11000000 | tf_op jit(solution)/shard_map/local_terms/pallas_call | solution.py:247
  82.6 0.0 collective-permute-done.11.refs_3_
  82.6 0.3 collective-permute-done.12.refs_4_
  82.9 3.4 %collective-permute-done.13.refs_5_ = bf16[4,5,40,128]{3,2,1,0:T(8,128)(2,1)S(1)} collective-permute-done((bf16[4,5,40,128]{3,2,1,0:T(8,128)(2,1)S(1)}, bf16[4,5,40,128]{3,2,1,0:T(8,128)(2,1)S(1)}, u32[]{:S(2)}, u32[]{:S(2)}) %collective-permute-start.13) | collective-permute-done | bytes 204832 | tf_op jit(solution)/shard_map/ppermute | solution.py:418
  86.4 1.8 %collective-permute-done.14.refs_6_ = bf16[4,5,40,128]{3,2,1,0:T(8,128)(2,1)S(1)} collective-permute-done((bf16[4,5,40,128]{3,2,1,0:T(8,128)(2,1)S(1)}, bf16[4,5,40,128]{3,2,1,0:T(8,128)(2,1)S(1)}, u32[]{:S(2)}, u32[]{:S(2)}) %collective-permute-start.14) | collective-permute-done | bytes 204832 | tf_op jit(solution)/shard_map/ppermute | solution.py:418
  88.1 3.5 %collective-permute-done.15.refs_7_ = bf16[4,5,40,128]{3,2,1,0:T(8,128)(2,1)S(1)} collective-permute-done((bf16[4,5,40,128]{3,2,1,0:T(8,128)(2,1)S(1)}, bf16[4,5,40,128]{3,2,1,0:T(8,128)(2,1)S(1)}, u32[]{:S(2)}, u32[]{:S(2)}) %collective-permute-start.15) | collective-permute-done | bytes 204832 | tf_op jit(solution)/shard_map/ppermute | solution.py:418
  91.6 0.7 copy-done.15
  92.3 1.9 %copy-done = f32[4,5,40,1024]{3,2,1,0:T(8,128)S(1)} copy-done((f32[4,5,40,1024]{3,2,1,0:T(8,128)S(1)}, f32[4,5,40,1024]{3,2,1,0:T(8,128)}, u32[]{:S(2)}) %copy-start) | copy-done | bytes 3276824
  94.2 2.8 %add_sources.1.total_ref = f32[4,5,40,1024]{3,2,1,0:T(8,128)S(1)} custom-call(s32[1]{0:T(128)} %bitcast.me_ref, f32[4,5,40,1024]{3,2,1,0:T(8,128)S(1)} %copy-done, bf16[4,5,40,128]{3,2,1,0:T(8,128)(2,1)} %get-tuple-element.40.refs_0_, bf16[4,5,40,128]{3,2,1,0:T(8,128)(2,1)} %copy-done.7, bf16[4,5,40,128]{3,2,1,0:T(8,128)(2,1)} %copy-done.8, ...), custom_call_target="tpu_custom_call" | custom-call | flops 1000000 | bytes 8000000 | tf_op jit(solution)/shard_map/add_sources/pallas_call | solution.py:285
  97.0 8.6 %all-to-all-done.1 = bf16[32,40,640]{2,1,0:T(8,128)(2,1)} async-done(((bf16[32,40,640]{2,1,0:T(8,128)(2,1)}), bf16[32,40,640]{2,1,0:T(8,128)(2,1)}, u32[]{:S(2)}, u32[]{:S(2)}) %all-to-all-start.1) | async-done | bytes 1638432 | tf_op jit(solution)/shard_map/all_to_all | solution.py:421
  105.6 2.3 %finish.1 = bf16[4,5,40,1024]{3,2,1,0:T(8,128)(2,1)} custom-call(f32[4,5,40,1024]{3,2,1,0:T(8,128)S(1)} %add_sources.1.total_ref, bf16[4,8,40,640]{3,2,1,0:T(8,128)(2,1)} %bitcast.4.slope_hbm), custom_call_target="tpu_custom_call" | custom-call | flops 1000000 | bytes 7000000 | tf_op jit(solution)/shard_map/finish/pallas_call | solution.py:385
  (45 shorter events, 0.1 us)
Async XLA Ops:
  2.9 54.0 %all-to-all-start = ((bf16[32,40,640]{2,1,0:T(8,128)(2,1)}), bf16[32,40,640]{2,1,0:T(8,128)(2,1)S(1)}, u32[]{:S(2)}, u32[]{:S(2)}) async-start(bf16[32,40,640]{2,1,0:T(8,128)(2,1)} %bitcast.6), calls=%async_computation | async-start | bytes 3276800 | tf_op jit(solution)/shard_map/all_to_all | solution.py:412
  14.4 30.1 %copy-start.1 = (bf16[32,32]{1,0:T(8,128)(2,1)S(1)}, bf16[32,32]{1,0:T(8,128)(2,1)}, u32[]{:S(2)}) copy-start(bf16[32,32]{1,0:T(8,128)(2,1)} %spectral_ref.1) | copy-start | bytes 6148
  18.3 5.2 %collective-permute-start = (bf16[4,5,40,128]{3,2,1,0:T(8,128)(2,1)}, bf16[4,5,40,128]{3,2,1,0:T(8,128)(2,1)S(1)}, u32[]{:S(2)}, u32[]{:S(2)}) collective-permute-start(bf16[4,5,40,128]{3,2,1,0:T(8,128)(2,1)} %get-tuple-element.28), channel_id=1, source_target_pairs={{0,32},{32,0},{64,96},{96,64},{128,160},{160,128},{192,224},{224,1... | collective-permute-start | bytes 614408 | tf_op jit(solution)/shard_map/ppermute | solution.py:416
  18.3 8.2 %collective-permute-start.1 = (bf16[4,5,40,128]{3,2,1,0:T(8,128)(2,1)}, bf16[4,5,40,128]{3,2,1,0:T(8,128)(2,1)S(1)}, u32[]{:S(2)}, u32[]{:S(2)}) collective-permute-start(bf16[4,5,40,128]{3,2,1,0:T(8,128)(2,1)} %get-tuple-element.29), channel_id=1, source_target_pairs={{0,64},{32,96},{64,0},{96,32},{128,192},{160,224},{192,128},{224,1... | collective-permute-start | bytes 614408 | tf_op jit(solution)/shard_map/ppermute | solution.py:416
  19.6 10.3 %collective-permute-start.2 = (bf16[4,5,40,128]{3,2,1,0:T(8,128)(2,1)}, bf16[4,5,40,128]{3,2,1,0:T(8,128)(2,1)S(1)}, u32[]{:S(2)}, u32[]{:S(2)}) collective-permute-start(bf16[4,5,40,128]{3,2,1,0:T(8,128)(2,1)} %get-tuple-element.30), channel_id=1, source_target_pairs={{0,96},{32,64},{64,32},{96,0},{128,224},{160,192},{192,160},{224,1... | collective-permute-start | bytes 614408 | tf_op jit(solution)/shard_map/ppermute | solution.py:416
  20.2 15.2 %collective-permute-start.3 = (bf16[4,5,40,128]{3,2,1,0:T(8,128)(2,1)}, bf16[4,5,40,128]{3,2,1,0:T(8,128)(2,1)S(1)}, u32[]{:S(2)}, u32[]{:S(2)}) collective-permute-start(bf16[4,5,40,128]{3,2,1,0:T(8,128)(2,1)} %get-tuple-element.31), channel_id=1, source_target_pairs={{0,128},{32,160},{64,192},{96,224},{128,0},{160,32},{192,64},{224,... | collective-permute-start | bytes 614408 | tf_op jit(solution)/shard_map/ppermute | solution.py:416
  20.7 18.1 %collective-permute-start.4 = (bf16[4,5,40,128]{3,2,1,0:T(8,128)(2,1)}, bf16[4,5,40,128]{3,2,1,0:T(8,128)(2,1)S(1)}, u32[]{:S(2)}, u32[]{:S(2)}) collective-permute-start(bf16[4,5,40,128]{3,2,1,0:T(8,128)(2,1)} %get-tuple-element.32), channel_id=1, source_target_pairs={{0,160},{32,128},{64,224},{96,192},{128,32},{160,0},{192,96},{224,... | collective-permute-start | bytes 614408 | tf_op jit(solution)/shard_map/ppermute | solution.py:416
  23.4 20.3 %copy-start.2 = (bf16[4,5,40,128]{3,2,1,0:T(8,128)(2,1)}, bf16[4,5,40,128]{3,2,1,0:T(8,128)(2,1)S(1)}, u32[]{:S(2)}) copy-start(bf16[4,5,40,128]{3,2,1,0:T(8,128)(2,1)S(1)} %collective-permute-done.refs_1_) | copy-start | bytes 614404
  23.4 16.9 %collective-permute-start.5 = (bf16[4,5,40,128]{3,2,1,0:T(8,128)(2,1)}, bf16[4,5,40,128]{3,2,1,0:T(8,128)(2,1)S(1)}, u32[]{:S(2)}, u32[]{:S(2)}) collective-permute-start(bf16[4,5,40,128]{3,2,1,0:T(8,128)(2,1)} %get-tuple-element.33), channel_id=1, source_target_pairs={{0,192},{32,224},{64,128},{96,160},{128,64},{160,96},{192,0},{224,... | collective-permute-start | bytes 614408 | tf_op jit(solution)/shard_map/ppermute | solution.py:416
  26.5 17.3 %copy-start.3 = (bf16[4,5,40,128]{3,2,1,0:T(8,128)(2,1)}, bf16[4,5,40,128]{3,2,1,0:T(8,128)(2,1)S(1)}, u32[]{:S(2)}) copy-start(bf16[4,5,40,128]{3,2,1,0:T(8,128)(2,1)S(1)} %collective-permute-done.1.refs_2_) | copy-start | bytes 614404
  26.5 17.2 %collective-permute-start.6 = (bf16[4,5,40,128]{3,2,1,0:T(8,128)(2,1)}, bf16[4,5,40,128]{3,2,1,0:T(8,128)(2,1)S(1)}, u32[]{:S(2)}, u32[]{:S(2)}) collective-permute-start(bf16[4,5,40,128]{3,2,1,0:T(8,128)(2,1)} %get-tuple-element.34), channel_id=1, source_target_pairs={{0,224},{32,192},{64,160},{96,128},{128,96},{160,64},{192,32},{224... | collective-permute-start | bytes 614408 | tf_op jit(solution)/shard_map/ppermute | solution.py:416
  30.0 13.8 %copy-start.4 = (bf16[4,5,40,128]{3,2,1,0:T(8,128)(2,1)}, bf16[4,5,40,128]{3,2,1,0:T(8,128)(2,1)S(1)}, u32[]{:S(2)}) copy-start(bf16[4,5,40,128]{3,2,1,0:T(8,128)(2,1)S(1)} %collective-permute-done.2.refs_3_) | copy-start | bytes 614404
  30.0 30.6 %collective-permute-start.7 = (bf16[4,5,1024]{2,1,0:T(8,128)(2,1)}, bf16[4,5,1024]{2,1,0:T(8,128)(2,1)S(1)}, u32[]{:S(2)}, u32[]{:S(2)}) collective-permute-start(bf16[4,5,1024]{2,1,0:T(8,128)(2,1)} %get-tuple-element.36), channel_id=1, source_target_pairs={{0,1},{1,2},{2,3},{3,4},{4,5},{5,6},{6,7},{7,8},{8,9},{9,10},{10,1... | collective-permute-start | bytes 122888 | tf_op jit(solution)/shard_map/ppermute | solution.py:414
  35.4 8.4 %copy-start.5 = (bf16[4,5,40,128]{3,2,1,0:T(8,128)(2,1)}, bf16[4,5,40,128]{3,2,1,0:T(8,128)(2,1)S(1)}, u32[]{:S(2)}) copy-start(bf16[4,5,40,128]{3,2,1,0:T(8,128)(2,1)S(1)} %collective-permute-done.3.refs_4_) | copy-start | bytes 614404
  35.4 25.2 %collective-permute-start.8 = (bf16[4,5,1024]{2,1,0:T(8,128)(2,1)}, bf16[4,5,1024]{2,1,0:T(8,128)(2,1)S(1)}, u32[]{:S(2)}, u32[]{:S(2)}) collective-permute-start(bf16[4,5,1024]{2,1,0:T(8,128)(2,1)} %get-tuple-element.37), channel_id=1, source_target_pairs={{1,0},{2,1},{3,2},{4,3},{5,4},{6,5},{7,6},{8,7},{9,8},{10,9},{11,1... | collective-permute-start | bytes 122888 | tf_op jit(solution)/shard_map/ppermute | solution.py:415
  38.8 5.0 %copy-start.6 = (bf16[4,5,40,128]{3,2,1,0:T(8,128)(2,1)}, bf16[4,5,40,128]{3,2,1,0:T(8,128)(2,1)S(1)}, u32[]{:S(2)}) copy-start(bf16[4,5,40,128]{3,2,1,0:T(8,128)(2,1)S(1)} %collective-permute-done.4.refs_5_) | copy-start | bytes 614404
  40.3 3.5 %copy-start.9 = (bf16[4,5,40,128]{3,2,1,0:T(8,128)(2,1)}, bf16[4,5,40,128]{3,2,1,0:T(8,128)(2,1)S(1)}, u32[]{:S(2)}) copy-start(bf16[4,5,40,128]{3,2,1,0:T(8,128)(2,1)S(1)} %collective-permute-done.5.refs_6_) | copy-start | bytes 614404
  43.8 0.7 copy-start.13
  60.6 0.6 copy-start.16
  60.6 0.6 copy-start.17
  60.6 5.3 %copy-start.24 = (bf16[4,5,40,128]{3,2,1,0:T(8,128)(2,1)S(1)}, bf16[4,5,40,128]{3,2,1,0:T(8,128)(2,1)}, u32[]{:S(2)}) copy-start(bf16[4,5,40,128]{3,2,1,0:T(8,128)(2,1)} %get-tuple-element.41) | copy-start | bytes 614404
  60.6 5.4 %copy-start.23 = (bf16[4,5,40,128]{3,2,1,0:T(8,128)(2,1)S(1)}, bf16[4,5,40,128]{3,2,1,0:T(8,128)(2,1)}, u32[]{:S(2)}) copy-start(bf16[4,5,40,128]{3,2,1,0:T(8,128)(2,1)} %get-tuple-element.42) | copy-start | bytes 614404
  60.7 6.7 %copy-start.22 = (bf16[4,5,40,128]{3,2,1,0:T(8,128)(2,1)S(1)}, bf16[4,5,40,128]{3,2,1,0:T(8,128)(2,1)}, u32[]{:S(2)}) copy-start(bf16[4,5,40,128]{3,2,1,0:T(8,128)(2,1)} %get-tuple-element.43) | copy-start | bytes 614404
  60.7 7.3 %copy-start.21 = (bf16[4,5,40,128]{3,2,1,0:T(8,128)(2,1)S(1)}, bf16[4,5,40,128]{3,2,1,0:T(8,128)(2,1)}, u32[]{:S(2)}) copy-start(bf16[4,5,40,128]{3,2,1,0:T(8,128)(2,1)} %get-tuple-element.44) | copy-start | bytes 614404
  60.7 7.8 %copy-start.20 = (bf16[4,5,40,128]{3,2,1,0:T(8,128)(2,1)S(1)}, bf16[4,5,40,128]{3,2,1,0:T(8,128)(2,1)}, u32[]{:S(2)}) copy-start(bf16[4,5,40,128]{3,2,1,0:T(8,128)(2,1)} %get-tuple-element.45) | copy-start | bytes 614404
  60.7 10.5 %copy-start.19 = (bf16[4,5,40,128]{3,2,1,0:T(8,128)(2,1)S(1)}, bf16[4,5,40,128]{3,2,1,0:T(8,128)(2,1)}, u32[]{:S(2)}) copy-start(bf16[4,5,40,128]{3,2,1,0:T(8,128)(2,1)} %get-tuple-element.46) | copy-start | bytes 614404
  60.7 13.4 %copy-start.18 = (bf16[4,5,40,128]{3,2,1,0:T(8,128)(2,1)S(1)}, bf16[4,5,40,128]{3,2,1,0:T(8,128)(2,1)}, u32[]{:S(2)}) copy-start(bf16[4,5,40,128]{3,2,1,0:T(8,128)(2,1)} %get-tuple-element.47) | copy-start | bytes 614404
  61.3 44.4 %all-to-all-start.1 = ((bf16[32,40,640]{2,1,0:T(8,128)(2,1)}), bf16[32,40,640]{2,1,0:T(8,128)(2,1)}, u32[]{:S(2)}, u32[]{:S(2)}) async-start(bf16[32,40,640]{2,1,0:T(8,128)(2,1)} %bitcast.7), calls=%async_computation.1 | async-start | bytes 3276800 | tf_op jit(solution)/shard_map/all_to_all | solution.py:421
  66.0 5.2 %collective-permute-start.9 = (bf16[4,5,40,128]{3,2,1,0:T(8,128)(2,1)S(1)}, bf16[4,5,40,128]{3,2,1,0:T(8,128)(2,1)S(1)}, u32[]{:S(2)}, u32[]{:S(2)}) collective-permute-start(bf16[4,5,40,128]{3,2,1,0:T(8,128)(2,1)S(1)} %copy-done.24), channel_id=1, source_target_pairs={{0,32},{32,0},{64,96},{96,64},{128,160},{160,128},{192,224},{224,1... | collective-permute-start | bytes 614408 | tf_op jit(solution)/shard_map/ppermute | solution.py:418
  66.1 8.0 %collective-permute-start.10 = (bf16[4,5,40,128]{3,2,1,0:T(8,128)(2,1)S(1)}, bf16[4,5,40,128]{3,2,1,0:T(8,128)(2,1)S(1)}, u32[]{:S(2)}, u32[]{:S(2)}) collective-permute-start(bf16[4,5,40,128]{3,2,1,0:T(8,128)(2,1)S(1)} %copy-done.23), channel_id=1, source_target_pairs={{0,64},{32,96},{64,0},{96,32},{128,192},{160,224},{192,128},{224,1... | collective-permute-start | bytes 614408 | tf_op jit(solution)/shard_map/ppermute | solution.py:418
  67.4 15.2 %collective-permute-start.11 = (bf16[4,5,40,128]{3,2,1,0:T(8,128)(2,1)S(1)}, bf16[4,5,40,128]{3,2,1,0:T(8,128)(2,1)S(1)}, u32[]{:S(2)}, u32[]{:S(2)}) collective-permute-start(bf16[4,5,40,128]{3,2,1,0:T(8,128)(2,1)S(1)} %copy-done.22), channel_id=1, source_target_pairs={{0,96},{32,64},{64,32},{96,0},{128,224},{160,192},{192,160},{224,1... | collective-permute-start | bytes 614408 | tf_op jit(solution)/shard_map/ppermute | solution.py:418
  68.0 14.9 %collective-permute-start.12 = (bf16[4,5,40,128]{3,2,1,0:T(8,128)(2,1)S(1)}, bf16[4,5,40,128]{3,2,1,0:T(8,128)(2,1)S(1)}, u32[]{:S(2)}, u32[]{:S(2)}) collective-permute-start(bf16[4,5,40,128]{3,2,1,0:T(8,128)(2,1)S(1)} %copy-done.21), channel_id=1, source_target_pairs={{0,128},{32,160},{64,192},{96,224},{128,0},{160,32},{192,64},{224,... | collective-permute-start | bytes 614408 | tf_op jit(solution)/shard_map/ppermute | solution.py:418
  68.5 17.9 %collective-permute-start.13 = (bf16[4,5,40,128]{3,2,1,0:T(8,128)(2,1)S(1)}, bf16[4,5,40,128]{3,2,1,0:T(8,128)(2,1)S(1)}, u32[]{:S(2)}, u32[]{:S(2)}) collective-permute-start(bf16[4,5,40,128]{3,2,1,0:T(8,128)(2,1)S(1)} %copy-done.20), channel_id=1, source_target_pairs={{0,160},{32,128},{64,224},{96,192},{128,32},{160,0},{192,96},{224,... | collective-permute-start | bytes 614408 | tf_op jit(solution)/shard_map/ppermute | solution.py:418
  71.2 11.4 %copy-start.7 = (bf16[4,5,40,128]{3,2,1,0:T(8,128)(2,1)}, bf16[4,5,40,128]{3,2,1,0:T(8,128)(2,1)S(1)}, u32[]{:S(2)}) copy-start(bf16[4,5,40,128]{3,2,1,0:T(8,128)(2,1)S(1)} %collective-permute-done.9.refs_1_) | copy-start | bytes 614404
  71.2 16.9 %collective-permute-start.14 = (bf16[4,5,40,128]{3,2,1,0:T(8,128)(2,1)S(1)}, bf16[4,5,40,128]{3,2,1,0:T(8,128)(2,1)S(1)}, u32[]{:S(2)}, u32[]{:S(2)}) collective-permute-start(bf16[4,5,40,128]{3,2,1,0:T(8,128)(2,1)S(1)} %copy-done.19), channel_id=1, source_target_pairs={{0,192},{32,224},{64,128},{96,160},{128,64},{160,96},{192,0},{224,... | collective-permute-start | bytes 614408 | tf_op jit(solution)/shard_map/ppermute | solution.py:418
  74.1 8.6 %copy-start.8 = (bf16[4,5,40,128]{3,2,1,0:T(8,128)(2,1)}, bf16[4,5,40,128]{3,2,1,0:T(8,128)(2,1)S(1)}, u32[]{:S(2)}) copy-start(bf16[4,5,40,128]{3,2,1,0:T(8,128)(2,1)S(1)} %collective-permute-done.10.refs_2_) | copy-start | bytes 614404
  74.1 17.5 %collective-permute-start.15 = (bf16[4,5,40,128]{3,2,1,0:T(8,128)(2,1)S(1)}, bf16[4,5,40,128]{3,2,1,0:T(8,128)(2,1)S(1)}, u32[]{:S(2)}, u32[]{:S(2)}) collective-permute-start(bf16[4,5,40,128]{3,2,1,0:T(8,128)(2,1)S(1)} %copy-done.18), channel_id=1, source_target_pairs={{0,224},{32,192},{64,160},{96,128},{128,96},{160,64},{192,32},{224... | collective-permute-start | bytes 614408 | tf_op jit(solution)/shard_map/ppermute | solution.py:418
  82.6 9.0 %copy-start.10 = (bf16[4,5,40,128]{3,2,1,0:T(8,128)(2,1)}, bf16[4,5,40,128]{3,2,1,0:T(8,128)(2,1)S(1)}, u32[]{:S(2)}) copy-start(bf16[4,5,40,128]{3,2,1,0:T(8,128)(2,1)S(1)} %collective-permute-done.11.refs_3_) | copy-start | bytes 614404
  82.9 8.7 %copy-start.11 = (bf16[4,5,40,128]{3,2,1,0:T(8,128)(2,1)}, bf16[4,5,40,128]{3,2,1,0:T(8,128)(2,1)S(1)}, u32[]{:S(2)}) copy-start(bf16[4,5,40,128]{3,2,1,0:T(8,128)(2,1)S(1)} %collective-permute-done.12.refs_4_) | copy-start | bytes 614404
  86.4 5.2 %copy-start.12 = (bf16[4,5,40,128]{3,2,1,0:T(8,128)(2,1)}, bf16[4,5,40,128]{3,2,1,0:T(8,128)(2,1)S(1)}, u32[]{:S(2)}) copy-start(bf16[4,5,40,128]{3,2,1,0:T(8,128)(2,1)S(1)} %collective-permute-done.13.refs_5_) | copy-start | bytes 614404
  88.1 3.5 %copy-start.14 = (bf16[4,5,40,128]{3,2,1,0:T(8,128)(2,1)}, bf16[4,5,40,128]{3,2,1,0:T(8,128)(2,1)S(1)}, u32[]{:S(2)}) copy-start(bf16[4,5,40,128]{3,2,1,0:T(8,128)(2,1)S(1)} %collective-permute-done.14.refs_6_) | copy-start | bytes 614404
  91.6 0.7 copy-start.15
  92.3 1.9 %copy-start = (f32[4,5,40,1024]{3,2,1,0:T(8,128)S(1)}, f32[4,5,40,1024]{3,2,1,0:T(8,128)}, u32[]{:S(2)}) copy-start(f32[4,5,40,1024]{3,2,1,0:T(8,128)} %local_terms.1.partial_hbm) | copy-start | bytes 9830404

commit v4 on v3

--- a/solution.py
+++ b/solution.py
@@ -256,7 +256,7 @@
             flops=2 * nt * nv * nj * ni * ni, bytes_accessed=11_000_000, transcendentals=600_000
         ),
         name="local_terms",
-    )(*[in_hbm(x) for x in (state, metric_i, metric_j, low, high, deriv_i)])
+    )(in_hbm(state), in_hbm(metric_i), in_hbm(metric_j), low, high, in_hbm(deriv_i))
 
 
 def add_kernel(me_ref, partial_hbm, *refs):
@@ -276,7 +276,8 @@
         for k in range(len(sources)):
             cols = pl.ds(pl.multiple_of((me_ref[0] ^ k) * LANES, LANES), LANES)
             for v in range(nv):
-                out_ref[t, v, :, cols] = partial_ref[t, v, :, cols] + taken[k, t, v].astype(jnp.float32)
+                total = partial_ref[t, v, :, cols] + taken[k, t, v].astype(jnp.float32)
+                out_ref[t, v, :, cols] = total.astype(jnp.bfloat16)
 
 
 def add_sources(me, partial, sources):
@@ -284,7 +285,7 @@
     hbm = pl.BlockSpec(memory_space=pltpu.HBM)
     return pl.pallas_call(
         add_kernel,
-        out_shape=pltpu.VMEM(partial.shape, jnp.float32),
+        out_shape=pltpu.VMEM(partial.shape, jnp.bfloat16),
         in_specs=[pl.BlockSpec(memory_space=pltpu.SMEM)] + [hbm] * (peers + 1),
         out_specs=pl.BlockSpec(memory_space=pltpu.VMEM),
         scratch_shapes=[
@@ -359,44 +360,40 @@
     )(held, lines, in_hbm(deriv_j))
 
 
-def finish_kernel(total_ref, slope_hbm, out_hbm, slope_ref, out_ref, in_sems, out_sems):
+def finish_kernel(total_ref, slope_ref, out_hbm, out_ref, sems):
     nt, nv = total_ref.shape[:2]
-    for t in range(nt):
-        pltpu.make_async_copy(slope_hbm.at[t], slope_ref.at[t], in_sems.at[t]).start()
 
     @pl.loop(0, nt)
     def _(t):
-        pltpu.make_async_copy(slope_hbm.at[t], slope_ref.at[t], in_sems.at[t]).wait()
         for b in range(slope_ref.shape[1]):
             cols = slice(b * LANES, (b + 1) * LANES)
             for v in range(nv):
                 s = slope_ref[t, b, :, v * LANES : (v + 1) * LANES].astype(jnp.float32)
-                out_ref[t, v, :, cols] = (total_ref[t, v, :, cols] + s).astype(jnp.bfloat16)
-        pltpu.make_async_copy(out_ref.at[t], out_hbm.at[t], out_sems.at[t]).start()
+                total = total_ref[t, v, :, cols].astype(jnp.float32)
+                out_ref[t, v, :, cols] = (total + s).astype(jnp.bfloat16)
+        pltpu.make_async_copy(out_ref.at[t], out_hbm.at[t], sems.at[t]).start()
 
     @pl.loop(0, nt)
     def _(t):
-        pltpu.make_async_copy(out_ref.at[t], out_hbm.at[t], out_sems.at[t]).wait()
+        pltpu.make_async_copy(out_ref.at[t], out_hbm.at[t], sems.at[t]).wait()
 
 
 def finish(total, slope):
     nt = total.shape[0]
-    hbm = pl.BlockSpec(memory_space=pltpu.HBM)
+    vmem = pl.BlockSpec(memory_space=pltpu.VMEM)
     return pl.pallas_call(
         finish_kernel,
         out_shape=jax.ShapeDtypeStruct(total.shape, jnp.bfloat16),
-        in_specs=[pl.BlockSpec(memory_space=pltpu.VMEM), hbm],
-        out_specs=hbm,
+        in_specs=[vmem, vmem],
+        out_specs=pl.BlockSpec(memory_space=pltpu.HBM),
         scratch_shapes=[
-            pltpu.VMEM(slope.shape, jnp.bfloat16),
             pltpu.VMEM(total.shape, jnp.bfloat16),
             pltpu.SemaphoreType.DMA((nt,)),
-            pltpu.SemaphoreType.DMA((nt,)),
         ],
-        compiler_params=pltpu.CompilerParams(vmem_limit_bytes=VMEM_LIMIT),
-        cost_estimate=pl.CostEstimate(flops=1_000_000, bytes_accessed=7_000_000, transcendentals=0),
+        compiler_params=pltpu.CompilerParams(vmem_limit_bytes=VMEM_SMALL),
+        cost_estimate=pl.CostEstimate(flops=1_000_000, bytes_accessed=5_000_000, transcendentals=0),
         name="finish",
-    )(total, in_hbm(slope))
+    )(total, slope)
 
 
 def on_device(state, spectral, deriv_i, deriv_j, metric_i, metric_j):

time: 109 us -> 107 us (0.982)
  Pallas kernels: 27.6 us -> 26.4 us
    unnamed x50 -> x46, local copies, waits for them, and re-layouts: 3.87 us -> 3.32 us
where the time goes in v4:
time: 107 us
  waiting for transfers between devices  43.5 us (41%)
  starting transfers between devices  32.8 us (31%)
  Pallas kernels  26.4 us (25%)
  local copies, waits for them, and re-layouts  3.32 us (3%)
    ppermute x7, waiting for transfers between devices, on_device(): lax.ppermute(own[k], 'tm', swaps[k])  14.8 us
    all_to_all x1, starting transfers between devices, on_device(): lax.all_to_all(outgoing, 'space', split_axis=0, concat_axis=0, tiled=True)  11.5 us
    ppermute x7, waiting for transfers between devices, on_device(): lax.ppermute(sources[k], 'tm', swaps[k])  11.1 us
    all_to_all x1, waiting for transfers between devices, on_device(): lax.all_to_all(outgoing, 'space', split_axis=0, concat_axis=0, tiled=True)  8.99 us
    all_to_all x1, waiting for transfers between devices, on_device(): lax.all_to_all(slope.reshape(count, nj, nv * LANES), 'space', split_axis=...  8.68 us
    pallas_call x1, Pallas kernels, local_terms(): pl.pallas_call(local_kernel, grid=(nt,), out_shape=pltpu.HBM((nt, nv, nj,...  8.48 us
    ppermute x7, starting transfers between devices, on_device(): lax.ppermute(sources[k], 'tm', swaps[k])  5.98 us
    ppermute x7, starting transfers between devices, on_device(): lax.ppermute(own[k], 'tm', swaps[k])  5.72 us
  transfers between devices with their start and end apart: 18, of which 13 were waited for; matrix products, arithmetic and copies ran while one was open for 0% of the time, Pallas kernels for 21%

profile of v4, /device:TPU:4, one launch (start us, length us, event | category | flops | bytes accessed | tf_op | source)
XLA Modules:
  0.0 106.5 jit_solution(8967542387959800921)
XLA Ops:
  0.0 2.9 %flux_j.1 = bf16[4,8,40,640]{3,2,1,0:T(8,128)(2,1)} custom-call(bf16[4,5,40,1024]{3,2,1,0:T(8,128)(2,1)} %state_ref.3, f32[3,40,1024]{2,1,0:T(8,128)} %metric_j_ref.1), custom_call_target="tpu_custom_call" | custom-call | flops 10000000 | bytes 4000000 | tf_op jit(solution)/shard_map/flux_j/pallas_call | solution.py:77
  2.9 11.5 %all-to-all-start = ((bf16[32,40,640]{2,1,0:T(8,128)(2,1)}), bf16[32,40,640]{2,1,0:T(8,128)(2,1)S(1)}, u32[]{:S(2)}, u32[]{:S(2)}) async-start(bf16[32,40,640]{2,1,0:T(8,128)(2,1)} %bitcast.7), calls=%async_computation | async-start | bytes 3276800 | tf_op jit(solution)/shard_map/all_to_all | solution.py:409
  14.4 0.0 copy-start.1
  14.4 3.8 %pack_blocks.1 = (bf16[4,5,1024]{2,1,0:T(8,128)(2,1)}, bf16[4,5,1024]{2,1,0:T(8,128)(2,1)}, bf16[4,5,40,128]{3,2,1,0:T(8,128)(2,1)}, bf16[4,5,40,128]{3,2,1,0:T(...) custom-call(s32[1]{0:T(128)} %bitcast.me_ref, ...), custom_call_target="tpu_custom_call" | custom-call | bytes 3300000 | tf_op jit(solution)/shard_map/pack_blocks/pallas_call | solution.py:111
  18.2 0.1 collective-permute-start
  18.3 1.3 %collective-permute-start.1 = (bf16[4,5,40,128]{3,2,1,0:T(8,128)(2,1)}, bf16[4,5,40,128]{3,2,1,0:T(8,128)(2,1)S(1)}, u32[]{:S(2)}, u32[]{:S(2)}) collective-permute-start(bf16[4,5,40,128]{3,2,1,0:T(8,128)(2,1)} %get-tuple-element.29), channel_id=1, source_target_pairs={{0,64},{32,96},{64,0},{96,32},{128,192},{160,224},{192,128},{224,1... | collective-permute-start | bytes 614408 | tf_op jit(solution)/shard_map/ppermute | solution.py:413
  19.6 0.6 collective-permute-start.2
  20.2 0.5 collective-permute-start.3
  20.7 2.7 %collective-permute-start.4 = (bf16[4,5,40,128]{3,2,1,0:T(8,128)(2,1)}, bf16[4,5,40,128]{3,2,1,0:T(8,128)(2,1)S(1)}, u32[]{:S(2)}, u32[]{:S(2)}) collective-permute-start(bf16[4,5,40,128]{3,2,1,0:T(8,128)(2,1)} %get-tuple-element.32), channel_id=1, source_target_pairs={{0,160},{32,128},{64,224},{96,192},{128,32},{160,0},{192,96},{224,... | collective-permute-start | bytes 614408 | tf_op jit(solution)/shard_map/ppermute | solution.py:413
  23.4 0.0 collective-permute-done.refs_1_
  23.4 0.5 collective-permute-start.5
  23.9 2.5 %collective-permute-done.1.refs_2_ = bf16[4,5,40,128]{3,2,1,0:T(8,128)(2,1)S(1)} collective-permute-done((bf16[4,5,40,128]{3,2,1,0:T(8,128)(2,1)}, bf16[4,5,40,128]{3,2,1,0:T(8,128)(2,1)S(1)}, u32[]{:S(2)}, u32[]{:S(2)}) %collective-permute-start.1) | collective-permute-done | bytes 204832 | tf_op jit(solution)/shard_map/ppermute | solution.py:413
  26.5 0.0 collective-permute-start.6
  26.5 3.4 %collective-permute-done.2.refs_3_ = bf16[4,5,40,128]{3,2,1,0:T(8,128)(2,1)S(1)} collective-permute-done((bf16[4,5,40,128]{3,2,1,0:T(8,128)(2,1)}, bf16[4,5,40,128]{3,2,1,0:T(8,128)(2,1)S(1)}, u32[]{:S(2)}, u32[]{:S(2)}) %collective-permute-start.2) | collective-permute-done | bytes 204832 | tf_op jit(solution)/shard_map/ppermute | solution.py:413
  29.9 3.7 %collective-permute-start.7 = (bf16[4,5,1024]{2,1,0:T(8,128)(2,1)}, bf16[4,5,1024]{2,1,0:T(8,128)(2,1)S(1)}, u32[]{:S(2)}, u32[]{:S(2)}) collective-permute-start(bf16[4,5,1024]{2,1,0:T(8,128)(2,1)} %get-tuple-element.36), channel_id=1, source_target_pairs={{0,1},{1,2},{2,3},{3,4},{4,5},{5,6},{6,7},{7,8},{8,9},{9,10},{10,1... | collective-permute-start | bytes 122888 | tf_op jit(solution)/shard_map/ppermute | solution.py:411
  33.6 1.7 %collective-permute-done.3.refs_4_ = bf16[4,5,40,128]{3,2,1,0:T(8,128)(2,1)S(1)} collective-permute-done((bf16[4,5,40,128]{3,2,1,0:T(8,128)(2,1)}, bf16[4,5,40,128]{3,2,1,0:T(8,128)(2,1)S(1)}, u32[]{:S(2)}, u32[]{:S(2)}) %collective-permute-start.3) | collective-permute-done | bytes 204832 | tf_op jit(solution)/shard_map/ppermute | solution.py:413
  35.3 1.3 %collective-permute-start.8 = (bf16[4,5,1024]{2,1,0:T(8,128)(2,1)}, bf16[4,5,1024]{2,1,0:T(8,128)(2,1)S(1)}, u32[]{:S(2)}, u32[]{:S(2)}) collective-permute-start(bf16[4,5,1024]{2,1,0:T(8,128)(2,1)} %get-tuple-element.37), channel_id=1, source_target_pairs={{1,0},{2,1},{3,2},{4,3},{5,4},{6,5},{7,6},{8,7},{9,8},{10,9},{11,1... | collective-permute-start | bytes 122888 | tf_op jit(solution)/shard_map/ppermute | solution.py:412
  36.6 2.1 %collective-permute-done.4.refs_5_ = bf16[4,5,40,128]{3,2,1,0:T(8,128)(2,1)S(1)} collective-permute-done((bf16[4,5,40,128]{3,2,1,0:T(8,128)(2,1)}, bf16[4,5,40,128]{3,2,1,0:T(8,128)(2,1)S(1)}, u32[]{:S(2)}, u32[]{:S(2)}) %collective-permute-start.4) | collective-permute-done | bytes 204832 | tf_op jit(solution)/shard_map/ppermute | solution.py:413
  38.8 1.5 %collective-permute-done.5.refs_6_ = bf16[4,5,40,128]{3,2,1,0:T(8,128)(2,1)S(1)} collective-permute-done((bf16[4,5,40,128]{3,2,1,0:T(8,128)(2,1)}, bf16[4,5,40,128]{3,2,1,0:T(8,128)(2,1)S(1)}, u32[]{:S(2)}, u32[]{:S(2)}) %collective-permute-start.5) | collective-permute-done | bytes 204832 | tf_op jit(solution)/shard_map/ppermute | solution.py:413
  40.3 3.5 %collective-permute-done.6.refs_7_ = bf16[4,5,40,128]{3,2,1,0:T(8,128)(2,1)S(1)} collective-permute-done((bf16[4,5,40,128]{3,2,1,0:T(8,128)(2,1)}, bf16[4,5,40,128]{3,2,1,0:T(8,128)(2,1)S(1)}, u32[]{:S(2)}, u32[]{:S(2)}) %collective-permute-start.6) | collective-permute-done | bytes 204832 | tf_op jit(solution)/shard_map/ppermute | solution.py:413
  43.7 0.0 copy-done.4
  43.8 0.6 copy-done.8
  44.4 3.5 %source_blocks.1 = (bf16[4,5,40,128]{3,2,1,0:T(8,128)(2,1)}, bf16[4,5,40,128]{3,2,1,0:T(8,128)(2,1)}, bf16[4,5,40,128]{3,2,1,0:T(8,128)(2,1)}, bf16[4,5,40,128]{...) custom-call(s32[1]{0:T(128)} %bitcast.me_ref, ...), custom_call_target="tpu_custom_call" | custom-call | flops 420000000 | bytes 10000000 | tf_op jit(solution)/shard_map/source_blocks/pallas_call | solution.py:191
  47.9 9.0 %all-to-all-done = bf16[32,40,640]{2,1,0:T(8,128)(2,1)S(1)} async-done(((bf16[32,40,640]{2,1,0:T(8,128)(2,1)}), bf16[32,40,640]{2,1,0:T(8,128)(2,1)S(1)}, u32[]{:S(2)}, u32[]{:S(2)}) %all-to-all-start) | async-done | bytes 1638432 | tf_op jit(solution)/shard_map/all_to_all | solution.py:409
  56.9 3.7 %slope_lines.1 = bf16[1280,640]{1,0:T(8,128)(2,1)} custom-call(bf16[640,1280]{1,0:T(8,128)(2,1)S(1)} %get-tuple-element.35.held_ref, bf16[1280,640]{1,0:T(8,128)(2,1)S(1)} %bitcast.6, bf16[1280,1280]{1,0:T(8,128)(2,1)} %deriv_hbm.3), custom_call_target="tpu_custom_call" | custom-call | flops 2097152000 | bytes 7000000 | tf_op jit(solution)/shard_map/slope_lines/pallas_call | solution.py:344
  60.6 0.0 collective-permute-done.7.low_ref
  60.6 0.0 collective-permute-done.8.high_ref
  60.7 4.6 %all-to-all-start.1 = ((bf16[32,40,640]{2,1,0:T(8,128)(2,1)}), bf16[32,40,640]{2,1,0:T(8,128)(2,1)S(1)}, u32[]{:S(2)}, u32[]{:S(2)}) async-start(bf16[32,40,640]{2,1,0:T(8,128)(2,1)} %bitcast.8), calls=%async_computation.1 | async-start | bytes 3276800 | tf_op jit(solution)/shard_map/all_to_all | solution.py:418
  65.3 0.1 collective-permute-start.9
  65.5 1.3 %collective-permute-start.10 = (bf16[4,5,40,128]{3,2,1,0:T(8,128)(2,1)S(1)}, bf16[4,5,40,128]{3,2,1,0:T(8,128)(2,1)S(1)}, u32[]{:S(2)}, u32[]{:S(2)}) collective-permute-start(bf16[4,5,40,128]{3,2,1,0:T(8,128)(2,1)S(1)} %copy-done.21), channel_id=1, source_target_pairs={{0,64},{32,96},{64,0},{96,32},{128,192},{160,224},{192,128},{224,1... | collective-permute-start | bytes 614408 | tf_op jit(solution)/shard_map/ppermute | solution.py:415
  66.7 0.6 collective-permute-start.11
  67.3 0.5 collective-permute-start.12
  67.9 2.7 %collective-permute-start.13 = (bf16[4,5,40,128]{3,2,1,0:T(8,128)(2,1)S(1)}, bf16[4,5,40,128]{3,2,1,0:T(8,128)(2,1)S(1)}, u32[]{:S(2)}, u32[]{:S(2)}) collective-permute-start(bf16[4,5,40,128]{3,2,1,0:T(8,128)(2,1)S(1)} %copy-done.18), channel_id=1, source_target_pairs={{0,160},{32,128},{64,224},{96,192},{128,32},{160,0},{192,96},{224,... | collective-permute-start | bytes 614408 | tf_op jit(solution)/shard_map/ppermute | solution.py:415
  70.5 0.0 collective-permute-done.9.refs_1_
  70.6 0.8 collective-permute-start.14
  71.4 2.1 %collective-permute-done.10.refs_2_ = bf16[4,5,40,128]{3,2,1,0:T(8,128)(2,1)S(1)} collective-permute-done((bf16[4,5,40,128]{3,2,1,0:T(8,128)(2,1)S(1)}, bf16[4,5,40,128]{3,2,1,0:T(8,128)(2,1)S(1)}, u32[]{:S(2)}, u32[]{:S(2)}) %collective-permute-start.10) | collective-permute-done | bytes 204832 | tf_op jit(solution)/shard_map/ppermute | solution.py:415
  73.4 0.0 collective-permute-start.15
  73.4 8.5 %local_terms.1.partial_hbm = f32[4,5,40,1024]{3,2,1,0:T(8,128)} custom-call(bf16[4,5,40,1024]{3,2,1,0:T(8,128)(2,1)} %state_ref.3, f32[3,40,1024]{2,1,0:T(8,128)} %metric_i_ref.1, f32[3,40,1024]{2,1,0:T(8,128)} %metric_j_ref.1, bf16[4,5,1024]{2,1,0:T(8,128)(2,1)S(1)} %collective-permute-done.7.low_ref, ...), custom_call_target="tpu_custom_call" | custom-call | flops 1677721600 | bytes 11000000 | tf_op jit(solution)/shard_map/local_terms/pallas_call | solution.py:247
  81.9 0.0 collective-permute-done.11.refs_3_
  81.9 0.3 collective-permute-done.12.refs_4_
  82.3 3.4 %collective-permute-done.13.refs_5_ = bf16[4,5,40,128]{3,2,1,0:T(8,128)(2,1)S(1)} collective-permute-done((bf16[4,5,40,128]{3,2,1,0:T(8,128)(2,1)S(1)}, bf16[4,5,40,128]{3,2,1,0:T(8,128)(2,1)S(1)}, u32[]{:S(2)}, u32[]{:S(2)}) %collective-permute-start.13) | collective-permute-done | bytes 204832 | tf_op jit(solution)/shard_map/ppermute | solution.py:415
  85.7 1.8 %collective-permute-done.14.refs_6_ = bf16[4,5,40,128]{3,2,1,0:T(8,128)(2,1)S(1)} collective-permute-done((bf16[4,5,40,128]{3,2,1,0:T(8,128)(2,1)S(1)}, bf16[4,5,40,128]{3,2,1,0:T(8,128)(2,1)S(1)}, u32[]{:S(2)}, u32[]{:S(2)}) %collective-permute-start.14) | collective-permute-done | bytes 204832 | tf_op jit(solution)/shard_map/ppermute | solution.py:415
  87.5 3.5 %collective-permute-done.15.refs_7_ = bf16[4,5,40,128]{3,2,1,0:T(8,128)(2,1)S(1)} collective-permute-done((bf16[4,5,40,128]{3,2,1,0:T(8,128)(2,1)S(1)}, bf16[4,5,40,128]{3,2,1,0:T(8,128)(2,1)S(1)}, u32[]{:S(2)}, u32[]{:S(2)}) %collective-permute-start.15) | collective-permute-done | bytes 204832 | tf_op jit(solution)/shard_map/ppermute | solution.py:415
  91.0 0.7 copy-done.15
  91.6 1.9 %copy-done = f32[4,5,40,1024]{3,2,1,0:T(8,128)S(1)} copy-done((f32[4,5,40,1024]{3,2,1,0:T(8,128)S(1)}, f32[4,5,40,1024]{3,2,1,0:T(8,128)}, u32[]{:S(2)}) %copy-start) | copy-done | bytes 3276824
  93.6 2.8 %add_sources.1.total_ref = bf16[4,5,40,1024]{3,2,1,0:T(8,128)(2,1)S(1)} custom-call(s32[1]{0:T(128)} %bitcast.me_ref, f32[4,5,40,1024]{3,2,1,0:T(8,128)S(1)} %copy-done, bf16[4,5,40,128]{3,2,1,0:T(8,128)(2,1)} %get-tuple-element.40.refs_0_, bf16[4,5,40,128]{3,2,1,0:T(8,128)(2,1)} %copy-done.9, bf16[4,5,40,128]{3,2,1,0:T(8,128)(2,1)} %copy-done.10, ...), custom_call_target="tpu_custom_call" | custom-call | flops 1000000 | bytes 8000000 | tf_op jit(solution)/shard_map/add_sources/pallas_call | solution.py:286
  96.4 8.7 %all-to-all-done.1 = bf16[32,40,640]{2,1,0:T(8,128)(2,1)S(1)} async-done(((bf16[32,40,640]{2,1,0:T(8,128)(2,1)}), bf16[32,40,640]{2,1,0:T(8,128)(2,1)S(1)}, u32[]{:S(2)}, u32[]{:S(2)}) %all-to-all-start.1) | async-done | bytes 1638432 | tf_op jit(solution)/shard_map/all_to_all | solution.py:418
  105.1 1.3 %finish.1 = bf16[4,5,40,1024]{3,2,1,0:T(8,128)(2,1)} custom-call(bf16[4,5,40,1024]{3,2,1,0:T(8,128)(2,1)S(1)} %add_sources.1.total_ref, bf16[4,8,40,640]{3,2,1,0:T(8,128)(2,1)S(1)} %bitcast.5), custom_call_target="tpu_custom_call" | custom-call | flops 1000000 | bytes 5000000 | tf_op jit(solution)/shard_map/finish/pallas_call | solution.py:384
  (41 shorter events, 0.1 us)
Async XLA Ops:
  2.9 54.0 %all-to-all-start = ((bf16[32,40,640]{2,1,0:T(8,128)(2,1)}), bf16[32,40,640]{2,1,0:T(8,128)(2,1)S(1)}, u32[]{:S(2)}, u32[]{:S(2)}) async-start(bf16[32,40,640]{2,1,0:T(8,128)(2,1)} %bitcast.7), calls=%async_computation | async-start | bytes 3276800 | tf_op jit(solution)/shard_map/all_to_all | solution.py:409
  14.4 30.0 %copy-start.1 = (bf16[32,32]{1,0:T(8,128)(2,1)S(1)}, bf16[32,32]{1,0:T(8,128)(2,1)}, u32[]{:S(2)}) copy-start(bf16[32,32]{1,0:T(8,128)(2,1)} %spectral_ref.1) | copy-start | bytes 6148
  18.2 5.2 %collective-permute-start = (bf16[4,5,40,128]{3,2,1,0:T(8,128)(2,1)}, bf16[4,5,40,128]{3,2,1,0:T(8,128)(2,1)S(1)}, u32[]{:S(2)}, u32[]{:S(2)}) collective-permute-start(bf16[4,5,40,128]{3,2,1,0:T(8,128)(2,1)} %get-tuple-element.28), channel_id=1, source_target_pairs={{0,32},{32,0},{64,96},{96,64},{128,160},{160,128},{192,224},{224,1... | collective-permute-start | bytes 614408 | tf_op jit(solution)/shard_map/ppermute | solution.py:413
  18.3 8.2 %collective-permute-start.1 = (bf16[4,5,40,128]{3,2,1,0:T(8,128)(2,1)}, bf16[4,5,40,128]{3,2,1,0:T(8,128)(2,1)S(1)}, u32[]{:S(2)}, u32[]{:S(2)}) collective-permute-start(bf16[4,5,40,128]{3,2,1,0:T(8,128)(2,1)} %get-tuple-element.29), channel_id=1, source_target_pairs={{0,64},{32,96},{64,0},{96,32},{128,192},{160,224},{192,128},{224,1... | collective-permute-start | bytes 614408 | tf_op jit(solution)/shard_map/ppermute | solution.py:413
  19.6 10.3 %collective-permute-start.2 = (bf16[4,5,40,128]{3,2,1,0:T(8,128)(2,1)}, bf16[4,5,40,128]{3,2,1,0:T(8,128)(2,1)S(1)}, u32[]{:S(2)}, u32[]{:S(2)}) collective-permute-start(bf16[4,5,40,128]{3,2,1,0:T(8,128)(2,1)} %get-tuple-element.30), channel_id=1, source_target_pairs={{0,96},{32,64},{64,32},{96,0},{128,224},{160,192},{192,160},{224,1... | collective-permute-start | bytes 614408 | tf_op jit(solution)/shard_map/ppermute | solution.py:413
  20.2 15.2 %collective-permute-start.3 = (bf16[4,5,40,128]{3,2,1,0:T(8,128)(2,1)}, bf16[4,5,40,128]{3,2,1,0:T(8,128)(2,1)S(1)}, u32[]{:S(2)}, u32[]{:S(2)}) collective-permute-start(bf16[4,5,40,128]{3,2,1,0:T(8,128)(2,1)} %get-tuple-element.31), channel_id=1, source_target_pairs={{0,128},{32,160},{64,192},{96,224},{128,0},{160,32},{192,64},{224,... | collective-permute-start | bytes 614408 | tf_op jit(solution)/shard_map/ppermute | solution.py:413
  20.7 18.1 %collective-permute-start.4 = (bf16[4,5,40,128]{3,2,1,0:T(8,128)(2,1)}, bf16[4,5,40,128]{3,2,1,0:T(8,128)(2,1)S(1)}, u32[]{:S(2)}, u32[]{:S(2)}) collective-permute-start(bf16[4,5,40,128]{3,2,1,0:T(8,128)(2,1)} %get-tuple-element.32), channel_id=1, source_target_pairs={{0,160},{32,128},{64,224},{96,192},{128,32},{160,0},{192,96},{224,... | collective-permute-start | bytes 614408 | tf_op jit(solution)/shard_map/ppermute | solution.py:413
  23.4 20.3 %copy-start.2 = (bf16[4,5,40,128]{3,2,1,0:T(8,128)(2,1)}, bf16[4,5,40,128]{3,2,1,0:T(8,128)(2,1)S(1)}, u32[]{:S(2)}) copy-start(bf16[4,5,40,128]{3,2,1,0:T(8,128)(2,1)S(1)} %collective-permute-done.refs_1_) | copy-start | bytes 614404
  23.4 16.9 %collective-permute-start.5 = (bf16[4,5,40,128]{3,2,1,0:T(8,128)(2,1)}, bf16[4,5,40,128]{3,2,1,0:T(8,128)(2,1)S(1)}, u32[]{:S(2)}, u32[]{:S(2)}) collective-permute-start(bf16[4,5,40,128]{3,2,1,0:T(8,128)(2,1)} %get-tuple-element.33), channel_id=1, source_target_pairs={{0,192},{32,224},{64,128},{96,160},{128,64},{160,96},{192,0},{224,... | collective-permute-start | bytes 614408 | tf_op jit(solution)/shard_map/ppermute | solution.py:413
  26.5 17.3 %copy-start.3 = (bf16[4,5,40,128]{3,2,1,0:T(8,128)(2,1)}, bf16[4,5,40,128]{3,2,1,0:T(8,128)(2,1)S(1)}, u32[]{:S(2)}) copy-start(bf16[4,5,40,128]{3,2,1,0:T(8,128)(2,1)S(1)} %collective-permute-done.1.refs_2_) | copy-start | bytes 614404
  26.5 17.2 %collective-permute-start.6 = (bf16[4,5,40,128]{3,2,1,0:T(8,128)(2,1)}, bf16[4,5,40,128]{3,2,1,0:T(8,128)(2,1)S(1)}, u32[]{:S(2)}, u32[]{:S(2)}) collective-permute-start(bf16[4,5,40,128]{3,2,1,0:T(8,128)(2,1)} %get-tuple-element.34), channel_id=1, source_target_pairs={{0,224},{32,192},{64,160},{96,128},{128,96},{160,64},{192,32},{224... | collective-permute-start | bytes 614408 | tf_op jit(solution)/shard_map/ppermute | solution.py:413
  29.9 13.8 %copy-start.4 = (bf16[4,5,40,128]{3,2,1,0:T(8,128)(2,1)}, bf16[4,5,40,128]{3,2,1,0:T(8,128)(2,1)S(1)}, u32[]{:S(2)}) copy-start(bf16[4,5,40,128]{3,2,1,0:T(8,128)(2,1)S(1)} %collective-permute-done.2.refs_3_) | copy-start | bytes 614404
  29.9 30.7 %collective-permute-start.7 = (bf16[4,5,1024]{2,1,0:T(8,128)(2,1)}, bf16[4,5,1024]{2,1,0:T(8,128)(2,1)S(1)}, u32[]{:S(2)}, u32[]{:S(2)}) collective-permute-start(bf16[4,5,1024]{2,1,0:T(8,128)(2,1)} %get-tuple-element.36), channel_id=1, source_target_pairs={{0,1},{1,2},{2,3},{3,4},{4,5},{5,6},{6,7},{7,8},{8,9},{9,10},{10,1... | collective-permute-start | bytes 122888 | tf_op jit(solution)/shard_map/ppermute | solution.py:411
  35.3 8.4 %copy-start.5 = (bf16[4,5,40,128]{3,2,1,0:T(8,128)(2,1)}, bf16[4,5,40,128]{3,2,1,0:T(8,128)(2,1)S(1)}, u32[]{:S(2)}) copy-start(bf16[4,5,40,128]{3,2,1,0:T(8,128)(2,1)S(1)} %collective-permute-done.3.refs_4_) | copy-start | bytes 614404
  35.3 25.3 %collective-permute-start.8 = (bf16[4,5,1024]{2,1,0:T(8,128)(2,1)}, bf16[4,5,1024]{2,1,0:T(8,128)(2,1)S(1)}, u32[]{:S(2)}, u32[]{:S(2)}) collective-permute-start(bf16[4,5,1024]{2,1,0:T(8,128)(2,1)} %get-tuple-element.37), channel_id=1, source_target_pairs={{1,0},{2,1},{3,2},{4,3},{5,4},{6,5},{7,6},{8,7},{9,8},{10,9},{11,1... | collective-permute-start | bytes 122888 | tf_op jit(solution)/shard_map/ppermute | solution.py:412
  38.8 5.0 %copy-start.6 = (bf16[4,5,40,128]{3,2,1,0:T(8,128)(2,1)}, bf16[4,5,40,128]{3,2,1,0:T(8,128)(2,1)S(1)}, u32[]{:S(2)}) copy-start(bf16[4,5,40,128]{3,2,1,0:T(8,128)(2,1)S(1)} %collective-permute-done.4.refs_5_) | copy-start | bytes 614404
  40.3 3.5 %copy-start.7 = (bf16[4,5,40,128]{3,2,1,0:T(8,128)(2,1)}, bf16[4,5,40,128]{3,2,1,0:T(8,128)(2,1)S(1)}, u32[]{:S(2)}) copy-start(bf16[4,5,40,128]{3,2,1,0:T(8,128)(2,1)S(1)} %collective-permute-done.5.refs_6_) | copy-start | bytes 614404
  43.7 0.7 copy-start.8
  60.6 4.7 %copy-start.22 = (bf16[4,5,40,128]{3,2,1,0:T(8,128)(2,1)S(1)}, bf16[4,5,40,128]{3,2,1,0:T(8,128)(2,1)}, u32[]{:S(2)}) copy-start(bf16[4,5,40,128]{3,2,1,0:T(8,128)(2,1)} %get-tuple-element.41) | copy-start | bytes 614404
  60.6 4.8 %copy-start.21 = (bf16[4,5,40,128]{3,2,1,0:T(8,128)(2,1)S(1)}, bf16[4,5,40,128]{3,2,1,0:T(8,128)(2,1)}, u32[]{:S(2)}) copy-start(bf16[4,5,40,128]{3,2,1,0:T(8,128)(2,1)} %get-tuple-element.42) | copy-start | bytes 614404
  60.6 6.1 %copy-start.20 = (bf16[4,5,40,128]{3,2,1,0:T(8,128)(2,1)S(1)}, bf16[4,5,40,128]{3,2,1,0:T(8,128)(2,1)}, u32[]{:S(2)}) copy-start(bf16[4,5,40,128]{3,2,1,0:T(8,128)(2,1)} %get-tuple-element.43) | copy-start | bytes 614404
  60.6 6.7 %copy-start.19 = (bf16[4,5,40,128]{3,2,1,0:T(8,128)(2,1)S(1)}, bf16[4,5,40,128]{3,2,1,0:T(8,128)(2,1)}, u32[]{:S(2)}) copy-start(bf16[4,5,40,128]{3,2,1,0:T(8,128)(2,1)} %get-tuple-element.44) | copy-start | bytes 614404
  60.7 7.2 %copy-start.18 = (bf16[4,5,40,128]{3,2,1,0:T(8,128)(2,1)S(1)}, bf16[4,5,40,128]{3,2,1,0:T(8,128)(2,1)}, u32[]{:S(2)}) copy-start(bf16[4,5,40,128]{3,2,1,0:T(8,128)(2,1)} %get-tuple-element.45) | copy-start | bytes 614404
  60.7 9.9 %copy-start.17 = (bf16[4,5,40,128]{3,2,1,0:T(8,128)(2,1)S(1)}, bf16[4,5,40,128]{3,2,1,0:T(8,128)(2,1)}, u32[]{:S(2)}) copy-start(bf16[4,5,40,128]{3,2,1,0:T(8,128)(2,1)} %get-tuple-element.46) | copy-start | bytes 614404
  60.7 12.8 %copy-start.16 = (bf16[4,5,40,128]{3,2,1,0:T(8,128)(2,1)S(1)}, bf16[4,5,40,128]{3,2,1,0:T(8,128)(2,1)}, u32[]{:S(2)}) copy-start(bf16[4,5,40,128]{3,2,1,0:T(8,128)(2,1)} %get-tuple-element.47) | copy-start | bytes 614404
  60.7 44.4 %all-to-all-start.1 = ((bf16[32,40,640]{2,1,0:T(8,128)(2,1)}), bf16[32,40,640]{2,1,0:T(8,128)(2,1)S(1)}, u32[]{:S(2)}, u32[]{:S(2)}) async-start(bf16[32,40,640]{2,1,0:T(8,128)(2,1)} %bitcast.8), calls=%async_computation.1 | async-start | bytes 3276800 | tf_op jit(solution)/shard_map/all_to_all | solution.py:418
  65.3 5.2 %collective-permute-start.9 = (bf16[4,5,40,128]{3,2,1,0:T(8,128)(2,1)S(1)}, bf16[4,5,40,128]{3,2,1,0:T(8,128)(2,1)S(1)}, u32[]{:S(2)}, u32[]{:S(2)}) collective-permute-start(bf16[4,5,40,128]{3,2,1,0:T(8,128)(2,1)S(1)} %copy-done.22), channel_id=1, source_target_pairs={{0,32},{32,0},{64,96},{96,64},{128,160},{160,128},{192,224},{224,1... | collective-permute-start | bytes 614408 | tf_op jit(solution)/shard_map/ppermute | solution.py:415
  65.5 8.0 %collective-permute-start.10 = (bf16[4,5,40,128]{3,2,1,0:T(8,128)(2,1)S(1)}, bf16[4,5,40,128]{3,2,1,0:T(8,128)(2,1)S(1)}, u32[]{:S(2)}, u32[]{:S(2)}) collective-permute-start(bf16[4,5,40,128]{3,2,1,0:T(8,128)(2,1)S(1)} %copy-done.21), channel_id=1, source_target_pairs={{0,64},{32,96},{64,0},{96,32},{128,192},{160,224},{192,128},{224,1... | collective-permute-start | bytes 614408 | tf_op jit(solution)/shard_map/ppermute | solution.py:415
  66.7 15.2 %collective-permute-start.11 = (bf16[4,5,40,128]{3,2,1,0:T(8,128)(2,1)S(1)}, bf16[4,5,40,128]{3,2,1,0:T(8,128)(2,1)S(1)}, u32[]{:S(2)}, u32[]{:S(2)}) collective-permute-start(bf16[4,5,40,128]{3,2,1,0:T(8,128)(2,1)S(1)} %copy-done.20), channel_id=1, source_target_pairs={{0,96},{32,64},{64,32},{96,0},{128,224},{160,192},{192,160},{224,1... | collective-permute-start | bytes 614408 | tf_op jit(solution)/shard_map/ppermute | solution.py:415
  67.3 14.9 %collective-permute-start.12 = (bf16[4,5,40,128]{3,2,1,0:T(8,128)(2,1)S(1)}, bf16[4,5,40,128]{3,2,1,0:T(8,128)(2,1)S(1)}, u32[]{:S(2)}, u32[]{:S(2)}) collective-permute-start(bf16[4,5,40,128]{3,2,1,0:T(8,128)(2,1)S(1)} %copy-done.19), channel_id=1, source_target_pairs={{0,128},{32,160},{64,192},{96,224},{128,0},{160,32},{192,64},{224,... | collective-permute-start | bytes 614408 | tf_op jit(solution)/shard_map/ppermute | solution.py:415
  67.9 17.9 %collective-permute-start.13 = (bf16[4,5,40,128]{3,2,1,0:T(8,128)(2,1)S(1)}, bf16[4,5,40,128]{3,2,1,0:T(8,128)(2,1)S(1)}, u32[]{:S(2)}, u32[]{:S(2)}) collective-permute-start(bf16[4,5,40,128]{3,2,1,0:T(8,128)(2,1)S(1)} %copy-done.18), channel_id=1, source_target_pairs={{0,160},{32,128},{64,224},{96,192},{128,32},{160,0},{192,96},{224,... | collective-permute-start | bytes 614408 | tf_op jit(solution)/shard_map/ppermute | solution.py:415
  70.6 11.4 %copy-start.9 = (bf16[4,5,40,128]{3,2,1,0:T(8,128)(2,1)}, bf16[4,5,40,128]{3,2,1,0:T(8,128)(2,1)S(1)}, u32[]{:S(2)}) copy-start(bf16[4,5,40,128]{3,2,1,0:T(8,128)(2,1)S(1)} %collective-permute-done.9.refs_1_) | copy-start | bytes 614404
  70.6 16.9 %collective-permute-start.14 = (bf16[4,5,40,128]{3,2,1,0:T(8,128)(2,1)S(1)}, bf16[4,5,40,128]{3,2,1,0:T(8,128)(2,1)S(1)}, u32[]{:S(2)}, u32[]{:S(2)}) collective-permute-start(bf16[4,5,40,128]{3,2,1,0:T(8,128)(2,1)S(1)} %copy-done.17), channel_id=1, source_target_pairs={{0,192},{32,224},{64,128},{96,160},{128,64},{160,96},{192,0},{224,... | collective-permute-start | bytes 614408 | tf_op jit(solution)/shard_map/ppermute | solution.py:415
  73.4 8.5 %copy-start.10 = (bf16[4,5,40,128]{3,2,1,0:T(8,128)(2,1)}, bf16[4,5,40,128]{3,2,1,0:T(8,128)(2,1)S(1)}, u32[]{:S(2)}) copy-start(bf16[4,5,40,128]{3,2,1,0:T(8,128)(2,1)S(1)} %collective-permute-done.10.refs_2_) | copy-start | bytes 614404
  73.4 17.5 %collective-permute-start.15 = (bf16[4,5,40,128]{3,2,1,0:T(8,128)(2,1)S(1)}, bf16[4,5,40,128]{3,2,1,0:T(8,128)(2,1)S(1)}, u32[]{:S(2)}, u32[]{:S(2)}) collective-permute-start(bf16[4,5,40,128]{3,2,1,0:T(8,128)(2,1)S(1)} %copy-done.16), channel_id=1, source_target_pairs={{0,224},{32,192},{64,160},{96,128},{128,96},{160,64},{192,32},{224... | collective-permute-start | bytes 614408 | tf_op jit(solution)/shard_map/ppermute | solution.py:415
  81.9 9.0 %copy-start.11 = (bf16[4,5,40,128]{3,2,1,0:T(8,128)(2,1)}, bf16[4,5,40,128]{3,2,1,0:T(8,128)(2,1)S(1)}, u32[]{:S(2)}) copy-start(bf16[4,5,40,128]{3,2,1,0:T(8,128)(2,1)S(1)} %collective-permute-done.11.refs_3_) | copy-start | bytes 614404
  82.3 8.7 %copy-start.12 = (bf16[4,5,40,128]{3,2,1,0:T(8,128)(2,1)}, bf16[4,5,40,128]{3,2,1,0:T(8,128)(2,1)S(1)}, u32[]{:S(2)}) copy-start(bf16[4,5,40,128]{3,2,1,0:T(8,128)(2,1)S(1)} %collective-permute-done.12.refs_4_) | copy-start | bytes 614404
  85.7 5.2 %copy-start.13 = (bf16[4,5,40,128]{3,2,1,0:T(8,128)(2,1)}, bf16[4,5,40,128]{3,2,1,0:T(8,128)(2,1)S(1)}, u32[]{:S(2)}) copy-start(bf16[4,5,40,128]{3,2,1,0:T(8,128)(2,1)S(1)} %collective-permute-done.13.refs_5_) | copy-start | bytes 614404
  87.5 3.5 %copy-start.14 = (bf16[4,5,40,128]{3,2,1,0:T(8,128)(2,1)}, bf16[4,5,40,128]{3,2,1,0:T(8,128)(2,1)S(1)}, u32[]{:S(2)}) copy-start(bf16[4,5,40,128]{3,2,1,0:T(8,128)(2,1)S(1)} %collective-permute-done.14.refs_6_) | copy-start | bytes 614404
  90.9 0.7 copy-start.15
  91.6 1.9 %copy-start = (f32[4,5,40,1024]{3,2,1,0:T(8,128)S(1)}, f32[4,5,40,1024]{3,2,1,0:T(8,128)}, u32[]{:S(2)}) copy-start(f32[4,5,40,1024]{3,2,1,0:T(8,128)} %local_terms.1.partial_hbm) | copy-start | bytes 9830404

commit v5 on v4

--- a/solution.py
+++ b/solution.py
@@ -1,3 +1,5 @@
+import functools
+
 import jax
 import jax.numpy as jnp
 from jax import lax
@@ -6,6 +8,7 @@
 from jax.sharding import PartitionSpec as P
 
 LANES = 128
+ORDER = (16, 25, 18, 31, 29, 20, 0, 4, 10, 7, 14, 17, 22, 28, 15, 12, 13, 27, 1, 24, 6, 19, 8, 9, 21, 23, 5, 26, 11, 30, 2, 3)
 VMEM_LIMIT = 28 * 1024 * 1024
 VMEM_SMALL = 12 * 1024 * 1024
 
@@ -92,33 +95,55 @@
     )(in_hbm(state), in_hbm(metric_j))
 
 
-def pack_kernel(me_ref, state_ref, first_ref, last_ref, *outs):
-    nv, nj = state_ref.shape[1:3]
-    for k, out in enumerate(outs):
-        cols = pl.ds(pl.multiple_of((me_ref[0] ^ k) * LANES, LANES), LANES)
-        for v in range(nv):
-            out[0, v] = state_ref[0, v, :, cols]
-    cons = [state_ref[0, v].astype(jnp.float32) for v in range(nv)]
-    first_ref[0] = jnp.concatenate([c[:1] for c in cons], axis=0).astype(jnp.bfloat16)
-    last_ref[0] = jnp.concatenate([c[nj - 1 :] for c in cons], axis=0).astype(jnp.bfloat16)
+def pack_kernel(me_ref, state_hbm, *refs):
+    state_ref, out_ref, edge_ref, in_sems, out_sems, edge_sems = refs[-6:]
+    edges, outs = refs[:2], refs[2:-6]
+    nt, nv, nj = state_ref.shape[:3]
+    for t in range(nt):
+        pltpu.make_async_copy(state_hbm.at[t], state_ref.at[t], in_sems.at[t]).start()
+
+    @pl.loop(0, nt)
+    def _(t):
+        pltpu.make_async_copy(state_hbm.at[t], state_ref.at[t], in_sems.at[t]).wait()
+        for k, out in enumerate(outs):
+            cols = pl.ds(pl.multiple_of((me_ref[0] ^ k) * LANES, LANES), LANES)
+            for v in range(nv):
+                out_ref[k, t, v] = state_ref[t, v, :, cols]
+            pltpu.make_async_copy(out_ref.at[k, t], out.at[t], out_sems.at[k, t]).start()
+        cons = [state_ref[t, v].astype(jnp.float32) for v in range(nv)]
+        for e, row in enumerate((0, nj - 1)):
+            rows = jnp.concatenate([c[row : row + 1] for c in cons], axis=0)
+            edge_ref[e, t] = rows.astype(jnp.bfloat16)
+            pltpu.make_async_copy(edge_ref.at[e, t], edges[e].at[t], edge_sems.at[e, t]).start()
+
+    @pl.loop(0, nt)
+    def _(t):
+        for k, out in enumerate(outs):
+            pltpu.make_async_copy(out_ref.at[k, t], out.at[t], out_sems.at[k, t]).wait()
+        for e, edge in enumerate(edges):
+            pltpu.make_async_copy(edge_ref.at[e, t], edge.at[t], edge_sems.at[e, t]).wait()
 
 
 def pack_blocks(me, state):
     nt, nv, nj, ni = state.shape
     peers = ni // LANES
-    block = pl.BlockSpec((1, nv, nj, LANES), lambda t: (t, 0, 0, 0))
-    edge = pl.BlockSpec((1, nv, ni), lambda t: (t, 0, 0))
+    hbm = pl.BlockSpec(memory_space=pltpu.HBM)
+    block = (nt, nv, nj, LANES)
+    edge = (nt, nv, ni)
     first, last, *blocks = pl.pallas_call(
         pack_kernel,
-        grid=(nt,),
-        out_shape=[pltpu.HBM((nt, nv, ni), state.dtype)] * 2
-        + [pltpu.HBM((nt, nv, nj, LANES), state.dtype)] * peers,
-        in_specs=[
-            pl.BlockSpec(memory_space=pltpu.SMEM),
-            pl.BlockSpec((1, nv, nj, ni), lambda t: (t, 0, 0, 0)),
+        out_shape=[pltpu.HBM(edge, state.dtype)] * 2 + [pltpu.HBM(block, state.dtype)] * peers,
+        in_specs=[pl.BlockSpec(memory_space=pltpu.SMEM), hbm],
+        out_specs=[hbm] * (peers + 2),
+        scratch_shapes=[
+            pltpu.VMEM(state.shape, state.dtype),
+            pltpu.VMEM((peers,) + block, state.dtype),
+            pltpu.VMEM((2,) + edge, state.dtype),
+            pltpu.SemaphoreType.DMA((nt,)),
+            pltpu.SemaphoreType.DMA((peers, nt)),
+            pltpu.SemaphoreType.DMA((2, nt)),
         ],
-        out_specs=[edge] * 2 + [block] * peers,
-        compiler_params=pltpu.CompilerParams(vmem_limit_bytes=VMEM_LIMIT),
+        compiler_params=pltpu.CompilerParams(vmem_limit_bytes=VMEM_SMALL),
         cost_estimate=pl.CostEstimate(flops=0, bytes_accessed=3_300_000, transcendentals=0),
         name="pack_blocks",
     )(me, in_hbm(state))
@@ -297,60 +322,65 @@
         compiler_params=pltpu.CompilerParams(vmem_limit_bytes=VMEM_SMALL),
         cost_estimate=pl.CostEstimate(flops=1_000_000, bytes_accessed=8_000_000, transcendentals=0),
         name="add_sources",
-    )(me, partial, *[in_hbm(x) for x in sources])
-
-
-def slope_kernel(held_ref, lines_ref, deriv_hbm, out_hbm, rest_ref, out_ref, in_sem, sems):
+    )(me, in_hbm(partial), *[in_hbm(x) for x in sources])
+
+
+def slope_kernel(order, held_ref, lines_ref, deriv_hbm, out_hbm, rest_ref, out_ref, in_sem, sems):
     half = held_ref.shape[0]
+    block = out_ref.shape[1]
+    blocks = half // block
     rest = pltpu.make_async_copy(deriv_hbm.at[pl.ds(half, half)], rest_ref, in_sem)
     rest.start()
-    sizes = (256, 256, half - 512)
-
-    def multiply(deriv_ref, base, first_sem):
-        row = 0
-        for c, size in enumerate(sizes):
-            rows = pl.ds(base + row, size)
-            out_ref[rows, :] = jnp.dot(
-                deriv_ref[row : row + size, :], lines_ref[...], preferred_element_type=jnp.float32
-            ).astype(jnp.bfloat16)
-            sent = pltpu.make_async_copy(out_ref.at[rows], out_hbm.at[rows], sems.at[first_sem + c])
-            sent.start()
-            row += size
+
+    def out_copy(source):
+        return pltpu.make_async_copy(
+            out_ref.at[source], out_hbm.at[order.index(source)], sems.at[source]
+        )
+
+    def multiply(deriv_ref, base):
+        first = 0
+        for count in (6, 6, blocks - 12):
+            rows = slice(first * block, (first + count) * block)
+            total = jnp.dot(deriv_ref[rows, :], lines_ref[...], preferred_element_type=jnp.float32)
+            for c in range(count):
+                source = base + first + c
+                out_ref[source] = total[c * block : (c + 1) * block].astype(jnp.bfloat16)
+                out_copy(source).start()
+            first += count
 
     @pl.loop(0, 3)
     def _(step):
         @pl.when(step == 0)
         def _():
-            multiply(held_ref, 0, 0)
+            multiply(held_ref, 0)
 
         @pl.when(step == 1)
         def _():
             rest.wait()
-            multiply(rest_ref, half, len(sizes))
+            multiply(rest_ref, blocks)
 
         @pl.when(step == 2)
         def _():
-            row = 0
-            for c, size in enumerate(sizes * 2):
-                rows = pl.ds(row, size)
-                pltpu.make_async_copy(out_ref.at[rows], out_hbm.at[rows], sems.at[c]).wait()
-                row += size
-
-
-def slope_lines(held, lines, deriv_j):
+            for source in range(2 * blocks):
+                out_copy(source).wait()
+
+
+def slope_lines(held, lines, deriv_j, order):
     size, width = lines.shape
+    count = len(order)
+    shape = (count, size // count, width)
     vmem = pl.BlockSpec(memory_space=pltpu.VMEM)
     hbm = pl.BlockSpec(memory_space=pltpu.HBM)
     return pl.pallas_call(
-        slope_kernel,
-        out_shape=pltpu.HBM((size, width), jnp.bfloat16),
+        functools.partial(slope_kernel, order),
+        out_shape=pltpu.HBM(shape, jnp.bfloat16),
         in_specs=[vmem, vmem, hbm],
         out_specs=hbm,
         scratch_shapes=[
             pltpu.VMEM(held.shape, jnp.bfloat16),
-            pltpu.VMEM((size, width), jnp.bfloat16),
+            pltpu.VMEM(shape, jnp.bfloat16),
             pltpu.SemaphoreType.DMA,
-            pltpu.SemaphoreType.DMA((6,)),
+            pltpu.SemaphoreType.DMA((count,)),
         ],
         compiler_params=pltpu.CompilerParams(vmem_limit_bytes=VMEM_SMALL),
         cost_estimate=pl.CostEstimate(
@@ -360,29 +390,35 @@
     )(held, lines, in_hbm(deriv_j))
 
 
-def finish_kernel(total_ref, slope_ref, out_hbm, out_ref, sems):
+def finish_kernel(order, total_ref, slope_ref, out_hbm, out_ref, sems):
     nt, nv = total_ref.shape[:2]
-
-    @pl.loop(0, nt)
-    def _(t):
-        for b in range(slope_ref.shape[1]):
+    blocks = slope_ref.shape[0] // nt
+
+    def one(t):
+        for b in range(blocks):
+            place = order.index(t * blocks + b)
             cols = slice(b * LANES, (b + 1) * LANES)
             for v in range(nv):
-                s = slope_ref[t, b, :, v * LANES : (v + 1) * LANES].astype(jnp.float32)
+                s = slope_ref[place, :, v * LANES : (v + 1) * LANES].astype(jnp.float32)
                 total = total_ref[t, v, :, cols].astype(jnp.float32)
                 out_ref[t, v, :, cols] = (total + s).astype(jnp.bfloat16)
         pltpu.make_async_copy(out_ref.at[t], out_hbm.at[t], sems.at[t]).start()
 
     @pl.loop(0, nt)
+    def _(step):
+        for t in range(nt):
+            pl.when(step == t)(functools.partial(one, t))
+
+    @pl.loop(0, nt)
     def _(t):
         pltpu.make_async_copy(out_ref.at[t], out_hbm.at[t], sems.at[t]).wait()
 
 
-def finish(total, slope):
+def finish(total, slope, order):
     nt = total.shape[0]
     vmem = pl.BlockSpec(memory_space=pltpu.VMEM)
     return pl.pallas_call(
-        finish_kernel,
+        functools.partial(finish_kernel, order),
         out_shape=jax.ShapeDtypeStruct(total.shape, jnp.bfloat16),
         in_specs=[vmem, vmem],
         out_specs=pl.BlockSpec(memory_space=pltpu.HBM),
@@ -413,14 +449,14 @@
     blocks = own[:1] + [lax.ppermute(own[k], "tm", swaps[k]) for k in range(1, peers)]
     sources, held = source_blocks(me, spectral, deriv_j, blocks)
     sources = sources[:1] + [lax.ppermute(sources[k], "tm", swaps[k]) for k in range(1, peers)]
-    slope = slope_lines(held, lines.reshape(count * nj, nv * LANES), deriv_j)
+    slope = slope_lines(held, lines.reshape(count * nj, nv * LANES), deriv_j, ORDER)
     slope, low, high = lax.optimization_barrier((slope, low, high))
     slope = lax.all_to_all(
-        slope.reshape(count, nj, nv * LANES), "space", split_axis=0, concat_axis=0, tiled=True
+        slope, "space", split_axis=0, concat_axis=0, tiled=True, axis_index_groups=[list(ORDER)]
     )
     partial = local_terms(state, metric_i, metric_j, low, high, deriv_i)
     total = add_sources(me, partial, sources)
-    return finish(total, slope.reshape(nt, ni // LANES, nj, nv * LANES))
+    return finish(total, slope, ORDER)
 
 
 def solution(mesh):

time: 107 us -> 107 us (level); the launches traced: 107 us -> 105 us
  local copies, waits for them, and re-layouts: 3.32 us -> 1.38 us
  starting transfers between devices: 32.8 us -> 33.9 us
    unnamed x46 -> x44, local copies, waits for them, and re-layouts: 3.32 us -> 1.38 us
    all_to_all x1, waiting for transfers between devices: 8.68 us -> 6.76 us  [on_device(): lax.all_to_all(slope, 'space', split_axis=0, concat_axis=0, tiled=True, a...]
    all_to_all x1, waiting for transfers between devices: 8.99 us -> 10.2 us  [on_device(): lax.all_to_all(outgoing, 'space', split_axis=0, concat_axis=0, tiled=True)]
    all_to_all x1, starting transfers between devices: 4.65 us -> 5.77 us  [on_device(): lax.all_to_all(slope, 'space', split_axis=0, concat_axis=0, tiled=True, a...]
where the time goes in v5:
time: 107 us; the launch traced here: 105 us
  waiting for transfers between devices  42.8 us (40%)
  starting transfers between devices  33.9 us (32%)
  Pallas kernels  26.1 us (24%)
  local copies, waits for them, and re-layouts  1.38 us (1%)
    ppermute x7, waiting for transfers between devices, on_device(): lax.ppermute(own[k], 'tm', swaps[k])  14.8 us
    all_to_all x1, starting transfers between devices, on_device(): lax.all_to_all(outgoing, 'space', split_axis=0, concat_axis=0, tiled=True)  11.5 us
    ppermute x7, waiting for transfers between devices, on_device(): lax.ppermute(sources[k], 'tm', swaps[k])  11.1 us
    all_to_all x1, waiting for transfers between devices, on_device(): lax.all_to_all(outgoing, 'space', split_axis=0, concat_axis=0, tiled=True)  10.2 us
    pallas_call x1, Pallas kernels, local_terms(): pl.pallas_call(local_kernel, grid=(nt,), out_shape=pltpu.HBM((nt, nv, nj,...  8.49 us
    all_to_all x1, waiting for transfers between devices, on_device(): lax.all_to_all(slope, 'space', split_axis=0, concat_axis=0, tiled=True, a...  6.76 us
    ppermute x7, starting transfers between devices, on_device(): lax.ppermute(sources[k], 'tm', swaps[k])  5.98 us
    all_to_all x1, starting transfers between devices, on_device(): lax.all_to_all(slope, 'space', split_axis=0, concat_axis=0, tiled=True, a...  5.77 us
  transfers between devices with their start and end apart: 18, of which 13 were waited for; matrix products, arithmetic and copies ran while one was open for 0% of the time, Pallas kernels for 21%

profile of v5, /device:TPU:4, one launch (start us, length us, event | category | flops | bytes accessed | tf_op | source)
XLA Modules:
  0.0 104.7 jit_solution(5305816168633990216)
XLA Ops:
  0.0 2.9 %flux_j.1 = bf16[4,8,40,640]{3,2,1,0:T(8,128)(2,1)} custom-call(bf16[4,5,40,1024]{3,2,1,0:T(8,128)(2,1)} %state_ref.1, f32[3,40,1024]{2,1,0:T(8,128)} %metric_j_ref.1), custom_call_target="tpu_custom_call" | custom-call | flops 10000000 | bytes 4000000 | tf_op jit(solution)/shard_map/flux_j/pallas_call | solution.py:80
  2.9 11.5 %all-to-all-start = ((bf16[32,40,640]{2,1,0:T(8,128)(2,1)}), bf16[32,40,640]{2,1,0:T(8,128)(2,1)S(1)}, u32[]{:S(2)}, u32[]{:S(2)}) async-start(bf16[32,40,640]{2,1,0:T(8,128)(2,1)} %bitcast.4), calls=%async_computation | async-start | bytes 3276800 | tf_op jit(solution)/shard_map/all_to_all | solution.py:445
  14.4 0.0 copy-start
  14.4 2.6 %pack_blocks.1 = (bf16[4,5,1024]{2,1,0:T(8,128)(2,1)}, bf16[4,5,1024]{2,1,0:T(8,128)(2,1)}, bf16[4,5,40,128]{3,2,1,0:T(8,128)(2,1)}, bf16[4,5,40,128]{3,2,1,0:T(...) custom-call(s32[1]{0:T(128)} %bitcast.me_ref, ...), custom_call_target="tpu_custom_call" | custom-call | bytes 3300000 | tf_op jit(solution)/shard_map/pack_blocks/pallas_call | solution.py:133
  17.0 0.1 collective-permute-start
  17.1 1.3 %collective-permute-start.1 = (bf16[4,5,40,128]{3,2,1,0:T(8,128)(2,1)}, bf16[4,5,40,128]{3,2,1,0:T(8,128)(2,1)S(1)}, u32[]{:S(2)}, u32[]{:S(2)}) collective-permute-start(bf16[4,5,40,128]{3,2,1,0:T(8,128)(2,1)} %get-tuple-element.29), channel_id=1, source_target_pairs={{0,64},{32,96},{64,0},{96,32},{128,192},{160,224},{192,128},{224,1... | collective-permute-start | bytes 614408 | tf_op jit(solution)/shard_map/ppermute | solution.py:449
  18.4 0.6 collective-permute-start.2
  19.0 0.5 collective-permute-start.3
  19.5 2.7 %collective-permute-start.4 = (bf16[4,5,40,128]{3,2,1,0:T(8,128)(2,1)}, bf16[4,5,40,128]{3,2,1,0:T(8,128)(2,1)S(1)}, u32[]{:S(2)}, u32[]{:S(2)}) collective-permute-start(bf16[4,5,40,128]{3,2,1,0:T(8,128)(2,1)} %get-tuple-element.32), channel_id=1, source_target_pairs={{0,160},{32,128},{64,224},{96,192},{128,32},{160,0},{192,96},{224,... | collective-permute-start | bytes 614408 | tf_op jit(solution)/shard_map/ppermute | solution.py:449
  22.2 0.0 collective-permute-done.refs_1_
  22.2 0.5 collective-permute-start.5
  22.7 2.6 %collective-permute-done.1.refs_2_ = bf16[4,5,40,128]{3,2,1,0:T(8,128)(2,1)S(1)} collective-permute-done((bf16[4,5,40,128]{3,2,1,0:T(8,128)(2,1)}, bf16[4,5,40,128]{3,2,1,0:T(8,128)(2,1)S(1)}, u32[]{:S(2)}, u32[]{:S(2)}) %collective-permute-start.1) | collective-permute-done | bytes 204832 | tf_op jit(solution)/shard_map/ppermute | solution.py:449
  25.3 0.0 collective-permute-start.6
  25.3 3.4 %collective-permute-done.2.refs_3_ = bf16[4,5,40,128]{3,2,1,0:T(8,128)(2,1)S(1)} collective-permute-done((bf16[4,5,40,128]{3,2,1,0:T(8,128)(2,1)}, bf16[4,5,40,128]{3,2,1,0:T(8,128)(2,1)S(1)}, u32[]{:S(2)}, u32[]{:S(2)}) %collective-permute-start.2) | collective-permute-done | bytes 204832 | tf_op jit(solution)/shard_map/ppermute | solution.py:449
  28.7 3.7 %collective-permute-start.7 = (bf16[4,5,1024]{2,1,0:T(8,128)(2,1)}, bf16[4,5,1024]{2,1,0:T(8,128)(2,1)S(1)}, u32[]{:S(2)}, u32[]{:S(2)}) collective-permute-start(bf16[4,5,1024]{2,1,0:T(8,128)(2,1)} %get-tuple-element.36), channel_id=1, source_target_pairs={{0,1},{1,2},{2,3},{3,4},{4,5},{5,6},{6,7},{7,8},{8,9},{9,10},{10,1... | collective-permute-start | bytes 122888 | tf_op jit(solution)/shard_map/ppermute | solution.py:447
  32.4 1.7 %collective-permute-done.3.refs_4_ = bf16[4,5,40,128]{3,2,1,0:T(8,128)(2,1)S(1)} collective-permute-done((bf16[4,5,40,128]{3,2,1,0:T(8,128)(2,1)}, bf16[4,5,40,128]{3,2,1,0:T(8,128)(2,1)S(1)}, u32[]{:S(2)}, u32[]{:S(2)}) %collective-permute-start.3) | collective-permute-done | bytes 204832 | tf_op jit(solution)/shard_map/ppermute | solution.py:449
  34.2 1.3 %collective-permute-start.8 = (bf16[4,5,1024]{2,1,0:T(8,128)(2,1)}, bf16[4,5,1024]{2,1,0:T(8,128)(2,1)S(1)}, u32[]{:S(2)}, u32[]{:S(2)}) collective-permute-start(bf16[4,5,1024]{2,1,0:T(8,128)(2,1)} %get-tuple-element.37), channel_id=1, source_target_pairs={{1,0},{2,1},{3,2},{4,3},{5,4},{6,5},{7,6},{8,7},{9,8},{10,9},{11,1... | collective-permute-start | bytes 122888 | tf_op jit(solution)/shard_map/ppermute | solution.py:448
  35.4 2.1 %collective-permute-done.4.refs_5_ = bf16[4,5,40,128]{3,2,1,0:T(8,128)(2,1)S(1)} collective-permute-done((bf16[4,5,40,128]{3,2,1,0:T(8,128)(2,1)}, bf16[4,5,40,128]{3,2,1,0:T(8,128)(2,1)S(1)}, u32[]{:S(2)}, u32[]{:S(2)}) %collective-permute-start.4) | collective-permute-done | bytes 204832 | tf_op jit(solution)/shard_map/ppermute | solution.py:449
  37.6 1.5 %collective-permute-done.5.refs_6_ = bf16[4,5,40,128]{3,2,1,0:T(8,128)(2,1)S(1)} collective-permute-done((bf16[4,5,40,128]{3,2,1,0:T(8,128)(2,1)}, bf16[4,5,40,128]{3,2,1,0:T(8,128)(2,1)S(1)}, u32[]{:S(2)}, u32[]{:S(2)}) %collective-permute-start.5) | collective-permute-done | bytes 204832 | tf_op jit(solution)/shard_map/ppermute | solution.py:449
  39.1 3.5 %collective-permute-done.6.refs_7_ = bf16[4,5,40,128]{3,2,1,0:T(8,128)(2,1)S(1)} collective-permute-done((bf16[4,5,40,128]{3,2,1,0:T(8,128)(2,1)}, bf16[4,5,40,128]{3,2,1,0:T(8,128)(2,1)S(1)}, u32[]{:S(2)}, u32[]{:S(2)}) %collective-permute-start.6) | collective-permute-done | bytes 204832 | tf_op jit(solution)/shard_map/ppermute | solution.py:449
  42.6 0.0 copy-done.2
  42.6 0.0 copy-done.4
  42.6 0.6 copy-done.7
  43.2 3.5 %source_blocks.1 = (bf16[4,5,40,128]{3,2,1,0:T(8,128)(2,1)}, bf16[4,5,40,128]{3,2,1,0:T(8,128)(2,1)}, bf16[4,5,40,128]{3,2,1,0:T(8,128)(2,1)}, bf16[4,5,40,128]{...) custom-call(s32[1]{0:T(128)} %bitcast.me_ref, ...), custom_call_target="tpu_custom_call" | custom-call | flops 420000000 | bytes 10000000 | tf_op jit(solution)/shard_map/source_blocks/pallas_call | solution.py:216
  46.7 10.2 %all-to-all-done = bf16[32,40,640]{2,1,0:T(8,128)(2,1)S(1)} async-done(((bf16[32,40,640]{2,1,0:T(8,128)(2,1)}), bf16[32,40,640]{2,1,0:T(8,128)(2,1)S(1)}, u32[]{:S(2)}, u32[]{:S(2)}) %all-to-all-start) | async-done | bytes 1638432 | tf_op jit(solution)/shard_map/all_to_all | solution.py:445
  56.9 3.9 %slope_lines.1 = bf16[32,40,640]{2,1,0:T(8,128)(2,1)} custom-call(bf16[640,1280]{1,0:T(8,128)(2,1)S(1)} %get-tuple-element.35.held_ref, bf16[1280,640]{1,0:T(8,128)(2,1)S(1)} %bitcast.3, bf16[1280,1280]{1,0:T(8,128)(2,1)} %deriv_hbm.3), custom_call_target="tpu_custom_call" | custom-call | flops 2097152000 | bytes 7000000 | tf_op jit(solution)/shard_map/slope_lines/pallas_call | solution.py:374
  60.9 0.0 collective-permute-done.7.low_ref
  60.9 0.0 collective-permute-done.8.high_ref
  60.9 5.8 %all-to-all-start.1 = ((bf16[32,40,640]{2,1,0:T(8,128)(2,1)}), bf16[32,40,640]{2,1,0:T(8,128)(2,1)S(1)}, u32[]{:S(2)}, u32[]{:S(2)}) async-start(bf16[32,40,640]{2,1,0:T(8,128)(2,1)} %slope_lines.1), calls=%async_computation.1 | async-start | bytes 3276800 | tf_op jit(solution)/shard_map/all_to_all | solution.py:454
  66.7 0.1 collective-permute-start.9
  66.8 1.3 %collective-permute-start.10 = (bf16[4,5,40,128]{3,2,1,0:T(8,128)(2,1)S(1)}, bf16[4,5,40,128]{3,2,1,0:T(8,128)(2,1)S(1)}, u32[]{:S(2)}, u32[]{:S(2)}) collective-permute-start(bf16[4,5,40,128]{3,2,1,0:T(8,128)(2,1)S(1)} %copy-done.20), channel_id=1, source_target_pairs={{0,64},{32,96},{64,0},{96,32},{128,192},{160,224},{192,128},{224,1... | collective-permute-start | bytes 614408 | tf_op jit(solution)/shard_map/ppermute | solution.py:451
  68.1 0.6 collective-permute-start.11
  68.7 0.5 collective-permute-start.12
  69.2 2.7 %collective-permute-start.13 = (bf16[4,5,40,128]{3,2,1,0:T(8,128)(2,1)S(1)}, bf16[4,5,40,128]{3,2,1,0:T(8,128)(2,1)S(1)}, u32[]{:S(2)}, u32[]{:S(2)}) collective-permute-start(bf16[4,5,40,128]{3,2,1,0:T(8,128)(2,1)S(1)} %copy-done.17), channel_id=1, source_target_pairs={{0,160},{32,128},{64,224},{96,192},{128,32},{160,0},{192,96},{224,... | collective-permute-start | bytes 614408 | tf_op jit(solution)/shard_map/ppermute | solution.py:451
  71.9 0.0 collective-permute-done.9.refs_1_
  71.9 0.8 collective-permute-start.14
  72.7 2.1 %collective-permute-done.10.refs_2_ = bf16[4,5,40,128]{3,2,1,0:T(8,128)(2,1)S(1)} collective-permute-done((bf16[4,5,40,128]{3,2,1,0:T(8,128)(2,1)S(1)}, bf16[4,5,40,128]{3,2,1,0:T(8,128)(2,1)S(1)}, u32[]{:S(2)}, u32[]{:S(2)}) %collective-permute-start.10) | collective-permute-done | bytes 204832 | tf_op jit(solution)/shard_map/ppermute | solution.py:451
  74.8 0.0 collective-permute-start.15
  74.8 8.5 %local_terms.1.partial_hbm = f32[4,5,40,1024]{3,2,1,0:T(8,128)} custom-call(bf16[4,5,40,1024]{3,2,1,0:T(8,128)(2,1)} %state_ref.1, f32[3,40,1024]{2,1,0:T(8,128)} %metric_i_ref.1, f32[3,40,1024]{2,1,0:T(8,128)} %metric_j_ref.1, bf16[4,5,1024]{2,1,0:T(8,128)(2,1)S(1)} %collective-permute-done.7.low_ref, ...), custom_call_target="tpu_custom_call" | custom-call | flops 1677721600 | bytes 11000000 | tf_op jit(solution)/shard_map/local_terms/pallas_call | solution.py:272
  83.3 0.0 collective-permute-done.11.refs_3_
  83.3 0.3 collective-permute-done.12.refs_4_
  83.6 3.4 %collective-permute-done.13.refs_5_ = bf16[4,5,40,128]{3,2,1,0:T(8,128)(2,1)S(1)} collective-permute-done((bf16[4,5,40,128]{3,2,1,0:T(8,128)(2,1)S(1)}, bf16[4,5,40,128]{3,2,1,0:T(8,128)(2,1)S(1)}, u32[]{:S(2)}, u32[]{:S(2)}) %collective-permute-start.13) | collective-permute-done | bytes 204832 | tf_op jit(solution)/shard_map/ppermute | solution.py:451
  87.1 1.8 %collective-permute-done.14.refs_6_ = bf16[4,5,40,128]{3,2,1,0:T(8,128)(2,1)S(1)} collective-permute-done((bf16[4,5,40,128]{3,2,1,0:T(8,128)(2,1)S(1)}, bf16[4,5,40,128]{3,2,1,0:T(8,128)(2,1)S(1)}, u32[]{:S(2)}, u32[]{:S(2)}) %collective-permute-start.14) | collective-permute-done | bytes 204832 | tf_op jit(solution)/shard_map/ppermute | solution.py:451
  88.8 3.5 %collective-permute-done.15.refs_7_ = bf16[4,5,40,128]{3,2,1,0:T(8,128)(2,1)S(1)} collective-permute-done((bf16[4,5,40,128]{3,2,1,0:T(8,128)(2,1)S(1)}, bf16[4,5,40,128]{3,2,1,0:T(8,128)(2,1)S(1)}, u32[]{:S(2)}, u32[]{:S(2)}) %collective-permute-start.15) | collective-permute-done | bytes 204832 | tf_op jit(solution)/shard_map/ppermute | solution.py:451
  92.3 0.7 copy-done.14
  93.0 3.4 %add_sources.1.total_ref = bf16[4,5,40,1024]{3,2,1,0:T(8,128)(2,1)S(1)} custom-call(s32[1]{0:T(128)} %bitcast.me_ref, f32[4,5,40,1024]{3,2,1,0:T(8,128)} %local_terms.1.partial_hbm, bf16[4,5,40,128]{3,2,1,0:T(8,128)(2,1)} %get-tuple-element.40.refs_0_, bf16[4,5,40,128]{3,2,1,0:T(8,128)(2,1)} %copy-done.8, bf16[4,5,40,128]{3,2,1,0:T(8,128)(2,1)} %copy-done.9, ...), custom_call_target="tpu_custom_call" | custom-call | flops 1000000 | bytes 8000000 | tf_op jit(solution)/shard_map/add_sources/pallas_call | solution.py:311
  96.4 6.8 %all-to-all-done.1.slope_ref = bf16[32,40,640]{2,1,0:T(8,128)(2,1)S(1)} async-done(((bf16[32,40,640]{2,1,0:T(8,128)(2,1)}), bf16[32,40,640]{2,1,0:T(8,128)(2,1)S(1)}, u32[]{:S(2)}, u32[]{:S(2)}) %all-to-all-start.1) | async-done | bytes 1638432 | tf_op jit(solution)/shard_map/all_to_all | solution.py:454
  103.2 1.3 %finish.1 = bf16[4,5,40,1024]{3,2,1,0:T(8,128)(2,1)} custom-call(bf16[4,5,40,1024]{3,2,1,0:T(8,128)(2,1)S(1)} %add_sources.1.total_ref, bf16[32,40,640]{2,1,0:T(8,128)(2,1)S(1)} %all-to-all-done.1.slope_ref), custom_call_target="tpu_custom_call" | custom-call | flops 1000000 | bytes 5000000 | tf_op jit(solution)/shard_map/finish/pallas_call | solution.py:420
  (39 shorter events, 0.1 us)
Async XLA Ops:
  2.9 54.0 %all-to-all-start = ((bf16[32,40,640]{2,1,0:T(8,128)(2,1)}), bf16[32,40,640]{2,1,0:T(8,128)(2,1)S(1)}, u32[]{:S(2)}, u32[]{:S(2)}) async-start(bf16[32,40,640]{2,1,0:T(8,128)(2,1)} %bitcast.4), calls=%async_computation | async-start | bytes 3276800 | tf_op jit(solution)/shard_map/all_to_all | solution.py:445
  14.4 28.9 %copy-start = (bf16[32,32]{1,0:T(8,128)(2,1)S(1)}, bf16[32,32]{1,0:T(8,128)(2,1)}, u32[]{:S(2)}) copy-start(bf16[32,32]{1,0:T(8,128)(2,1)} %spectral_ref.1) | copy-start | bytes 6148
  17.0 5.2 %collective-permute-start = (bf16[4,5,40,128]{3,2,1,0:T(8,128)(2,1)}, bf16[4,5,40,128]{3,2,1,0:T(8,128)(2,1)S(1)}, u32[]{:S(2)}, u32[]{:S(2)}) collective-permute-start(bf16[4,5,40,128]{3,2,1,0:T(8,128)(2,1)} %get-tuple-element.28), channel_id=1, source_target_pairs={{0,32},{32,0},{64,96},{96,64},{128,160},{160,128},{192,224},{224,1... | collective-permute-start | bytes 614408 | tf_op jit(solution)/shard_map/ppermute | solution.py:449
  17.1 8.2 %collective-permute-start.1 = (bf16[4,5,40,128]{3,2,1,0:T(8,128)(2,1)}, bf16[4,5,40,128]{3,2,1,0:T(8,128)(2,1)S(1)}, u32[]{:S(2)}, u32[]{:S(2)}) collective-permute-start(bf16[4,5,40,128]{3,2,1,0:T(8,128)(2,1)} %get-tuple-element.29), channel_id=1, source_target_pairs={{0,64},{32,96},{64,0},{96,32},{128,192},{160,224},{192,128},{224,1... | collective-permute-start | bytes 614408 | tf_op jit(solution)/shard_map/ppermute | solution.py:449
  18.4 10.3 %collective-permute-start.2 = (bf16[4,5,40,128]{3,2,1,0:T(8,128)(2,1)}, bf16[4,5,40,128]{3,2,1,0:T(8,128)(2,1)S(1)}, u32[]{:S(2)}, u32[]{:S(2)}) collective-permute-start(bf16[4,5,40,128]{3,2,1,0:T(8,128)(2,1)} %get-tuple-element.30), channel_id=1, source_target_pairs={{0,96},{32,64},{64,32},{96,0},{128,224},{160,192},{192,160},{224,1... | collective-permute-start | bytes 614408 | tf_op jit(solution)/shard_map/ppermute | solution.py:449
  19.0 15.2 %collective-permute-start.3 = (bf16[4,5,40,128]{3,2,1,0:T(8,128)(2,1)}, bf16[4,5,40,128]{3,2,1,0:T(8,128)(2,1)S(1)}, u32[]{:S(2)}, u32[]{:S(2)}) collective-permute-start(bf16[4,5,40,128]{3,2,1,0:T(8,128)(2,1)} %get-tuple-element.31), channel_id=1, source_target_pairs={{0,128},{32,160},{64,192},{96,224},{128,0},{160,32},{192,64},{224,... | collective-permute-start | bytes 614408 | tf_op jit(solution)/shard_map/ppermute | solution.py:449
  19.5 18.1 %collective-permute-start.4 = (bf16[4,5,40,128]{3,2,1,0:T(8,128)(2,1)}, bf16[4,5,40,128]{3,2,1,0:T(8,128)(2,1)S(1)}, u32[]{:S(2)}, u32[]{:S(2)}) collective-permute-start(bf16[4,5,40,128]{3,2,1,0:T(8,128)(2,1)} %get-tuple-element.32), channel_id=1, source_target_pairs={{0,160},{32,128},{64,224},{96,192},{128,32},{160,0},{192,96},{224,... | collective-permute-start | bytes 614408 | tf_op jit(solution)/shard_map/ppermute | solution.py:449
  22.2 20.3 %copy-start.1 = (bf16[4,5,40,128]{3,2,1,0:T(8,128)(2,1)}, bf16[4,5,40,128]{3,2,1,0:T(8,128)(2,1)S(1)}, u32[]{:S(2)}) copy-start(bf16[4,5,40,128]{3,2,1,0:T(8,128)(2,1)S(1)} %collective-permute-done.refs_1_) | copy-start | bytes 614404
  22.2 16.9 %collective-permute-start.5 = (bf16[4,5,40,128]{3,2,1,0:T(8,128)(2,1)}, bf16[4,5,40,128]{3,2,1,0:T(8,128)(2,1)S(1)}, u32[]{:S(2)}, u32[]{:S(2)}) collective-permute-start(bf16[4,5,40,128]{3,2,1,0:T(8,128)(2,1)} %get-tuple-element.33), channel_id=1, source_target_pairs={{0,192},{32,224},{64,128},{96,160},{128,64},{160,96},{192,0},{224,... | collective-permute-start | bytes 614408 | tf_op jit(solution)/shard_map/ppermute | solution.py:449
  25.3 17.3 %copy-start.2 = (bf16[4,5,40,128]{3,2,1,0:T(8,128)(2,1)}, bf16[4,5,40,128]{3,2,1,0:T(8,128)(2,1)S(1)}, u32[]{:S(2)}) copy-start(bf16[4,5,40,128]{3,2,1,0:T(8,128)(2,1)S(1)} %collective-permute-done.1.refs_2_) | copy-start | bytes 614404
  25.3 17.2 %collective-permute-start.6 = (bf16[4,5,40,128]{3,2,1,0:T(8,128)(2,1)}, bf16[4,5,40,128]{3,2,1,0:T(8,128)(2,1)S(1)}, u32[]{:S(2)}, u32[]{:S(2)}) collective-permute-start(bf16[4,5,40,128]{3,2,1,0:T(8,128)(2,1)} %get-tuple-element.34), channel_id=1, source_target_pairs={{0,224},{32,192},{64,160},{96,128},{128,96},{160,64},{192,32},{224... | collective-permute-start | bytes 614408 | tf_op jit(solution)/shard_map/ppermute | solution.py:449
  28.7 13.8 %copy-start.3 = (bf16[4,5,40,128]{3,2,1,0:T(8,128)(2,1)}, bf16[4,5,40,128]{3,2,1,0:T(8,128)(2,1)S(1)}, u32[]{:S(2)}) copy-start(bf16[4,5,40,128]{3,2,1,0:T(8,128)(2,1)S(1)} %collective-permute-done.2.refs_3_) | copy-start | bytes 614404
  28.7 32.2 %collective-permute-start.7 = (bf16[4,5,1024]{2,1,0:T(8,128)(2,1)}, bf16[4,5,1024]{2,1,0:T(8,128)(2,1)S(1)}, u32[]{:S(2)}, u32[]{:S(2)}) collective-permute-start(bf16[4,5,1024]{2,1,0:T(8,128)(2,1)} %get-tuple-element.36), channel_id=1, source_target_pairs={{0,1},{1,2},{2,3},{3,4},{4,5},{5,6},{6,7},{7,8},{8,9},{9,10},{10,1... | collective-permute-start | bytes 122888 | tf_op jit(solution)/shard_map/ppermute | solution.py:447
  34.2 8.4 %copy-start.4 = (bf16[4,5,40,128]{3,2,1,0:T(8,128)(2,1)}, bf16[4,5,40,128]{3,2,1,0:T(8,128)(2,1)S(1)}, u32[]{:S(2)}) copy-start(bf16[4,5,40,128]{3,2,1,0:T(8,128)(2,1)S(1)} %collective-permute-done.3.refs_4_) | copy-start | bytes 614404
  34.2 26.8 %collective-permute-start.8 = (bf16[4,5,1024]{2,1,0:T(8,128)(2,1)}, bf16[4,5,1024]{2,1,0:T(8,128)(2,1)S(1)}, u32[]{:S(2)}, u32[]{:S(2)}) collective-permute-start(bf16[4,5,1024]{2,1,0:T(8,128)(2,1)} %get-tuple-element.37), channel_id=1, source_target_pairs={{1,0},{2,1},{3,2},{4,3},{5,4},{6,5},{7,6},{8,7},{9,8},{10,9},{11,1... | collective-permute-start | bytes 122888 | tf_op jit(solution)/shard_map/ppermute | solution.py:448
  37.6 5.0 %copy-start.5 = (bf16[4,5,40,128]{3,2,1,0:T(8,128)(2,1)}, bf16[4,5,40,128]{3,2,1,0:T(8,128)(2,1)S(1)}, u32[]{:S(2)}) copy-start(bf16[4,5,40,128]{3,2,1,0:T(8,128)(2,1)S(1)} %collective-permute-done.4.refs_5_) | copy-start | bytes 614404
  39.1 3.5 %copy-start.6 = (bf16[4,5,40,128]{3,2,1,0:T(8,128)(2,1)}, bf16[4,5,40,128]{3,2,1,0:T(8,128)(2,1)S(1)}, u32[]{:S(2)}) copy-start(bf16[4,5,40,128]{3,2,1,0:T(8,128)(2,1)S(1)} %collective-permute-done.5.refs_6_) | copy-start | bytes 614404
  42.5 0.7 copy-start.7
  60.8 5.9 %copy-start.21 = (bf16[4,5,40,128]{3,2,1,0:T(8,128)(2,1)S(1)}, bf16[4,5,40,128]{3,2,1,0:T(8,128)(2,1)}, u32[]{:S(2)}) copy-start(bf16[4,5,40,128]{3,2,1,0:T(8,128)(2,1)} %get-tuple-element.41) | copy-start | bytes 614404
  60.8 6.0 %copy-start.20 = (bf16[4,5,40,128]{3,2,1,0:T(8,128)(2,1)S(1)}, bf16[4,5,40,128]{3,2,1,0:T(8,128)(2,1)}, u32[]{:S(2)}) copy-start(bf16[4,5,40,128]{3,2,1,0:T(8,128)(2,1)} %get-tuple-element.42) | copy-start | bytes 614404
  60.9 7.3 %copy-start.19 = (bf16[4,5,40,128]{3,2,1,0:T(8,128)(2,1)S(1)}, bf16[4,5,40,128]{3,2,1,0:T(8,128)(2,1)}, u32[]{:S(2)}) copy-start(bf16[4,5,40,128]{3,2,1,0:T(8,128)(2,1)} %get-tuple-element.43) | copy-start | bytes 614404
  60.9 7.8 %copy-start.18 = (bf16[4,5,40,128]{3,2,1,0:T(8,128)(2,1)S(1)}, bf16[4,5,40,128]{3,2,1,0:T(8,128)(2,1)}, u32[]{:S(2)}) copy-start(bf16[4,5,40,128]{3,2,1,0:T(8,128)(2,1)} %get-tuple-element.44) | copy-start | bytes 614404
  60.9 8.3 %copy-start.17 = (bf16[4,5,40,128]{3,2,1,0:T(8,128)(2,1)S(1)}, bf16[4,5,40,128]{3,2,1,0:T(8,128)(2,1)}, u32[]{:S(2)}) copy-start(bf16[4,5,40,128]{3,2,1,0:T(8,128)(2,1)} %get-tuple-element.45) | copy-start | bytes 614404
  60.9 11.0 %copy-start.16 = (bf16[4,5,40,128]{3,2,1,0:T(8,128)(2,1)S(1)}, bf16[4,5,40,128]{3,2,1,0:T(8,128)(2,1)}, u32[]{:S(2)}) copy-start(bf16[4,5,40,128]{3,2,1,0:T(8,128)(2,1)} %get-tuple-element.46) | copy-start | bytes 614404
  60.9 13.9 %copy-start.15 = (bf16[4,5,40,128]{3,2,1,0:T(8,128)(2,1)S(1)}, bf16[4,5,40,128]{3,2,1,0:T(8,128)(2,1)}, u32[]{:S(2)}) copy-start(bf16[4,5,40,128]{3,2,1,0:T(8,128)(2,1)} %get-tuple-element.47) | copy-start | bytes 614404
  60.9 42.3 %all-to-all-start.1 = ((bf16[32,40,640]{2,1,0:T(8,128)(2,1)}), bf16[32,40,640]{2,1,0:T(8,128)(2,1)S(1)}, u32[]{:S(2)}, u32[]{:S(2)}) async-start(bf16[32,40,640]{2,1,0:T(8,128)(2,1)} %slope_lines.1), calls=%async_computation.1 | async-start | bytes 3276800 | tf_op jit(solution)/shard_map/all_to_all | solution.py:454
  66.7 5.2 %collective-permute-start.9 = (bf16[4,5,40,128]{3,2,1,0:T(8,128)(2,1)S(1)}, bf16[4,5,40,128]{3,2,1,0:T(8,128)(2,1)S(1)}, u32[]{:S(2)}, u32[]{:S(2)}) collective-permute-start(bf16[4,5,40,128]{3,2,1,0:T(8,128)(2,1)S(1)} %copy-done.21), channel_id=1, source_target_pairs={{0,32},{32,0},{64,96},{96,64},{128,160},{160,128},{192,224},{224,1... | collective-permute-start | bytes 614408 | tf_op jit(solution)/shard_map/ppermute | solution.py:451
  66.8 8.0 %collective-permute-start.10 = (bf16[4,5,40,128]{3,2,1,0:T(8,128)(2,1)S(1)}, bf16[4,5,40,128]{3,2,1,0:T(8,128)(2,1)S(1)}, u32[]{:S(2)}, u32[]{:S(2)}) collective-permute-start(bf16[4,5,40,128]{3,2,1,0:T(8,128)(2,1)S(1)} %copy-done.20), channel_id=1, source_target_pairs={{0,64},{32,96},{64,0},{96,32},{128,192},{160,224},{192,128},{224,1... | collective-permute-start | bytes 614408 | tf_op jit(solution)/shard_map/ppermute | solution.py:451
  68.1 15.2 %collective-permute-start.11 = (bf16[4,5,40,128]{3,2,1,0:T(8,128)(2,1)S(1)}, bf16[4,5,40,128]{3,2,1,0:T(8,128)(2,1)S(1)}, u32[]{:S(2)}, u32[]{:S(2)}) collective-permute-start(bf16[4,5,40,128]{3,2,1,0:T(8,128)(2,1)S(1)} %copy-done.19), channel_id=1, source_target_pairs={{0,96},{32,64},{64,32},{96,0},{128,224},{160,192},{192,160},{224,1... | collective-permute-start | bytes 614408 | tf_op jit(solution)/shard_map/ppermute | solution.py:451
  68.7 14.9 %collective-permute-start.12 = (bf16[4,5,40,128]{3,2,1,0:T(8,128)(2,1)S(1)}, bf16[4,5,40,128]{3,2,1,0:T(8,128)(2,1)S(1)}, u32[]{:S(2)}, u32[]{:S(2)}) collective-permute-start(bf16[4,5,40,128]{3,2,1,0:T(8,128)(2,1)S(1)} %copy-done.18), channel_id=1, source_target_pairs={{0,128},{32,160},{64,192},{96,224},{128,0},{160,32},{192,64},{224,... | collective-permute-start | bytes 614408 | tf_op jit(solution)/shard_map/ppermute | solution.py:451
  69.2 17.9 %collective-permute-start.13 = (bf16[4,5,40,128]{3,2,1,0:T(8,128)(2,1)S(1)}, bf16[4,5,40,128]{3,2,1,0:T(8,128)(2,1)S(1)}, u32[]{:S(2)}, u32[]{:S(2)}) collective-permute-start(bf16[4,5,40,128]{3,2,1,0:T(8,128)(2,1)S(1)} %copy-done.17), channel_id=1, source_target_pairs={{0,160},{32,128},{64,224},{96,192},{128,32},{160,0},{192,96},{224,... | collective-permute-start | bytes 614408 | tf_op jit(solution)/shard_map/ppermute | solution.py:451
  71.9 11.4 %copy-start.8 = (bf16[4,5,40,128]{3,2,1,0:T(8,128)(2,1)}, bf16[4,5,40,128]{3,2,1,0:T(8,128)(2,1)S(1)}, u32[]{:S(2)}) copy-start(bf16[4,5,40,128]{3,2,1,0:T(8,128)(2,1)S(1)} %collective-permute-done.9.refs_1_) | copy-start | bytes 614404
  71.9 16.9 %collective-permute-start.14 = (bf16[4,5,40,128]{3,2,1,0:T(8,128)(2,1)S(1)}, bf16[4,5,40,128]{3,2,1,0:T(8,128)(2,1)S(1)}, u32[]{:S(2)}, u32[]{:S(2)}) collective-permute-start(bf16[4,5,40,128]{3,2,1,0:T(8,128)(2,1)S(1)} %copy-done.16), channel_id=1, source_target_pairs={{0,192},{32,224},{64,128},{96,160},{128,64},{160,96},{192,0},{224,... | collective-permute-start | bytes 614408 | tf_op jit(solution)/shard_map/ppermute | solution.py:451
  74.8 8.5 %copy-start.9 = (bf16[4,5,40,128]{3,2,1,0:T(8,128)(2,1)}, bf16[4,5,40,128]{3,2,1,0:T(8,128)(2,1)S(1)}, u32[]{:S(2)}) copy-start(bf16[4,5,40,128]{3,2,1,0:T(8,128)(2,1)S(1)} %collective-permute-done.10.refs_2_) | copy-start | bytes 614404
  74.8 17.5 %collective-permute-start.15 = (bf16[4,5,40,128]{3,2,1,0:T(8,128)(2,1)S(1)}, bf16[4,5,40,128]{3,2,1,0:T(8,128)(2,1)S(1)}, u32[]{:S(2)}, u32[]{:S(2)}) collective-permute-start(bf16[4,5,40,128]{3,2,1,0:T(8,128)(2,1)S(1)} %copy-done.15), channel_id=1, source_target_pairs={{0,224},{32,192},{64,160},{96,128},{128,96},{160,64},{192,32},{224... | collective-permute-start | bytes 614408 | tf_op jit(solution)/shard_map/ppermute | solution.py:451
  83.3 9.0 %copy-start.10 = (bf16[4,5,40,128]{3,2,1,0:T(8,128)(2,1)}, bf16[4,5,40,128]{3,2,1,0:T(8,128)(2,1)S(1)}, u32[]{:S(2)}) copy-start(bf16[4,5,40,128]{3,2,1,0:T(8,128)(2,1)S(1)} %collective-permute-done.11.refs_3_) | copy-start | bytes 614404
  83.6 8.7 %copy-start.11 = (bf16[4,5,40,128]{3,2,1,0:T(8,128)(2,1)}, bf16[4,5,40,128]{3,2,1,0:T(8,128)(2,1)S(1)}, u32[]{:S(2)}) copy-start(bf16[4,5,40,128]{3,2,1,0:T(8,128)(2,1)S(1)} %collective-permute-done.12.refs_4_) | copy-start | bytes 614404
  87.1 5.2 %copy-start.12 = (bf16[4,5,40,128]{3,2,1,0:T(8,128)(2,1)}, bf16[4,5,40,128]{3,2,1,0:T(8,128)(2,1)S(1)}, u32[]{:S(2)}) copy-start(bf16[4,5,40,128]{3,2,1,0:T(8,128)(2,1)S(1)} %collective-permute-done.13.refs_5_) | copy-start | bytes 614404
  88.8 3.5 %copy-start.13 = (bf16[4,5,40,128]{3,2,1,0:T(8,128)(2,1)}, bf16[4,5,40,128]{3,2,1,0:T(8,128)(2,1)S(1)}, u32[]{:S(2)}) copy-start(bf16[4,5,40,128]{3,2,1,0:T(8,128)(2,1)S(1)} %collective-permute-done.14.refs_6_) | copy-start | bytes 614404
  92.3 0.7 copy-start.14

commit v6 on v5

--- a/solution.py
+++ b/solution.py
@@ -339,7 +339,7 @@
 
     def multiply(deriv_ref, base):
         first = 0
-        for count in (6, 6, blocks - 12):
+        for count in (blocks // 2, blocks // 2):
             rows = slice(first * block, (first + count) * block)
             total = jnp.dot(deriv_ref[rows, :], lines_ref[...], preferred_element_type=jnp.float32)
             for c in range(count):

time: 107 us -> 106 us (level)
  no operation moved by 1% of the time
where the time goes in v6:
time: 106 us; the launch traced here: 104 us
  waiting for transfers between devices  43 us (41%)
  starting transfers between devices  33.7 us (32%)
  Pallas kernels  26.1 us (25%)
  local copies, waits for them, and re-layouts  1.38 us (1%)
    ppermute x7, waiting for transfers between devices, on_device(): lax.ppermute(own[k], 'tm', swaps[k])  14.8 us
    all_to_all x1, starting transfers between devices, on_device(): lax.all_to_all(outgoing, 'space', split_axis=0, concat_axis=0, tiled=True)  11.5 us
    ppermute x7, waiting for transfers between devices, on_device(): lax.ppermute(sources[k], 'tm', swaps[k])  11.1 us
    all_to_all x1, waiting for transfers between devices, on_device(): lax.all_to_all(outgoing, 'space', split_axis=0, concat_axis=0, tiled=True)  10.2 us
    pallas_call x1, Pallas kernels, local_terms(): pl.pallas_call(local_kernel, grid=(nt,), out_shape=pltpu.HBM((nt, nv, nj,...  8.49 us
    all_to_all x1, waiting for transfers between devices, on_device(): lax.all_to_all(slope, 'space', split_axis=0, concat_axis=0, tiled=True, a...  6.94 us
    ppermute x7, starting transfers between devices, on_device(): lax.ppermute(sources[k], 'tm', swaps[k])  5.8 us
    all_to_all x1, starting transfers between devices, on_device(): lax.all_to_all(slope, 'space', split_axis=0, concat_axis=0, tiled=True, a...  5.77 us
  transfers between devices with their start and end apart: 18, of which 13 were waited for; matrix products, arithmetic and copies ran while one was open for 0% of the time, Pallas kernels for 21%

profile of v6, /device:TPU:4, one launch (start us, length us, event | category | flops | bytes accessed | tf_op | source)
XLA Modules:
  0.0 104.5 jit_solution(11420095071780974701)
XLA Ops:
  0.0 2.9 %flux_j.1 = bf16[4,8,40,640]{3,2,1,0:T(8,128)(2,1)} custom-call(bf16[4,5,40,1024]{3,2,1,0:T(8,128)(2,1)} %state_ref.1, f32[3,40,1024]{2,1,0:T(8,128)} %metric_j_ref.1), custom_call_target="tpu_custom_call" | custom-call | flops 10000000 | bytes 4000000 | tf_op jit(solution)/shard_map/flux_j/pallas_call | solution.py:80
  2.9 11.5 %all-to-all-start = ((bf16[32,40,640]{2,1,0:T(8,128)(2,1)}), bf16[32,40,640]{2,1,0:T(8,128)(2,1)S(1)}, u32[]{:S(2)}, u32[]{:S(2)}) async-start(bf16[32,40,640]{2,1,0:T(8,128)(2,1)} %bitcast.4), calls=%async_computation | async-start | bytes 3276800 | tf_op jit(solution)/shard_map/all_to_all | solution.py:445
  14.4 0.0 copy-start
  14.4 2.6 %pack_blocks.1 = (bf16[4,5,1024]{2,1,0:T(8,128)(2,1)}, bf16[4,5,1024]{2,1,0:T(8,128)(2,1)}, bf16[4,5,40,128]{3,2,1,0:T(8,128)(2,1)}, bf16[4,5,40,128]{3,2,1,0:T(...) custom-call(s32[1]{0:T(128)} %bitcast.me_ref, ...), custom_call_target="tpu_custom_call" | custom-call | bytes 3300000 | tf_op jit(solution)/shard_map/pack_blocks/pallas_call | solution.py:133
  17.0 0.1 collective-permute-start
  17.1 1.3 %collective-permute-start.1 = (bf16[4,5,40,128]{3,2,1,0:T(8,128)(2,1)}, bf16[4,5,40,128]{3,2,1,0:T(8,128)(2,1)S(1)}, u32[]{:S(2)}, u32[]{:S(2)}) collective-permute-start(bf16[4,5,40,128]{3,2,1,0:T(8,128)(2,1)} %get-tuple-element.29), channel_id=1, source_target_pairs={{0,64},{32,96},{64,0},{96,32},{128,192},{160,224},{192,128},{224,1... | collective-permute-start | bytes 614408 | tf_op jit(solution)/shard_map/ppermute | solution.py:449
  18.4 0.6 collective-permute-start.2
  19.0 0.5 collective-permute-start.3
  19.5 2.7 %collective-permute-start.4 = (bf16[4,5,40,128]{3,2,1,0:T(8,128)(2,1)}, bf16[4,5,40,128]{3,2,1,0:T(8,128)(2,1)S(1)}, u32[]{:S(2)}, u32[]{:S(2)}) collective-permute-start(bf16[4,5,40,128]{3,2,1,0:T(8,128)(2,1)} %get-tuple-element.32), channel_id=1, source_target_pairs={{0,160},{32,128},{64,224},{96,192},{128,32},{160,0},{192,96},{224,... | collective-permute-start | bytes 614408 | tf_op jit(solution)/shard_map/ppermute | solution.py:449
  22.2 0.0 collective-permute-done.refs_1_
  22.2 0.5 collective-permute-start.5
  22.7 2.6 %collective-permute-done.1.refs_2_ = bf16[4,5,40,128]{3,2,1,0:T(8,128)(2,1)S(1)} collective-permute-done((bf16[4,5,40,128]{3,2,1,0:T(8,128)(2,1)}, bf16[4,5,40,128]{3,2,1,0:T(8,128)(2,1)S(1)}, u32[]{:S(2)}, u32[]{:S(2)}) %collective-permute-start.1) | collective-permute-done | bytes 204832 | tf_op jit(solution)/shard_map/ppermute | solution.py:449
  25.3 0.0 collective-permute-start.6
  25.3 3.4 %collective-permute-done.2.refs_3_ = bf16[4,5,40,128]{3,2,1,0:T(8,128)(2,1)S(1)} collective-permute-done((bf16[4,5,40,128]{3,2,1,0:T(8,128)(2,1)}, bf16[4,5,40,128]{3,2,1,0:T(8,128)(2,1)S(1)}, u32[]{:S(2)}, u32[]{:S(2)}) %collective-permute-start.2) | collective-permute-done | bytes 204832 | tf_op jit(solution)/shard_map/ppermute | solution.py:449
  28.7 3.7 %collective-permute-start.7 = (bf16[4,5,1024]{2,1,0:T(8,128)(2,1)}, bf16[4,5,1024]{2,1,0:T(8,128)(2,1)S(1)}, u32[]{:S(2)}, u32[]{:S(2)}) collective-permute-start(bf16[4,5,1024]{2,1,0:T(8,128)(2,1)} %get-tuple-element.36), channel_id=1, source_target_pairs={{0,1},{1,2},{2,3},{3,4},{4,5},{5,6},{6,7},{7,8},{8,9},{9,10},{10,1... | collective-permute-start | bytes 122888 | tf_op jit(solution)/shard_map/ppermute | solution.py:447
  32.4 1.7 %collective-permute-done.3.refs_4_ = bf16[4,5,40,128]{3,2,1,0:T(8,128)(2,1)S(1)} collective-permute-done((bf16[4,5,40,128]{3,2,1,0:T(8,128)(2,1)}, bf16[4,5,40,128]{3,2,1,0:T(8,128)(2,1)S(1)}, u32[]{:S(2)}, u32[]{:S(2)}) %collective-permute-start.3) | collective-permute-done | bytes 204832 | tf_op jit(solution)/shard_map/ppermute | solution.py:449
  34.2 1.3 %collective-permute-start.8 = (bf16[4,5,1024]{2,1,0:T(8,128)(2,1)}, bf16[4,5,1024]{2,1,0:T(8,128)(2,1)S(1)}, u32[]{:S(2)}, u32[]{:S(2)}) collective-permute-start(bf16[4,5,1024]{2,1,0:T(8,128)(2,1)} %get-tuple-element.37), channel_id=1, source_target_pairs={{1,0},{2,1},{3,2},{4,3},{5,4},{6,5},{7,6},{8,7},{9,8},{10,9},{11,1... | collective-permute-start | bytes 122888 | tf_op jit(solution)/shard_map/ppermute | solution.py:448
  35.4 2.1 %collective-permute-done.4.refs_5_ = bf16[4,5,40,128]{3,2,1,0:T(8,128)(2,1)S(1)} collective-permute-done((bf16[4,5,40,128]{3,2,1,0:T(8,128)(2,1)}, bf16[4,5,40,128]{3,2,1,0:T(8,128)(2,1)S(1)}, u32[]{:S(2)}, u32[]{:S(2)}) %collective-permute-start.4) | collective-permute-done | bytes 204832 | tf_op jit(solution)/shard_map/ppermute | solution.py:449
  37.6 1.5 %collective-permute-done.5.refs_6_ = bf16[4,5,40,128]{3,2,1,0:T(8,128)(2,1)S(1)} collective-permute-done((bf16[4,5,40,128]{3,2,1,0:T(8,128)(2,1)}, bf16[4,5,40,128]{3,2,1,0:T(8,128)(2,1)S(1)}, u32[]{:S(2)}, u32[]{:S(2)}) %collective-permute-start.5) | collective-permute-done | bytes 204832 | tf_op jit(solution)/shard_map/ppermute | solution.py:449
  39.1 3.5 %collective-permute-done.6.refs_7_ = bf16[4,5,40,128]{3,2,1,0:T(8,128)(2,1)S(1)} collective-permute-done((bf16[4,5,40,128]{3,2,1,0:T(8,128)(2,1)}, bf16[4,5,40,128]{3,2,1,0:T(8,128)(2,1)S(1)}, u32[]{:S(2)}, u32[]{:S(2)}) %collective-permute-start.6) | collective-permute-done | bytes 204832 | tf_op jit(solution)/shard_map/ppermute | solution.py:449
  42.6 0.0 copy-done.1
  42.6 0.0 copy-done.3
  42.6 0.6 copy-done.7
  43.2 3.5 %source_blocks.1 = (bf16[4,5,40,128]{3,2,1,0:T(8,128)(2,1)}, bf16[4,5,40,128]{3,2,1,0:T(8,128)(2,1)}, bf16[4,5,40,128]{3,2,1,0:T(8,128)(2,1)}, bf16[4,5,40,128]{...) custom-call(s32[1]{0:T(128)} %bitcast.me_ref, ...), custom_call_target="tpu_custom_call" | custom-call | flops 420000000 | bytes 10000000 | tf_op jit(solution)/shard_map/source_blocks/pallas_call | solution.py:216
  46.7 10.2 %all-to-all-done = bf16[32,40,640]{2,1,0:T(8,128)(2,1)S(1)} async-done(((bf16[32,40,640]{2,1,0:T(8,128)(2,1)}), bf16[32,40,640]{2,1,0:T(8,128)(2,1)S(1)}, u32[]{:S(2)}, u32[]{:S(2)}) %all-to-all-start) | async-done | bytes 1638432 | tf_op jit(solution)/shard_map/all_to_all | solution.py:445
  56.9 3.9 %slope_lines.1 = bf16[32,40,640]{2,1,0:T(8,128)(2,1)} custom-call(bf16[640,1280]{1,0:T(8,128)(2,1)S(1)} %get-tuple-element.35.held_ref, bf16[1280,640]{1,0:T(8,128)(2,1)S(1)} %bitcast.3, bf16[1280,1280]{1,0:T(8,128)(2,1)} %deriv_hbm.3), custom_call_target="tpu_custom_call" | custom-call | flops 2097152000 | bytes 7000000 | tf_op jit(solution)/shard_map/slope_lines/pallas_call | solution.py:374
  60.9 0.0 collective-permute-done.7.low_ref
  60.9 0.0 collective-permute-done.8.high_ref
  60.9 5.8 %all-to-all-start.1 = ((bf16[32,40,640]{2,1,0:T(8,128)(2,1)}), bf16[32,40,640]{2,1,0:T(8,128)(2,1)S(1)}, u32[]{:S(2)}, u32[]{:S(2)}) async-start(bf16[32,40,640]{2,1,0:T(8,128)(2,1)} %slope_lines.1), calls=%async_computation.1 | async-start | bytes 3276800 | tf_op jit(solution)/shard_map/all_to_all | solution.py:454
  66.7 0.1 collective-permute-start.9
  66.8 1.3 %collective-permute-start.10 = (bf16[4,5,40,128]{3,2,1,0:T(8,128)(2,1)S(1)}, bf16[4,5,40,128]{3,2,1,0:T(8,128)(2,1)S(1)}, u32[]{:S(2)}, u32[]{:S(2)}) collective-permute-start(bf16[4,5,40,128]{3,2,1,0:T(8,128)(2,1)S(1)} %copy-done.20), channel_id=1, source_target_pairs={{0,64},{32,96},{64,0},{96,32},{128,192},{160,224},{192,128},{224,1... | collective-permute-start | bytes 614408 | tf_op jit(solution)/shard_map/ppermute | solution.py:451
  68.1 0.6 collective-permute-start.11
  68.7 0.5 collective-permute-start.12
  69.2 2.7 %collective-permute-start.13 = (bf16[4,5,40,128]{3,2,1,0:T(8,128)(2,1)S(1)}, bf16[4,5,40,128]{3,2,1,0:T(8,128)(2,1)S(1)}, u32[]{:S(2)}, u32[]{:S(2)}) collective-permute-start(bf16[4,5,40,128]{3,2,1,0:T(8,128)(2,1)S(1)} %copy-done.17), channel_id=1, source_target_pairs={{0,160},{32,128},{64,224},{96,192},{128,32},{160,0},{192,96},{224,... | collective-permute-start | bytes 614408 | tf_op jit(solution)/shard_map/ppermute | solution.py:451
  71.9 0.0 collective-permute-done.9.refs_1_
  71.9 0.6 collective-permute-start.14
  72.5 2.3 %collective-permute-done.10.refs_2_ = bf16[4,5,40,128]{3,2,1,0:T(8,128)(2,1)S(1)} collective-permute-done((bf16[4,5,40,128]{3,2,1,0:T(8,128)(2,1)S(1)}, bf16[4,5,40,128]{3,2,1,0:T(8,128)(2,1)S(1)}, u32[]{:S(2)}, u32[]{:S(2)}) %collective-permute-start.10) | collective-permute-done | bytes 204832 | tf_op jit(solution)/shard_map/ppermute | solution.py:451
  74.8 0.0 collective-permute-start.15
  74.8 8.5 %local_terms.1.partial_hbm = f32[4,5,40,1024]{3,2,1,0:T(8,128)} custom-call(bf16[4,5,40,1024]{3,2,1,0:T(8,128)(2,1)} %state_ref.1, f32[3,40,1024]{2,1,0:T(8,128)} %metric_i_ref.1, f32[3,40,1024]{2,1,0:T(8,128)} %metric_j_ref.1, bf16[4,5,1024]{2,1,0:T(8,128)(2,1)S(1)} %collective-permute-done.7.low_ref, ...), custom_call_target="tpu_custom_call" | custom-call | flops 1677721600 | bytes 11000000 | tf_op jit(solution)/shard_map/local_terms/pallas_call | solution.py:272
  83.3 0.0 collective-permute-done.11.refs_3_
  83.3 0.3 collective-permute-done.12.refs_4_
  83.6 3.4 %collective-permute-done.13.refs_5_ = bf16[4,5,40,128]{3,2,1,0:T(8,128)(2,1)S(1)} collective-permute-done((bf16[4,5,40,128]{3,2,1,0:T(8,128)(2,1)S(1)}, bf16[4,5,40,128]{3,2,1,0:T(8,128)(2,1)S(1)}, u32[]{:S(2)}, u32[]{:S(2)}) %collective-permute-start.13) | collective-permute-done | bytes 204832 | tf_op jit(solution)/shard_map/ppermute | solution.py:451
  87.1 1.6 %collective-permute-done.14.refs_6_ = bf16[4,5,40,128]{3,2,1,0:T(8,128)(2,1)S(1)} collective-permute-done((bf16[4,5,40,128]{3,2,1,0:T(8,128)(2,1)S(1)}, bf16[4,5,40,128]{3,2,1,0:T(8,128)(2,1)S(1)}, u32[]{:S(2)}, u32[]{:S(2)}) %collective-permute-start.14) | collective-permute-done | bytes 204832 | tf_op jit(solution)/shard_map/ppermute | solution.py:451
  88.6 3.5 %collective-permute-done.15.refs_7_ = bf16[4,5,40,128]{3,2,1,0:T(8,128)(2,1)S(1)} collective-permute-done((bf16[4,5,40,128]{3,2,1,0:T(8,128)(2,1)S(1)}, bf16[4,5,40,128]{3,2,1,0:T(8,128)(2,1)S(1)}, u32[]{:S(2)}, u32[]{:S(2)}) %collective-permute-start.15) | collective-permute-done | bytes 204832 | tf_op jit(solution)/shard_map/ppermute | solution.py:451
  92.1 0.7 copy-done.14
  92.8 3.4 %add_sources.1.total_ref = bf16[4,5,40,1024]{3,2,1,0:T(8,128)(2,1)S(1)} custom-call(s32[1]{0:T(128)} %bitcast.me_ref, f32[4,5,40,1024]{3,2,1,0:T(8,128)} %local_terms.1.partial_hbm, bf16[4,5,40,128]{3,2,1,0:T(8,128)(2,1)} %get-tuple-element.40.refs_0_, bf16[4,5,40,128]{3,2,1,0:T(8,128)(2,1)} %copy-done.8, bf16[4,5,40,128]{3,2,1,0:T(8,128)(2,1)} %copy-done.9, ...), custom_call_target="tpu_custom_call" | custom-call | flops 1000000 | bytes 8000000 | tf_op jit(solution)/shard_map/add_sources/pallas_call | solution.py:311
  96.2 6.9 %all-to-all-done.1.slope_ref = bf16[32,40,640]{2,1,0:T(8,128)(2,1)S(1)} async-done(((bf16[32,40,640]{2,1,0:T(8,128)(2,1)}), bf16[32,40,640]{2,1,0:T(8,128)(2,1)S(1)}, u32[]{:S(2)}, u32[]{:S(2)}) %all-to-all-start.1) | async-done | bytes 1638432 | tf_op jit(solution)/shard_map/all_to_all | solution.py:454
  103.1 1.3 %finish.1 = bf16[4,5,40,1024]{3,2,1,0:T(8,128)(2,1)} custom-call(bf16[4,5,40,1024]{3,2,1,0:T(8,128)(2,1)S(1)} %add_sources.1.total_ref, bf16[32,40,640]{2,1,0:T(8,128)(2,1)S(1)} %all-to-all-done.1.slope_ref), custom_call_target="tpu_custom_call" | custom-call | flops 1000000 | bytes 5000000 | tf_op jit(solution)/shard_map/finish/pallas_call | solution.py:420
  (39 shorter events, 0.1 us)
Async XLA Ops:
  2.9 54.0 %all-to-all-start = ((bf16[32,40,640]{2,1,0:T(8,128)(2,1)}), bf16[32,40,640]{2,1,0:T(8,128)(2,1)S(1)}, u32[]{:S(2)}, u32[]{:S(2)}) async-start(bf16[32,40,640]{2,1,0:T(8,128)(2,1)} %bitcast.4), calls=%async_computation | async-start | bytes 3276800 | tf_op jit(solution)/shard_map/all_to_all | solution.py:445
  14.4 28.9 %copy-start = (bf16[32,32]{1,0:T(8,128)(2,1)S(1)}, bf16[32,32]{1,0:T(8,128)(2,1)}, u32[]{:S(2)}) copy-start(bf16[32,32]{1,0:T(8,128)(2,1)} %spectral_ref.1) | copy-start | bytes 6148
  17.0 5.2 %collective-permute-start = (bf16[4,5,40,128]{3,2,1,0:T(8,128)(2,1)}, bf16[4,5,40,128]{3,2,1,0:T(8,128)(2,1)S(1)}, u32[]{:S(2)}, u32[]{:S(2)}) collective-permute-start(bf16[4,5,40,128]{3,2,1,0:T(8,128)(2,1)} %get-tuple-element.28), channel_id=1, source_target_pairs={{0,32},{32,0},{64,96},{96,64},{128,160},{160,128},{192,224},{224,1... | collective-permute-start | bytes 614408 | tf_op jit(solution)/shard_map/ppermute | solution.py:449
  17.1 8.2 %collective-permute-start.1 = (bf16[4,5,40,128]{3,2,1,0:T(8,128)(2,1)}, bf16[4,5,40,128]{3,2,1,0:T(8,128)(2,1)S(1)}, u32[]{:S(2)}, u32[]{:S(2)}) collective-permute-start(bf16[4,5,40,128]{3,2,1,0:T(8,128)(2,1)} %get-tuple-element.29), channel_id=1, source_target_pairs={{0,64},{32,96},{64,0},{96,32},{128,192},{160,224},{192,128},{224,1... | collective-permute-start | bytes 614408 | tf_op jit(solution)/shard_map/ppermute | solution.py:449
  18.4 10.3 %collective-permute-start.2 = (bf16[4,5,40,128]{3,2,1,0:T(8,128)(2,1)}, bf16[4,5,40,128]{3,2,1,0:T(8,128)(2,1)S(1)}, u32[]{:S(2)}, u32[]{:S(2)}) collective-permute-start(bf16[4,5,40,128]{3,2,1,0:T(8,128)(2,1)} %get-tuple-element.30), channel_id=1, source_target_pairs={{0,96},{32,64},{64,32},{96,0},{128,224},{160,192},{192,160},{224,1... | collective-permute-start | bytes 614408 | tf_op jit(solution)/shard_map/ppermute | solution.py:449
  19.0 15.2 %collective-permute-start.3 = (bf16[4,5,40,128]{3,2,1,0:T(8,128)(2,1)}, bf16[4,5,40,128]{3,2,1,0:T(8,128)(2,1)S(1)}, u32[]{:S(2)}, u32[]{:S(2)}) collective-permute-start(bf16[4,5,40,128]{3,2,1,0:T(8,128)(2,1)} %get-tuple-element.31), channel_id=1, source_target_pairs={{0,128},{32,160},{64,192},{96,224},{128,0},{160,32},{192,64},{224,... | collective-permute-start | bytes 614408 | tf_op jit(solution)/shard_map/ppermute | solution.py:449
  19.5 18.1 %collective-permute-start.4 = (bf16[4,5,40,128]{3,2,1,0:T(8,128)(2,1)}, bf16[4,5,40,128]{3,2,1,0:T(8,128)(2,1)S(1)}, u32[]{:S(2)}, u32[]{:S(2)}) collective-permute-start(bf16[4,5,40,128]{3,2,1,0:T(8,128)(2,1)} %get-tuple-element.32), channel_id=1, source_target_pairs={{0,160},{32,128},{64,224},{96,192},{128,32},{160,0},{192,96},{224,... | collective-permute-start | bytes 614408 | tf_op jit(solution)/shard_map/ppermute | solution.py:449
  22.2 20.3 %copy-start.1 = (bf16[4,5,40,128]{3,2,1,0:T(8,128)(2,1)}, bf16[4,5,40,128]{3,2,1,0:T(8,128)(2,1)S(1)}, u32[]{:S(2)}) copy-start(bf16[4,5,40,128]{3,2,1,0:T(8,128)(2,1)S(1)} %collective-permute-done.refs_1_) | copy-start | bytes 614404
  22.2 16.9 %collective-permute-start.5 = (bf16[4,5,40,128]{3,2,1,0:T(8,128)(2,1)}, bf16[4,5,40,128]{3,2,1,0:T(8,128)(2,1)S(1)}, u32[]{:S(2)}, u32[]{:S(2)}) collective-permute-start(bf16[4,5,40,128]{3,2,1,0:T(8,128)(2,1)} %get-tuple-element.33), channel_id=1, source_target_pairs={{0,192},{32,224},{64,128},{96,160},{128,64},{160,96},{192,0},{224,... | collective-permute-start | bytes 614408 | tf_op jit(solution)/shard_map/ppermute | solution.py:449
  25.3 17.3 %copy-start.2 = (bf16[4,5,40,128]{3,2,1,0:T(8,128)(2,1)}, bf16[4,5,40,128]{3,2,1,0:T(8,128)(2,1)S(1)}, u32[]{:S(2)}) copy-start(bf16[4,5,40,128]{3,2,1,0:T(8,128)(2,1)S(1)} %collective-permute-done.1.refs_2_) | copy-start | bytes 614404
  25.3 17.2 %collective-permute-start.6 = (bf16[4,5,40,128]{3,2,1,0:T(8,128)(2,1)}, bf16[4,5,40,128]{3,2,1,0:T(8,128)(2,1)S(1)}, u32[]{:S(2)}, u32[]{:S(2)}) collective-permute-start(bf16[4,5,40,128]{3,2,1,0:T(8,128)(2,1)} %get-tuple-element.34), channel_id=1, source_target_pairs={{0,224},{32,192},{64,160},{96,128},{128,96},{160,64},{192,32},{224... | collective-permute-start | bytes 614408 | tf_op jit(solution)/shard_map/ppermute | solution.py:449
  28.7 13.8 %copy-start.3 = (bf16[4,5,40,128]{3,2,1,0:T(8,128)(2,1)}, bf16[4,5,40,128]{3,2,1,0:T(8,128)(2,1)S(1)}, u32[]{:S(2)}) copy-start(bf16[4,5,40,128]{3,2,1,0:T(8,128)(2,1)S(1)} %collective-permute-done.2.refs_3_) | copy-start | bytes 614404
  28.7 32.1 %collective-permute-start.7 = (bf16[4,5,1024]{2,1,0:T(8,128)(2,1)}, bf16[4,5,1024]{2,1,0:T(8,128)(2,1)S(1)}, u32[]{:S(2)}, u32[]{:S(2)}) collective-permute-start(bf16[4,5,1024]{2,1,0:T(8,128)(2,1)} %get-tuple-element.36), channel_id=1, source_target_pairs={{0,1},{1,2},{2,3},{3,4},{4,5},{5,6},{6,7},{7,8},{8,9},{9,10},{10,1... | collective-permute-start | bytes 122888 | tf_op jit(solution)/shard_map/ppermute | solution.py:447
  34.2 8.4 %copy-start.4 = (bf16[4,5,40,128]{3,2,1,0:T(8,128)(2,1)}, bf16[4,5,40,128]{3,2,1,0:T(8,128)(2,1)S(1)}, u32[]{:S(2)}) copy-start(bf16[4,5,40,128]{3,2,1,0:T(8,128)(2,1)S(1)} %collective-permute-done.3.refs_4_) | copy-start | bytes 614404
  34.2 26.7 %collective-permute-start.8 = (bf16[4,5,1024]{2,1,0:T(8,128)(2,1)}, bf16[4,5,1024]{2,1,0:T(8,128)(2,1)S(1)}, u32[]{:S(2)}, u32[]{:S(2)}) collective-permute-start(bf16[4,5,1024]{2,1,0:T(8,128)(2,1)} %get-tuple-element.37), channel_id=1, source_target_pairs={{1,0},{2,1},{3,2},{4,3},{5,4},{6,5},{7,6},{8,7},{9,8},{10,9},{11,1... | collective-permute-start | bytes 122888 | tf_op jit(solution)/shard_map/ppermute | solution.py:448
  37.6 5.0 %copy-start.5 = (bf16[4,5,40,128]{3,2,1,0:T(8,128)(2,1)}, bf16[4,5,40,128]{3,2,1,0:T(8,128)(2,1)S(1)}, u32[]{:S(2)}) copy-start(bf16[4,5,40,128]{3,2,1,0:T(8,128)(2,1)S(1)} %collective-permute-done.4.refs_5_) | copy-start | bytes 614404
  39.1 3.5 %copy-start.6 = (bf16[4,5,40,128]{3,2,1,0:T(8,128)(2,1)}, bf16[4,5,40,128]{3,2,1,0:T(8,128)(2,1)S(1)}, u32[]{:S(2)}) copy-start(bf16[4,5,40,128]{3,2,1,0:T(8,128)(2,1)S(1)} %collective-permute-done.5.refs_6_) | copy-start | bytes 614404
  42.5 0.7 copy-start.7
  60.8 5.9 %copy-start.21 = (bf16[4,5,40,128]{3,2,1,0:T(8,128)(2,1)S(1)}, bf16[4,5,40,128]{3,2,1,0:T(8,128)(2,1)}, u32[]{:S(2)}) copy-start(bf16[4,5,40,128]{3,2,1,0:T(8,128)(2,1)} %get-tuple-element.41) | copy-start | bytes 614404
  60.8 6.0 %copy-start.20 = (bf16[4,5,40,128]{3,2,1,0:T(8,128)(2,1)S(1)}, bf16[4,5,40,128]{3,2,1,0:T(8,128)(2,1)}, u32[]{:S(2)}) copy-start(bf16[4,5,40,128]{3,2,1,0:T(8,128)(2,1)} %get-tuple-element.42) | copy-start | bytes 614404
  60.8 7.3 %copy-start.19 = (bf16[4,5,40,128]{3,2,1,0:T(8,128)(2,1)S(1)}, bf16[4,5,40,128]{3,2,1,0:T(8,128)(2,1)}, u32[]{:S(2)}) copy-start(bf16[4,5,40,128]{3,2,1,0:T(8,128)(2,1)} %get-tuple-element.43) | copy-start | bytes 614404
  60.8 7.8 %copy-start.18 = (bf16[4,5,40,128]{3,2,1,0:T(8,128)(2,1)S(1)}, bf16[4,5,40,128]{3,2,1,0:T(8,128)(2,1)}, u32[]{:S(2)}) copy-start(bf16[4,5,40,128]{3,2,1,0:T(8,128)(2,1)} %get-tuple-element.44) | copy-start | bytes 614404
  60.8 8.3 %copy-start.17 = (bf16[4,5,40,128]{3,2,1,0:T(8,128)(2,1)S(1)}, bf16[4,5,40,128]{3,2,1,0:T(8,128)(2,1)}, u32[]{:S(2)}) copy-start(bf16[4,5,40,128]{3,2,1,0:T(8,128)(2,1)} %get-tuple-element.45) | copy-start | bytes 614404
  60.9 11.0 %copy-start.16 = (bf16[4,5,40,128]{3,2,1,0:T(8,128)(2,1)S(1)}, bf16[4,5,40,128]{3,2,1,0:T(8,128)(2,1)}, u32[]{:S(2)}) copy-start(bf16[4,5,40,128]{3,2,1,0:T(8,128)(2,1)} %get-tuple-element.46) | copy-start | bytes 614404
  60.9 13.9 %copy-start.15 = (bf16[4,5,40,128]{3,2,1,0:T(8,128)(2,1)S(1)}, bf16[4,5,40,128]{3,2,1,0:T(8,128)(2,1)}, u32[]{:S(2)}) copy-start(bf16[4,5,40,128]{3,2,1,0:T(8,128)(2,1)} %get-tuple-element.47) | copy-start | bytes 614404
  60.9 42.3 %all-to-all-start.1 = ((bf16[32,40,640]{2,1,0:T(8,128)(2,1)}), bf16[32,40,640]{2,1,0:T(8,128)(2,1)S(1)}, u32[]{:S(2)}, u32[]{:S(2)}) async-start(bf16[32,40,640]{2,1,0:T(8,128)(2,1)} %slope_lines.1), calls=%async_computation.1 | async-start | bytes 3276800 | tf_op jit(solution)/shard_map/all_to_all | solution.py:454
  66.7 5.2 %collective-permute-start.9 = (bf16[4,5,40,128]{3,2,1,0:T(8,128)(2,1)S(1)}, bf16[4,5,40,128]{3,2,1,0:T(8,128)(2,1)S(1)}, u32[]{:S(2)}, u32[]{:S(2)}) collective-permute-start(bf16[4,5,40,128]{3,2,1,0:T(8,128)(2,1)S(1)} %copy-done.21), channel_id=1, source_target_pairs={{0,32},{32,0},{64,96},{96,64},{128,160},{160,128},{192,224},{224,1... | collective-permute-start | bytes 614408 | tf_op jit(solution)/shard_map/ppermute | solution.py:451
  66.8 8.0 %collective-permute-start.10 = (bf16[4,5,40,128]{3,2,1,0:T(8,128)(2,1)S(1)}, bf16[4,5,40,128]{3,2,1,0:T(8,128)(2,1)S(1)}, u32[]{:S(2)}, u32[]{:S(2)}) collective-permute-start(bf16[4,5,40,128]{3,2,1,0:T(8,128)(2,1)S(1)} %copy-done.20), channel_id=1, source_target_pairs={{0,64},{32,96},{64,0},{96,32},{128,192},{160,224},{192,128},{224,1... | collective-permute-start | bytes 614408 | tf_op jit(solution)/shard_map/ppermute | solution.py:451
  68.1 15.2 %collective-permute-start.11 = (bf16[4,5,40,128]{3,2,1,0:T(8,128)(2,1)S(1)}, bf16[4,5,40,128]{3,2,1,0:T(8,128)(2,1)S(1)}, u32[]{:S(2)}, u32[]{:S(2)}) collective-permute-start(bf16[4,5,40,128]{3,2,1,0:T(8,128)(2,1)S(1)} %copy-done.19), channel_id=1, source_target_pairs={{0,96},{32,64},{64,32},{96,0},{128,224},{160,192},{192,160},{224,1... | collective-permute-start | bytes 614408 | tf_op jit(solution)/shard_map/ppermute | solution.py:451
  68.7 14.9 %collective-permute-start.12 = (bf16[4,5,40,128]{3,2,1,0:T(8,128)(2,1)S(1)}, bf16[4,5,40,128]{3,2,1,0:T(8,128)(2,1)S(1)}, u32[]{:S(2)}, u32[]{:S(2)}) collective-permute-start(bf16[4,5,40,128]{3,2,1,0:T(8,128)(2,1)S(1)} %copy-done.18), channel_id=1, source_target_pairs={{0,128},{32,160},{64,192},{96,224},{128,0},{160,32},{192,64},{224,... | collective-permute-start | bytes 614408 | tf_op jit(solution)/shard_map/ppermute | solution.py:451
  69.2 17.9 %collective-permute-start.13 = (bf16[4,5,40,128]{3,2,1,0:T(8,128)(2,1)S(1)}, bf16[4,5,40,128]{3,2,1,0:T(8,128)(2,1)S(1)}, u32[]{:S(2)}, u32[]{:S(2)}) collective-permute-start(bf16[4,5,40,128]{3,2,1,0:T(8,128)(2,1)S(1)} %copy-done.17), channel_id=1, source_target_pairs={{0,160},{32,128},{64,224},{96,192},{128,32},{160,0},{192,96},{224,... | collective-permute-start | bytes 614408 | tf_op jit(solution)/shard_map/ppermute | solution.py:451
  71.9 11.4 %copy-start.8 = (bf16[4,5,40,128]{3,2,1,0:T(8,128)(2,1)}, bf16[4,5,40,128]{3,2,1,0:T(8,128)(2,1)S(1)}, u32[]{:S(2)}) copy-start(bf16[4,5,40,128]{3,2,1,0:T(8,128)(2,1)S(1)} %collective-permute-done.9.refs_1_) | copy-start | bytes 614404
  71.9 16.7 %collective-permute-start.14 = (bf16[4,5,40,128]{3,2,1,0:T(8,128)(2,1)S(1)}, bf16[4,5,40,128]{3,2,1,0:T(8,128)(2,1)S(1)}, u32[]{:S(2)}, u32[]{:S(2)}) collective-permute-start(bf16[4,5,40,128]{3,2,1,0:T(8,128)(2,1)S(1)} %copy-done.16), channel_id=1, source_target_pairs={{0,192},{32,224},{64,128},{96,160},{128,64},{160,96},{192,0},{224,... | collective-permute-start | bytes 614408 | tf_op jit(solution)/shard_map/ppermute | solution.py:451
  74.8 8.5 %copy-start.9 = (bf16[4,5,40,128]{3,2,1,0:T(8,128)(2,1)}, bf16[4,5,40,128]{3,2,1,0:T(8,128)(2,1)S(1)}, u32[]{:S(2)}) copy-start(bf16[4,5,40,128]{3,2,1,0:T(8,128)(2,1)S(1)} %collective-permute-done.10.refs_2_) | copy-start | bytes 614404
  74.8 17.3 %collective-permute-start.15 = (bf16[4,5,40,128]{3,2,1,0:T(8,128)(2,1)S(1)}, bf16[4,5,40,128]{3,2,1,0:T(8,128)(2,1)S(1)}, u32[]{:S(2)}, u32[]{:S(2)}) collective-permute-start(bf16[4,5,40,128]{3,2,1,0:T(8,128)(2,1)S(1)} %copy-done.15), channel_id=1, source_target_pairs={{0,224},{32,192},{64,160},{96,128},{128,96},{160,64},{192,32},{224... | collective-permute-start | bytes 614408 | tf_op jit(solution)/shard_map/ppermute | solution.py:451
  83.3 8.8 %copy-start.10 = (bf16[4,5,40,128]{3,2,1,0:T(8,128)(2,1)}, bf16[4,5,40,128]{3,2,1,0:T(8,128)(2,1)S(1)}, u32[]{:S(2)}) copy-start(bf16[4,5,40,128]{3,2,1,0:T(8,128)(2,1)S(1)} %collective-permute-done.11.refs_3_) | copy-start | bytes 614404
  83.6 8.5 %copy-start.11 = (bf16[4,5,40,128]{3,2,1,0:T(8,128)(2,1)}, bf16[4,5,40,128]{3,2,1,0:T(8,128)(2,1)S(1)}, u32[]{:S(2)}) copy-start(bf16[4,5,40,128]{3,2,1,0:T(8,128)(2,1)S(1)} %collective-permute-done.12.refs_4_) | copy-start | bytes 614404
  87.1 5.1 %copy-start.12 = (bf16[4,5,40,128]{3,2,1,0:T(8,128)(2,1)}, bf16[4,5,40,128]{3,2,1,0:T(8,128)(2,1)S(1)}, u32[]{:S(2)}) copy-start(bf16[4,5,40,128]{3,2,1,0:T(8,128)(2,1)S(1)} %collective-permute-done.13.refs_5_) | copy-start | bytes 614404
  88.6 3.5 %copy-start.13 = (bf16[4,5,40,128]{3,2,1,0:T(8,128)(2,1)}, bf16[4,5,40,128]{3,2,1,0:T(8,128)(2,1)S(1)}, u32[]{:S(2)}) copy-start(bf16[4,5,40,128]{3,2,1,0:T(8,128)(2,1)S(1)} %collective-permute-done.14.refs_6_) | copy-start | bytes 614404
  92.1 0.7 copy-start.14

commit v7 on v6

--- a/solution.py
+++ b/solution.py
@@ -339,7 +339,7 @@
 
     def multiply(deriv_ref, base):
         first = 0
-        for count in (blocks // 2, blocks // 2):
+        for count in (blocks - 6, 6):
             rows = slice(first * block, (first + count) * block)
             total = jnp.dot(deriv_ref[rows, :], lines_ref[...], preferred_element_type=jnp.float32)
             for c in range(count):

time: 106 us -> 107 us (level)
  no operation moved by 1% of the time
where the time goes in v7:
time: 107 us; the launch traced here: 105 us
  waiting for transfers between devices  42.8 us (40%)
  starting transfers between devices  33.9 us (32%)
  Pallas kernels  26.1 us (24%)
  local copies, waits for them, and re-layouts  1.38 us (1%)
    ppermute x7, waiting for transfers between devices, on_device(): lax.ppermute(own[k], 'tm', swaps[k])  14.8 us
    all_to_all x1, starting transfers between devices, on_device(): lax.all_to_all(outgoing, 'space', split_axis=0, concat_axis=0, tiled=True)  11.5 us
    ppermute x7, waiting for transfers between devices, on_device(): lax.ppermute(sources[k], 'tm', swaps[k])  11.1 us
    all_to_all x1, waiting for transfers between devices, on_device(): lax.all_to_all(outgoing, 'space', split_axis=0, concat_axis=0, tiled=True)  10.2 us
    pallas_call x1, Pallas kernels, local_terms(): pl.pallas_call(local_kernel, grid=(nt,), out_shape=pltpu.HBM((nt, nv, nj,...  8.49 us
    all_to_all x1, waiting for transfers between devices, on_device(): lax.all_to_all(slope, 'space', split_axis=0, concat_axis=0, tiled=True, a...  6.76 us
    ppermute x7, starting transfers between devices, on_device(): lax.ppermute(sources[k], 'tm', swaps[k])  5.98 us
    all_to_all x1, starting transfers between devices, on_device(): lax.all_to_all(slope, 'space', split_axis=0, concat_axis=0, tiled=True, a...  5.77 us
  transfers between devices with their start and end apart: 18, of which 13 were waited for; matrix products, arithmetic and copies ran while one was open for 0% of the time, Pallas kernels for 21%

profile of v7, /device:TPU:4, one launch (start us, length us, event | category | flops | bytes accessed | tf_op | source)
XLA Modules:
  0.0 104.7 jit_solution(9410533877377721566)
XLA Ops:
  0.0 2.9 %flux_j.1 = bf16[4,8,40,640]{3,2,1,0:T(8,128)(2,1)} custom-call(bf16[4,5,40,1024]{3,2,1,0:T(8,128)(2,1)} %state_ref.1, f32[3,40,1024]{2,1,0:T(8,128)} %metric_j_ref.1), custom_call_target="tpu_custom_call" | custom-call | flops 10000000 | bytes 4000000 | tf_op jit(solution)/shard_map/flux_j/pallas_call | solution.py:80
  2.9 11.5 %all-to-all-start = ((bf16[32,40,640]{2,1,0:T(8,128)(2,1)}), bf16[32,40,640]{2,1,0:T(8,128)(2,1)S(1)}, u32[]{:S(2)}, u32[]{:S(2)}) async-start(bf16[32,40,640]{2,1,0:T(8,128)(2,1)} %bitcast.4), calls=%async_computation | async-start | bytes 3276800 | tf_op jit(solution)/shard_map/all_to_all | solution.py:445
  14.4 0.0 copy-start
  14.4 2.6 %pack_blocks.1 = (bf16[4,5,1024]{2,1,0:T(8,128)(2,1)}, bf16[4,5,1024]{2,1,0:T(8,128)(2,1)}, bf16[4,5,40,128]{3,2,1,0:T(8,128)(2,1)}, bf16[4,5,40,128]{3,2,1,0:T(...) custom-call(s32[1]{0:T(128)} %bitcast.me_ref, ...), custom_call_target="tpu_custom_call" | custom-call | bytes 3300000 | tf_op jit(solution)/shard_map/pack_blocks/pallas_call | solution.py:133
  17.0 0.1 collective-permute-start
  17.1 1.3 %collective-permute-start.1 = (bf16[4,5,40,128]{3,2,1,0:T(8,128)(2,1)}, bf16[4,5,40,128]{3,2,1,0:T(8,128)(2,1)S(1)}, u32[]{:S(2)}, u32[]{:S(2)}) collective-permute-start(bf16[4,5,40,128]{3,2,1,0:T(8,128)(2,1)} %get-tuple-element.29), channel_id=1, source_target_pairs={{0,64},{32,96},{64,0},{96,32},{128,192},{160,224},{192,128},{224,1... | collective-permute-start | bytes 614408 | tf_op jit(solution)/shard_map/ppermute | solution.py:449
  18.4 0.6 collective-permute-start.2
  19.0 0.5 collective-permute-start.3
  19.5 2.7 %collective-permute-start.4 = (bf16[4,5,40,128]{3,2,1,0:T(8,128)(2,1)}, bf16[4,5,40,128]{3,2,1,0:T(8,128)(2,1)S(1)}, u32[]{:S(2)}, u32[]{:S(2)}) collective-permute-start(bf16[4,5,40,128]{3,2,1,0:T(8,128)(2,1)} %get-tuple-element.32), channel_id=1, source_target_pairs={{0,160},{32,128},{64,224},{96,192},{128,32},{160,0},{192,96},{224,... | collective-permute-start | bytes 614408 | tf_op jit(solution)/shard_map/ppermute | solution.py:449
  22.2 0.0 collective-permute-done.refs_1_
  22.2 0.5 collective-permute-start.5
  22.7 2.6 %collective-permute-done.1.refs_2_ = bf16[4,5,40,128]{3,2,1,0:T(8,128)(2,1)S(1)} collective-permute-done((bf16[4,5,40,128]{3,2,1,0:T(8,128)(2,1)}, bf16[4,5,40,128]{3,2,1,0:T(8,128)(2,1)S(1)}, u32[]{:S(2)}, u32[]{:S(2)}) %collective-permute-start.1) | collective-permute-done | bytes 204832 | tf_op jit(solution)/shard_map/ppermute | solution.py:449
  25.3 0.0 collective-permute-start.6
  25.3 3.4 %collective-permute-done.2.refs_3_ = bf16[4,5,40,128]{3,2,1,0:T(8,128)(2,1)S(1)} collective-permute-done((bf16[4,5,40,128]{3,2,1,0:T(8,128)(2,1)}, bf16[4,5,40,128]{3,2,1,0:T(8,128)(2,1)S(1)}, u32[]{:S(2)}, u32[]{:S(2)}) %collective-permute-start.2) | collective-permute-done | bytes 204832 | tf_op jit(solution)/shard_map/ppermute | solution.py:449
  28.7 3.7 %collective-permute-start.7 = (bf16[4,5,1024]{2,1,0:T(8,128)(2,1)}, bf16[4,5,1024]{2,1,0:T(8,128)(2,1)S(1)}, u32[]{:S(2)}, u32[]{:S(2)}) collective-permute-start(bf16[4,5,1024]{2,1,0:T(8,128)(2,1)} %get-tuple-element.36), channel_id=1, source_target_pairs={{0,1},{1,2},{2,3},{3,4},{4,5},{5,6},{6,7},{7,8},{8,9},{9,10},{10,1... | collective-permute-start | bytes 122888 | tf_op jit(solution)/shard_map/ppermute | solution.py:447
  32.4 1.7 %collective-permute-done.3.refs_4_ = bf16[4,5,40,128]{3,2,1,0:T(8,128)(2,1)S(1)} collective-permute-done((bf16[4,5,40,128]{3,2,1,0:T(8,128)(2,1)}, bf16[4,5,40,128]{3,2,1,0:T(8,128)(2,1)S(1)}, u32[]{:S(2)}, u32[]{:S(2)}) %collective-permute-start.3) | collective-permute-done | bytes 204832 | tf_op jit(solution)/shard_map/ppermute | solution.py:449
  34.2 1.3 %collective-permute-start.8 = (bf16[4,5,1024]{2,1,0:T(8,128)(2,1)}, bf16[4,5,1024]{2,1,0:T(8,128)(2,1)S(1)}, u32[]{:S(2)}, u32[]{:S(2)}) collective-permute-start(bf16[4,5,1024]{2,1,0:T(8,128)(2,1)} %get-tuple-element.37), channel_id=1, source_target_pairs={{1,0},{2,1},{3,2},{4,3},{5,4},{6,5},{7,6},{8,7},{9,8},{10,9},{11,1... | collective-permute-start | bytes 122888 | tf_op jit(solution)/shard_map/ppermute | solution.py:448
  35.4 2.1 %collective-permute-done.4.refs_5_ = bf16[4,5,40,128]{3,2,1,0:T(8,128)(2,1)S(1)} collective-permute-done((bf16[4,5,40,128]{3,2,1,0:T(8,128)(2,1)}, bf16[4,5,40,128]{3,2,1,0:T(8,128)(2,1)S(1)}, u32[]{:S(2)}, u32[]{:S(2)}) %collective-permute-start.4) | collective-permute-done | bytes 204832 | tf_op jit(solution)/shard_map/ppermute | solution.py:449
  37.6 1.5 %collective-permute-done.5.refs_6_ = bf16[4,5,40,128]{3,2,1,0:T(8,128)(2,1)S(1)} collective-permute-done((bf16[4,5,40,128]{3,2,1,0:T(8,128)(2,1)}, bf16[4,5,40,128]{3,2,1,0:T(8,128)(2,1)S(1)}, u32[]{:S(2)}, u32[]{:S(2)}) %collective-permute-start.5) | collective-permute-done | bytes 204832 | tf_op jit(solution)/shard_map/ppermute | solution.py:449
  39.1 3.5 %collective-permute-done.6.refs_7_ = bf16[4,5,40,128]{3,2,1,0:T(8,128)(2,1)S(1)} collective-permute-done((bf16[4,5,40,128]{3,2,1,0:T(8,128)(2,1)}, bf16[4,5,40,128]{3,2,1,0:T(8,128)(2,1)S(1)}, u32[]{:S(2)}, u32[]{:S(2)}) %collective-permute-start.6) | collective-permute-done | bytes 204832 | tf_op jit(solution)/shard_map/ppermute | solution.py:449
  42.6 0.0 copy-done.2
  42.6 0.0 copy-done.4
  42.6 0.6 copy-done.7
  43.2 3.5 %source_blocks.1 = (bf16[4,5,40,128]{3,2,1,0:T(8,128)(2,1)}, bf16[4,5,40,128]{3,2,1,0:T(8,128)(2,1)}, bf16[4,5,40,128]{3,2,1,0:T(8,128)(2,1)}, bf16[4,5,40,128]{...) custom-call(s32[1]{0:T(128)} %bitcast.me_ref, ...), custom_call_target="tpu_custom_call" | custom-call | flops 420000000 | bytes 10000000 | tf_op jit(solution)/shard_map/source_blocks/pallas_call | solution.py:216
  46.7 10.2 %all-to-all-done = bf16[32,40,640]{2,1,0:T(8,128)(2,1)S(1)} async-done(((bf16[32,40,640]{2,1,0:T(8,128)(2,1)}), bf16[32,40,640]{2,1,0:T(8,128)(2,1)S(1)}, u32[]{:S(2)}, u32[]{:S(2)}) %all-to-all-start) | async-done | bytes 1638432 | tf_op jit(solution)/shard_map/all_to_all | solution.py:445
  56.9 3.9 %slope_lines.1 = bf16[32,40,640]{2,1,0:T(8,128)(2,1)} custom-call(bf16[640,1280]{1,0:T(8,128)(2,1)S(1)} %get-tuple-element.35.held_ref, bf16[1280,640]{1,0:T(8,128)(2,1)S(1)} %bitcast.3, bf16[1280,1280]{1,0:T(8,128)(2,1)} %deriv_hbm.3), custom_call_target="tpu_custom_call" | custom-call | flops 2097152000 | bytes 7000000 | tf_op jit(solution)/shard_map/slope_lines/pallas_call | solution.py:374
  60.9 0.0 collective-permute-done.7.low_ref
  60.9 0.0 collective-permute-done.8.high_ref
  60.9 5.8 %all-to-all-start.1 = ((bf16[32,40,640]{2,1,0:T(8,128)(2,1)}), bf16[32,40,640]{2,1,0:T(8,128)(2,1)S(1)}, u32[]{:S(2)}, u32[]{:S(2)}) async-start(bf16[32,40,640]{2,1,0:T(8,128)(2,1)} %slope_lines.1), calls=%async_computation.1 | async-start | bytes 3276800 | tf_op jit(solution)/shard_map/all_to_all | solution.py:454
  66.7 0.1 collective-permute-start.9
  66.8 1.3 %collective-permute-start.10 = (bf16[4,5,40,128]{3,2,1,0:T(8,128)(2,1)S(1)}, bf16[4,5,40,128]{3,2,1,0:T(8,128)(2,1)S(1)}, u32[]{:S(2)}, u32[]{:S(2)}) collective-permute-start(bf16[4,5,40,128]{3,2,1,0:T(8,128)(2,1)S(1)} %copy-done.20), channel_id=1, source_target_pairs={{0,64},{32,96},{64,0},{96,32},{128,192},{160,224},{192,128},{224,1... | collective-permute-start | bytes 614408 | tf_op jit(solution)/shard_map/ppermute | solution.py:451
  68.1 0.6 collective-permute-start.11
  68.7 0.5 collective-permute-start.12
  69.2 2.7 %collective-permute-start.13 = (bf16[4,5,40,128]{3,2,1,0:T(8,128)(2,1)S(1)}, bf16[4,5,40,128]{3,2,1,0:T(8,128)(2,1)S(1)}, u32[]{:S(2)}, u32[]{:S(2)}) collective-permute-start(bf16[4,5,40,128]{3,2,1,0:T(8,128)(2,1)S(1)} %copy-done.17), channel_id=1, source_target_pairs={{0,160},{32,128},{64,224},{96,192},{128,32},{160,0},{192,96},{224,... | collective-permute-start | bytes 614408 | tf_op jit(solution)/shard_map/ppermute | solution.py:451
  71.9 0.0 collective-permute-done.9.refs_1_
  71.9 0.8 collective-permute-start.14
  72.7 2.1 %collective-permute-done.10.refs_2_ = bf16[4,5,40,128]{3,2,1,0:T(8,128)(2,1)S(1)} collective-permute-done((bf16[4,5,40,128]{3,2,1,0:T(8,128)(2,1)S(1)}, bf16[4,5,40,128]{3,2,1,0:T(8,128)(2,1)S(1)}, u32[]{:S(2)}, u32[]{:S(2)}) %collective-permute-start.10) | collective-permute-done | bytes 204832 | tf_op jit(solution)/shard_map/ppermute | solution.py:451
  74.8 0.0 collective-permute-start.15
  74.8 8.5 %local_terms.1.partial_hbm = f32[4,5,40,1024]{3,2,1,0:T(8,128)} custom-call(bf16[4,5,40,1024]{3,2,1,0:T(8,128)(2,1)} %state_ref.1, f32[3,40,1024]{2,1,0:T(8,128)} %metric_i_ref.1, f32[3,40,1024]{2,1,0:T(8,128)} %metric_j_ref.1, bf16[4,5,1024]{2,1,0:T(8,128)(2,1)S(1)} %collective-permute-done.7.low_ref, ...), custom_call_target="tpu_custom_call" | custom-call | flops 1677721600 | bytes 11000000 | tf_op jit(solution)/shard_map/local_terms/pallas_call | solution.py:272
  83.3 0.0 collective-permute-done.11.refs_3_
  83.3 0.3 collective-permute-done.12.refs_4_
  83.6 3.4 %collective-permute-done.13.refs_5_ = bf16[4,5,40,128]{3,2,1,0:T(8,128)(2,1)S(1)} collective-permute-done((bf16[4,5,40,128]{3,2,1,0:T(8,128)(2,1)S(1)}, bf16[4,5,40,128]{3,2,1,0:T(8,128)(2,1)S(1)}, u32[]{:S(2)}, u32[]{:S(2)}) %collective-permute-start.13) | collective-permute-done | bytes 204832 | tf_op jit(solution)/shard_map/ppermute | solution.py:451
  87.1 1.8 %collective-permute-done.14.refs_6_ = bf16[4,5,40,128]{3,2,1,0:T(8,128)(2,1)S(1)} collective-permute-done((bf16[4,5,40,128]{3,2,1,0:T(8,128)(2,1)S(1)}, bf16[4,5,40,128]{3,2,1,0:T(8,128)(2,1)S(1)}, u32[]{:S(2)}, u32[]{:S(2)}) %collective-permute-start.14) | collective-permute-done | bytes 204832 | tf_op jit(solution)/shard_map/ppermute | solution.py:451
  88.8 3.5 %collective-permute-done.15.refs_7_ = bf16[4,5,40,128]{3,2,1,0:T(8,128)(2,1)S(1)} collective-permute-done((bf16[4,5,40,128]{3,2,1,0:T(8,128)(2,1)S(1)}, bf16[4,5,40,128]{3,2,1,0:T(8,128)(2,1)S(1)}, u32[]{:S(2)}, u32[]{:S(2)}) %collective-permute-start.15) | collective-permute-done | bytes 204832 | tf_op jit(solution)/shard_map/ppermute | solution.py:451
  92.3 0.7 copy-done.14
  93.0 3.4 %add_sources.1.total_ref = bf16[4,5,40,1024]{3,2,1,0:T(8,128)(2,1)S(1)} custom-call(s32[1]{0:T(128)} %bitcast.me_ref, f32[4,5,40,1024]{3,2,1,0:T(8,128)} %local_terms.1.partial_hbm, bf16[4,5,40,128]{3,2,1,0:T(8,128)(2,1)} %get-tuple-element.40.refs_0_, bf16[4,5,40,128]{3,2,1,0:T(8,128)(2,1)} %copy-done.8, bf16[4,5,40,128]{3,2,1,0:T(8,128)(2,1)} %copy-done.9, ...), custom_call_target="tpu_custom_call" | custom-call | flops 1000000 | bytes 8000000 | tf_op jit(solution)/shard_map/add_sources/pallas_call | solution.py:311
  96.4 6.8 %all-to-all-done.1.slope_ref = bf16[32,40,640]{2,1,0:T(8,128)(2,1)S(1)} async-done(((bf16[32,40,640]{2,1,0:T(8,128)(2,1)}), bf16[32,40,640]{2,1,0:T(8,128)(2,1)S(1)}, u32[]{:S(2)}, u32[]{:S(2)}) %all-to-all-start.1) | async-done | bytes 1638432 | tf_op jit(solution)/shard_map/all_to_all | solution.py:454
  103.2 1.3 %finish.1 = bf16[4,5,40,1024]{3,2,1,0:T(8,128)(2,1)} custom-call(bf16[4,5,40,1024]{3,2,1,0:T(8,128)(2,1)S(1)} %add_sources.1.total_ref, bf16[32,40,640]{2,1,0:T(8,128)(2,1)S(1)} %all-to-all-done.1.slope_ref), custom_call_target="tpu_custom_call" | custom-call | flops 1000000 | bytes 5000000 | tf_op jit(solution)/shard_map/finish/pallas_call | solution.py:420
  (39 shorter events, 0.1 us)
Async XLA Ops:
  2.9 54.0 %all-to-all-start = ((bf16[32,40,640]{2,1,0:T(8,128)(2,1)}), bf16[32,40,640]{2,1,0:T(8,128)(2,1)S(1)}, u32[]{:S(2)}, u32[]{:S(2)}) async-start(bf16[32,40,640]{2,1,0:T(8,128)(2,1)} %bitcast.4), calls=%async_computation | async-start | bytes 3276800 | tf_op jit(solution)/shard_map/all_to_all | solution.py:445
  14.4 28.9 %copy-start = (bf16[32,32]{1,0:T(8,128)(2,1)S(1)}, bf16[32,32]{1,0:T(8,128)(2,1)}, u32[]{:S(2)}) copy-start(bf16[32,32]{1,0:T(8,128)(2,1)} %spectral_ref.1) | copy-start | bytes 6148
  17.0 5.2 %collective-permute-start = (bf16[4,5,40,128]{3,2,1,0:T(8,128)(2,1)}, bf16[4,5,40,128]{3,2,1,0:T(8,128)(2,1)S(1)}, u32[]{:S(2)}, u32[]{:S(2)}) collective-permute-start(bf16[4,5,40,128]{3,2,1,0:T(8,128)(2,1)} %get-tuple-element.28), channel_id=1, source_target_pairs={{0,32},{32,0},{64,96},{96,64},{128,160},{160,128},{192,224},{224,1... | collective-permute-start | bytes 614408 | tf_op jit(solution)/shard_map/ppermute | solution.py:449
  17.1 8.2 %collective-permute-start.1 = (bf16[4,5,40,128]{3,2,1,0:T(8,128)(2,1)}, bf16[4,5,40,128]{3,2,1,0:T(8,128)(2,1)S(1)}, u32[]{:S(2)}, u32[]{:S(2)}) collective-permute-start(bf16[4,5,40,128]{3,2,1,0:T(8,128)(2,1)} %get-tuple-element.29), channel_id=1, source_target_pairs={{0,64},{32,96},{64,0},{96,32},{128,192},{160,224},{192,128},{224,1... | collective-permute-start | bytes 614408 | tf_op jit(solution)/shard_map/ppermute | solution.py:449
  18.4 10.3 %collective-permute-start.2 = (bf16[4,5,40,128]{3,2,1,0:T(8,128)(2,1)}, bf16[4,5,40,128]{3,2,1,0:T(8,128)(2,1)S(1)}, u32[]{:S(2)}, u32[]{:S(2)}) collective-permute-start(bf16[4,5,40,128]{3,2,1,0:T(8,128)(2,1)} %get-tuple-element.30), channel_id=1, source_target_pairs={{0,96},{32,64},{64,32},{96,0},{128,224},{160,192},{192,160},{224,1... | collective-permute-start | bytes 614408 | tf_op jit(solution)/shard_map/ppermute | solution.py:449
  19.0 15.2 %collective-permute-start.3 = (bf16[4,5,40,128]{3,2,1,0:T(8,128)(2,1)}, bf16[4,5,40,128]{3,2,1,0:T(8,128)(2,1)S(1)}, u32[]{:S(2)}, u32[]{:S(2)}) collective-permute-start(bf16[4,5,40,128]{3,2,1,0:T(8,128)(2,1)} %get-tuple-element.31), channel_id=1, source_target_pairs={{0,128},{32,160},{64,192},{96,224},{128,0},{160,32},{192,64},{224,... | collective-permute-start | bytes 614408 | tf_op jit(solution)/shard_map/ppermute | solution.py:449
  19.5 18.1 %collective-permute-start.4 = (bf16[4,5,40,128]{3,2,1,0:T(8,128)(2,1)}, bf16[4,5,40,128]{3,2,1,0:T(8,128)(2,1)S(1)}, u32[]{:S(2)}, u32[]{:S(2)}) collective-permute-start(bf16[4,5,40,128]{3,2,1,0:T(8,128)(2,1)} %get-tuple-element.32), channel_id=1, source_target_pairs={{0,160},{32,128},{64,224},{96,192},{128,32},{160,0},{192,96},{224,... | collective-permute-start | bytes 614408 | tf_op jit(solution)/shard_map/ppermute | solution.py:449
  22.2 20.3 %copy-start.1 = (bf16[4,5,40,128]{3,2,1,0:T(8,128)(2,1)}, bf16[4,5,40,128]{3,2,1,0:T(8,128)(2,1)S(1)}, u32[]{:S(2)}) copy-start(bf16[4,5,40,128]{3,2,1,0:T(8,128)(2,1)S(1)} %collective-permute-done.refs_1_) | copy-start | bytes 614404
  22.2 16.9 %collective-permute-start.5 = (bf16[4,5,40,128]{3,2,1,0:T(8,128)(2,1)}, bf16[4,5,40,128]{3,2,1,0:T(8,128)(2,1)S(1)}, u32[]{:S(2)}, u32[]{:S(2)}) collective-permute-start(bf16[4,5,40,128]{3,2,1,0:T(8,128)(2,1)} %get-tuple-element.33), channel_id=1, source_target_pairs={{0,192},{32,224},{64,128},{96,160},{128,64},{160,96},{192,0},{224,... | collective-permute-start | bytes 614408 | tf_op jit(solution)/shard_map/ppermute | solution.py:449
  25.3 17.3 %copy-start.2 = (bf16[4,5,40,128]{3,2,1,0:T(8,128)(2,1)}, bf16[4,5,40,128]{3,2,1,0:T(8,128)(2,1)S(1)}, u32[]{:S(2)}) copy-start(bf16[4,5,40,128]{3,2,1,0:T(8,128)(2,1)S(1)} %collective-permute-done.1.refs_2_) | copy-start | bytes 614404
  25.3 17.2 %collective-permute-start.6 = (bf16[4,5,40,128]{3,2,1,0:T(8,128)(2,1)}, bf16[4,5,40,128]{3,2,1,0:T(8,128)(2,1)S(1)}, u32[]{:S(2)}, u32[]{:S(2)}) collective-permute-start(bf16[4,5,40,128]{3,2,1,0:T(8,128)(2,1)} %get-tuple-element.34), channel_id=1, source_target_pairs={{0,224},{32,192},{64,160},{96,128},{128,96},{160,64},{192,32},{224... | collective-permute-start | bytes 614408 | tf_op jit(solution)/shard_map/ppermute | solution.py:449
  28.7 13.8 %copy-start.3 = (bf16[4,5,40,128]{3,2,1,0:T(8,128)(2,1)}, bf16[4,5,40,128]{3,2,1,0:T(8,128)(2,1)S(1)}, u32[]{:S(2)}) copy-start(bf16[4,5,40,128]{3,2,1,0:T(8,128)(2,1)S(1)} %collective-permute-done.2.refs_3_) | copy-start | bytes 614404
  28.7 32.2 %collective-permute-start.7 = (bf16[4,5,1024]{2,1,0:T(8,128)(2,1)}, bf16[4,5,1024]{2,1,0:T(8,128)(2,1)S(1)}, u32[]{:S(2)}, u32[]{:S(2)}) collective-permute-start(bf16[4,5,1024]{2,1,0:T(8,128)(2,1)} %get-tuple-element.36), channel_id=1, source_target_pairs={{0,1},{1,2},{2,3},{3,4},{4,5},{5,6},{6,7},{7,8},{8,9},{9,10},{10,1... | collective-permute-start | bytes 122888 | tf_op jit(solution)/shard_map/ppermute | solution.py:447
  34.2 8.4 %copy-start.4 = (bf16[4,5,40,128]{3,2,1,0:T(8,128)(2,1)}, bf16[4,5,40,128]{3,2,1,0:T(8,128)(2,1)S(1)}, u32[]{:S(2)}) copy-start(bf16[4,5,40,128]{3,2,1,0:T(8,128)(2,1)S(1)} %collective-permute-done.3.refs_4_) | copy-start | bytes 614404
  34.2 26.7 %collective-permute-start.8 = (bf16[4,5,1024]{2,1,0:T(8,128)(2,1)}, bf16[4,5,1024]{2,1,0:T(8,128)(2,1)S(1)}, u32[]{:S(2)}, u32[]{:S(2)}) collective-permute-start(bf16[4,5,1024]{2,1,0:T(8,128)(2,1)} %get-tuple-element.37), channel_id=1, source_target_pairs={{1,0},{2,1},{3,2},{4,3},{5,4},{6,5},{7,6},{8,7},{9,8},{10,9},{11,1... | collective-permute-start | bytes 122888 | tf_op jit(solution)/shard_map/ppermute | solution.py:448
  37.6 5.0 %copy-start.5 = (bf16[4,5,40,128]{3,2,1,0:T(8,128)(2,1)}, bf16[4,5,40,128]{3,2,1,0:T(8,128)(2,1)S(1)}, u32[]{:S(2)}) copy-start(bf16[4,5,40,128]{3,2,1,0:T(8,128)(2,1)S(1)} %collective-permute-done.4.refs_5_) | copy-start | bytes 614404
  39.1 3.5 %copy-start.6 = (bf16[4,5,40,128]{3,2,1,0:T(8,128)(2,1)}, bf16[4,5,40,128]{3,2,1,0:T(8,128)(2,1)S(1)}, u32[]{:S(2)}) copy-start(bf16[4,5,40,128]{3,2,1,0:T(8,128)(2,1)S(1)} %collective-permute-done.5.refs_6_) | copy-start | bytes 614404
  42.5 0.7 copy-start.7
  60.8 5.9 %copy-start.21 = (bf16[4,5,40,128]{3,2,1,0:T(8,128)(2,1)S(1)}, bf16[4,5,40,128]{3,2,1,0:T(8,128)(2,1)}, u32[]{:S(2)}) copy-start(bf16[4,5,40,128]{3,2,1,0:T(8,128)(2,1)} %get-tuple-element.41) | copy-start | bytes 614404
  60.8 6.0 %copy-start.20 = (bf16[4,5,40,128]{3,2,1,0:T(8,128)(2,1)S(1)}, bf16[4,5,40,128]{3,2,1,0:T(8,128)(2,1)}, u32[]{:S(2)}) copy-start(bf16[4,5,40,128]{3,2,1,0:T(8,128)(2,1)} %get-tuple-element.42) | copy-start | bytes 614404
  60.8 7.3 %copy-start.19 = (bf16[4,5,40,128]{3,2,1,0:T(8,128)(2,1)S(1)}, bf16[4,5,40,128]{3,2,1,0:T(8,128)(2,1)}, u32[]{:S(2)}) copy-start(bf16[4,5,40,128]{3,2,1,0:T(8,128)(2,1)} %get-tuple-element.43) | copy-start | bytes 614404
  60.9 7.8 %copy-start.18 = (bf16[4,5,40,128]{3,2,1,0:T(8,128)(2,1)S(1)}, bf16[4,5,40,128]{3,2,1,0:T(8,128)(2,1)}, u32[]{:S(2)}) copy-start(bf16[4,5,40,128]{3,2,1,0:T(8,128)(2,1)} %get-tuple-element.44) | copy-start | bytes 614404
  60.9 8.3 %copy-start.17 = (bf16[4,5,40,128]{3,2,1,0:T(8,128)(2,1)S(1)}, bf16[4,5,40,128]{3,2,1,0:T(8,128)(2,1)}, u32[]{:S(2)}) copy-start(bf16[4,5,40,128]{3,2,1,0:T(8,128)(2,1)} %get-tuple-element.45) | copy-start | bytes 614404
  60.9 11.0 %copy-start.16 = (bf16[4,5,40,128]{3,2,1,0:T(8,128)(2,1)S(1)}, bf16[4,5,40,128]{3,2,1,0:T(8,128)(2,1)}, u32[]{:S(2)}) copy-start(bf16[4,5,40,128]{3,2,1,0:T(8,128)(2,1)} %get-tuple-element.46) | copy-start | bytes 614404
  60.9 13.9 %copy-start.15 = (bf16[4,5,40,128]{3,2,1,0:T(8,128)(2,1)S(1)}, bf16[4,5,40,128]{3,2,1,0:T(8,128)(2,1)}, u32[]{:S(2)}) copy-start(bf16[4,5,40,128]{3,2,1,0:T(8,128)(2,1)} %get-tuple-element.47) | copy-start | bytes 614404
  60.9 42.3 %all-to-all-start.1 = ((bf16[32,40,640]{2,1,0:T(8,128)(2,1)}), bf16[32,40,640]{2,1,0:T(8,128)(2,1)S(1)}, u32[]{:S(2)}, u32[]{:S(2)}) async-start(bf16[32,40,640]{2,1,0:T(8,128)(2,1)} %slope_lines.1), calls=%async_computation.1 | async-start | bytes 3276800 | tf_op jit(solution)/shard_map/all_to_all | solution.py:454
  66.7 5.2 %collective-permute-start.9 = (bf16[4,5,40,128]{3,2,1,0:T(8,128)(2,1)S(1)}, bf16[4,5,40,128]{3,2,1,0:T(8,128)(2,1)S(1)}, u32[]{:S(2)}, u32[]{:S(2)}) collective-permute-start(bf16[4,5,40,128]{3,2,1,0:T(8,128)(2,1)S(1)} %copy-done.21), channel_id=1, source_target_pairs={{0,32},{32,0},{64,96},{96,64},{128,160},{160,128},{192,224},{224,1... | collective-permute-start | bytes 614408 | tf_op jit(solution)/shard_map/ppermute | solution.py:451
  66.8 8.0 %collective-permute-start.10 = (bf16[4,5,40,128]{3,2,1,0:T(8,128)(2,1)S(1)}, bf16[4,5,40,128]{3,2,1,0:T(8,128)(2,1)S(1)}, u32[]{:S(2)}, u32[]{:S(2)}) collective-permute-start(bf16[4,5,40,128]{3,2,1,0:T(8,128)(2,1)S(1)} %copy-done.20), channel_id=1, source_target_pairs={{0,64},{32,96},{64,0},{96,32},{128,192},{160,224},{192,128},{224,1... | collective-permute-start | bytes 614408 | tf_op jit(solution)/shard_map/ppermute | solution.py:451
  68.1 15.2 %collective-permute-start.11 = (bf16[4,5,40,128]{3,2,1,0:T(8,128)(2,1)S(1)}, bf16[4,5,40,128]{3,2,1,0:T(8,128)(2,1)S(1)}, u32[]{:S(2)}, u32[]{:S(2)}) collective-permute-start(bf16[4,5,40,128]{3,2,1,0:T(8,128)(2,1)S(1)} %copy-done.19), channel_id=1, source_target_pairs={{0,96},{32,64},{64,32},{96,0},{128,224},{160,192},{192,160},{224,1... | collective-permute-start | bytes 614408 | tf_op jit(solution)/shard_map/ppermute | solution.py:451
  68.7 14.9 %collective-permute-start.12 = (bf16[4,5,40,128]{3,2,1,0:T(8,128)(2,1)S(1)}, bf16[4,5,40,128]{3,2,1,0:T(8,128)(2,1)S(1)}, u32[]{:S(2)}, u32[]{:S(2)}) collective-permute-start(bf16[4,5,40,128]{3,2,1,0:T(8,128)(2,1)S(1)} %copy-done.18), channel_id=1, source_target_pairs={{0,128},{32,160},{64,192},{96,224},{128,0},{160,32},{192,64},{224,... | collective-permute-start | bytes 614408 | tf_op jit(solution)/shard_map/ppermute | solution.py:451
  69.2 17.9 %collective-permute-start.13 = (bf16[4,5,40,128]{3,2,1,0:T(8,128)(2,1)S(1)}, bf16[4,5,40,128]{3,2,1,0:T(8,128)(2,1)S(1)}, u32[]{:S(2)}, u32[]{:S(2)}) collective-permute-start(bf16[4,5,40,128]{3,2,1,0:T(8,128)(2,1)S(1)} %copy-done.17), channel_id=1, source_target_pairs={{0,160},{32,128},{64,224},{96,192},{128,32},{160,0},{192,96},{224,... | collective-permute-start | bytes 614408 | tf_op jit(solution)/shard_map/ppermute | solution.py:451
  71.9 11.4 %copy-start.8 = (bf16[4,5,40,128]{3,2,1,0:T(8,128)(2,1)}, bf16[4,5,40,128]{3,2,1,0:T(8,128)(2,1)S(1)}, u32[]{:S(2)}) copy-start(bf16[4,5,40,128]{3,2,1,0:T(8,128)(2,1)S(1)} %collective-permute-done.9.refs_1_) | copy-start | bytes 614404
  71.9 16.9 %collective-permute-start.14 = (bf16[4,5,40,128]{3,2,1,0:T(8,128)(2,1)S(1)}, bf16[4,5,40,128]{3,2,1,0:T(8,128)(2,1)S(1)}, u32[]{:S(2)}, u32[]{:S(2)}) collective-permute-start(bf16[4,5,40,128]{3,2,1,0:T(8,128)(2,1)S(1)} %copy-done.16), channel_id=1, source_target_pairs={{0,192},{32,224},{64,128},{96,160},{128,64},{160,96},{192,0},{224,... | collective-permute-start | bytes 614408 | tf_op jit(solution)/shard_map/ppermute | solution.py:451
  74.8 8.5 %copy-start.9 = (bf16[4,5,40,128]{3,2,1,0:T(8,128)(2,1)}, bf16[4,5,40,128]{3,2,1,0:T(8,128)(2,1)S(1)}, u32[]{:S(2)}) copy-start(bf16[4,5,40,128]{3,2,1,0:T(8,128)(2,1)S(1)} %collective-permute-done.10.refs_2_) | copy-start | bytes 614404
  74.8 17.5 %collective-permute-start.15 = (bf16[4,5,40,128]{3,2,1,0:T(8,128)(2,1)S(1)}, bf16[4,5,40,128]{3,2,1,0:T(8,128)(2,1)S(1)}, u32[]{:S(2)}, u32[]{:S(2)}) collective-permute-start(bf16[4,5,40,128]{3,2,1,0:T(8,128)(2,1)S(1)} %copy-done.15), channel_id=1, source_target_pairs={{0,224},{32,192},{64,160},{96,128},{128,96},{160,64},{192,32},{224... | collective-permute-start | bytes 614408 | tf_op jit(solution)/shard_map/ppermute | solution.py:451
  83.3 9.0 %copy-start.10 = (bf16[4,5,40,128]{3,2,1,0:T(8,128)(2,1)}, bf16[4,5,40,128]{3,2,1,0:T(8,128)(2,1)S(1)}, u32[]{:S(2)}) copy-start(bf16[4,5,40,128]{3,2,1,0:T(8,128)(2,1)S(1)} %collective-permute-done.11.refs_3_) | copy-start | bytes 614404
  83.6 8.7 %copy-start.11 = (bf16[4,5,40,128]{3,2,1,0:T(8,128)(2,1)}, bf16[4,5,40,128]{3,2,1,0:T(8,128)(2,1)S(1)}, u32[]{:S(2)}) copy-start(bf16[4,5,40,128]{3,2,1,0:T(8,128)(2,1)S(1)} %collective-permute-done.12.refs_4_) | copy-start | bytes 614404
  87.1 5.2 %copy-start.12 = (bf16[4,5,40,128]{3,2,1,0:T(8,128)(2,1)}, bf16[4,5,40,128]{3,2,1,0:T(8,128)(2,1)S(1)}, u32[]{:S(2)}) copy-start(bf16[4,5,40,128]{3,2,1,0:T(8,128)(2,1)S(1)} %collective-permute-done.13.refs_5_) | copy-start | bytes 614404
  88.8 3.5 %copy-start.13 = (bf16[4,5,40,128]{3,2,1,0:T(8,128)(2,1)}, bf16[4,5,40,128]{3,2,1,0:T(8,128)(2,1)S(1)}, u32[]{:S(2)}) copy-start(bf16[4,5,40,128]{3,2,1,0:T(8,128)(2,1)S(1)} %collective-permute-done.14.refs_6_) | copy-start | bytes 614404
  92.3 0.7 copy-start.14
